TPU v7x, 32 devices: a whole 2x2x4 slice. The times are simulated.
32 devices in a mesh: grp: 2 (over x), ctx: 4 (over y, core), exp: 4 (over z).
Axes of the slice: x: 2, y: 2, z: 4, core: 2. Of those that a mesh axis runs over, the one named last changes fastest.
Arguments:
- hidden_in: bfloat16 [8, 1024, 2048], P(('grp', 'exp'), 'ctx'), may hold values from -6 to 6
- out_grad: bfloat16 [8, 1024, 2048], P(('grp', 'exp'), 'ctx'), may hold values from -6 to 6
- doc_lengths: int32 [8, 6], P(('grp', 'exp')), may hold values from 1 to 1019, as said below
- routes: int32 [8, 1024, 8], P(('grp', 'exp'), 'ctx'), may hold values from 0 to 15, all different within a row; in each aligned block of 256 rows (0 to 255, 256 to 511, ..., all dimensions but the last counted through in order) at most 160 rows name the same one
- attention_input_weight: bfloat16 [2048, 5120], P(('ctx', 'exp')), may hold values from -0.125 to 0.125
- attn_out_weight: bfloat16 [2048, 4096], P(('ctx', 'exp')), may hold values from -0.75 to 0.75
- norm_gains: bfloat16 [2048, 2], replicated, may hold values from 0.25 to 1.75
- head_gains: bfloat16 [128, 2], replicated, may hold values from 0.25 to 1.75
- router_weight: bfloat16 [2048, 16], replicated, may hold values from -0.06591797 to 0.06591797
- expert_in: bfloat16 [2048, 16, 2, 768], P('ctx', 'exp'), may hold values from -0.125 to 0.125
- expert_out: bfloat16 [2048, 16, 768], P('ctx', 'exp'), may hold values from -0.875 to 0.875
Outputs:
- output: bfloat16 [8, 1024, 2048], P(('grp', 'exp'), 'ctx')
- input_grad: bfloat16 [8, 1024, 2048], P(('grp', 'exp'), 'ctx')
- attn_in_grad: float32 [2048, 5120], P(('ctx', 'exp'))
- attn_out_grad: float32 [2048, 4096], P(('ctx', 'exp'))
- norm_gains_grad: float32 [2048, 2], replicated
- head_gains_grad: float32 [128, 2], replicated
- router_grad: float32 [2048, 16], replicated
- expert_in_grad: float32 [2048, 16, 2, 768], P('ctx', 'exp')
- expert_out_grad: float32 [2048, 16, 768], P('ctx', 'exp')
Inputs may be any that keep to these rules, and one draw needn't show every extreme that they name: `doc_lengths`: each row lists the lengths of the 6 documents of one sequence in order; they sum to 1024. A token's 8 routes name different experts; among the tokens of one device (aligned blocks of 256 positions) no expert is named more than 160 times, a bound that some block reaches.
All inputs are finite; a program needn't handle non-finite values.
Results may differ from a plain program's by a relative error of at most 0.02.
Values may be sent and summed in bfloat16 or wider, within the bound.
A program may use at most 512 MiB of HBM per device.

v0:
```python
import jax
import jax.numpy as jnp
from jax import lax
from jax.sharding import PartitionSpec as P

epsilon = 1e-06
rotary_base = 1000000.0
key_span = 512


def doc_tables(lengths, positions):
    doc_ends = jnp.cumsum(lengths)
    passed = positions[:, None] >= doc_ends[None, :]
    doc_index = jnp.sum(passed.astype(jnp.int32), axis=1)
    first_pos = jnp.sum(jnp.where(passed, lengths[None, :], 0), axis=1)
    return (doc_index, positions - first_pos)


def rotate(values, relative, sign):
    half_dim = values.shape[-1] // 2
    freqs = rotary_base ** (-2.0 * jnp.arange(half_dim, dtype=jnp.float32) / values.shape[-1])
    angles = relative.astype(jnp.float32)[:, None] * freqs[None, :]
    cosine = jnp.cos(angles)[:, None, :]
    sine = sign * jnp.sin(angles)[:, None, :]
    first = values[..., :half_dim]
    second = values[..., half_dim:]
    return jnp.concatenate(
        [first * cosine - second * sine, second * cosine + first * sine], axis=-1
    )


def norm_forward(values, gain_vec):
    scale_vec = lax.rsqrt(jnp.mean(values * values, axis=-1, keepdims=True) + epsilon)
    unit_vec = values * scale_vec
    return (unit_vec * gain_vec, unit_vec, scale_vec)


def norm_backward(upstream, unit_vec, scale_vec, gain_vec):
    along = upstream * gain_vec
    return scale_vec * (along - unit_vec * jnp.mean(along * unit_vec, axis=-1, keepdims=True))


def per_device(
    hidden_in,
    out_grad,
    doc_lengths,
    routes,
    attention_input_weight,
    attn_out_weight,
    norm_gains,
    head_gains,
    router_weight,
    expert_in,
    expert_out,
):
    hidden = hidden_in[0].astype(jnp.float32)
    tokens_here, model_width = hidden.shape
    head_dim = head_gains.shape[0]
    expert_count = router_weight.shape[1]
    local_experts = expert_in.shape[1]
    route_picks = routes.shape[2]
    cycle_size = lax.axis_size("ctx")
    cycle_place = lax.axis_index("ctx")
    seq_length = tokens_here * cycle_size
    lengths = doc_lengths[0]
    query_pos = cycle_place * tokens_here + jnp.arange(tokens_here, dtype=jnp.int32)
    query_doc, query_rel = doc_tables(lengths, query_pos)
    gain_attn = norm_gains[:, 0].astype(jnp.float32)
    gain_ffn = norm_gains[:, 1].astype(jnp.float32)
    gain_query = head_gains[:, 0].astype(jnp.float32)
    gain_key = head_gains[:, 1].astype(jnp.float32)
    normed, hidden_unit, hidden_scale = norm_forward(hidden, gain_attn)
    normed_low = normed.astype(jnp.bfloat16)
    weight_in, weight_out = (
        lax.all_gather(attention_input_weight, ("ctx", "exp"), axis=0, tiled=True),
        lax.all_gather(attn_out_weight, ("ctx", "exp"), axis=0, tiled=True),
    )
    joined_projection = jnp.dot(normed_low, weight_in, preferred_element_type=jnp.float32)
    joined_width = weight_in.shape[1]
    query_width = weight_out.shape[1]
    head_count = query_width // head_dim
    kv_width = (joined_width - query_width) // 2
    kv_heads = kv_width // head_dim
    query_group_size = head_count // kv_heads
    query_raw = joined_projection[:, :query_width].reshape(tokens_here, head_count, head_dim)
    key_raw = joined_projection[:, query_width : query_width + kv_width].reshape(
        tokens_here, kv_heads, head_dim
    )
    value_low = joined_projection[:, query_width + kv_width :].astype(jnp.bfloat16)
    query_normed, query_unit, query_scale = norm_forward(query_raw, gain_query)
    key_normed, key_unit, key_scale = norm_forward(key_raw, gain_key)
    query_low = rotate(query_normed, query_rel, 1.0).astype(jnp.bfloat16)
    key_low = rotate(key_normed, query_rel, 1.0).astype(jnp.bfloat16)
    keys_local = jnp.stack([key_low.reshape(tokens_here, kv_width), value_low], axis=1)
    keys_all, in_all, out_all = (
        lax.all_gather(keys_local, "ctx", axis=0, tiled=True),
        lax.all_gather(expert_in, "ctx", axis=0, tiled=True),
        lax.all_gather(expert_out, "ctx", axis=0, tiled=True),
    )
    span = min(key_span, seq_length)
    block_count = seq_length // span
    key_blocks = keys_all.reshape(block_count, span, 2, kv_heads, head_dim)
    block_ids = jnp.arange(block_count, dtype=jnp.int32)
    query_rows = (
        query_low.reshape(tokens_here, kv_heads, query_group_size, head_dim)
        .transpose(1, 2, 0, 3)
        .reshape(kv_heads, query_group_size * tokens_here, head_dim)
    )
    score_scale = head_dim ** (-0.5)

    def block_scores(block_id, key_block):
        raw_scores = (
            jnp.einsum(
                "hrd,khd->hrk", query_rows, key_block[:, 0], preferred_element_type=jnp.float32
            )
            * score_scale
        )
        key_pos = block_id * span + jnp.arange(span, dtype=jnp.int32)
        key_doc = doc_tables(lengths, key_pos)[0]
        allowed = (key_pos[None, :] <= query_pos[:, None]) & (
            key_doc[None, :] == query_doc[:, None]
        )
        allowed = jnp.tile(allowed, (query_group_size, 1))[None]
        return (jnp.where(allowed, raw_scores, -1e30), allowed)

    def stats_step(running, scan_item):
        best_score, mass_sum = running
        block_id, key_block = scan_item
        masked, allowed = block_scores(block_id, key_block)
        new_best = jnp.maximum(best_score, jnp.max(masked, axis=-1))
        fresh = jnp.sum(jnp.where(allowed, jnp.exp(masked - new_best[..., None]), 0.0), axis=-1)
        return ((new_best, mass_sum * jnp.exp(best_score - new_best) + fresh), None)

    start_best = jnp.full((kv_heads, query_group_size * tokens_here), -1e30, jnp.float32)
    (best_score, mass_sum), unused = lax.scan(
        stats_step, (start_best, jnp.zeros_like(start_best)), (block_ids, key_blocks)
    )
    log_total = best_score + jnp.log(mass_sum)

    def value_step(summed, scan_item):
        block_id, key_block = scan_item
        masked, allowed = block_scores(block_id, key_block)
        weights = jnp.where(allowed, jnp.exp(masked - log_total[..., None]), 0.0).astype(
            jnp.bfloat16
        )
        return (
            summed
            + jnp.einsum(
                "hrk,khd->hrd", weights, key_block[:, 1], preferred_element_type=jnp.float32
            ),
            None,
        )

    start_rows = jnp.zeros((kv_heads, query_group_size * tokens_here, head_dim), jnp.float32)
    attended, unused = lax.scan(value_step, start_rows, (block_ids, key_blocks))
    attended_low = (
        attended.reshape(kv_heads, query_group_size, tokens_here, head_dim)
        .transpose(2, 0, 1, 3)
        .reshape(tokens_here, query_width)
        .astype(jnp.bfloat16)
    )
    branch = jnp.einsum("rc,dc->rd", attended_low, weight_out, preferred_element_type=jnp.float32)
    middle = hidden + branch
    ffn_normed, middle_unit, middle_scale = norm_forward(middle, gain_ffn)
    ffn_low = ffn_normed.astype(jnp.bfloat16)
    logits = jnp.dot(ffn_low, router_weight, preferred_element_type=jnp.float32)
    probs = jax.nn.softmax(logits, axis=-1)
    route_here = routes[0]
    route_hits = (
        route_here[:, :, None] == jnp.arange(expert_count, dtype=jnp.int32)[None, None, :]
    ).astype(jnp.float32)
    selected = jnp.sum(route_hits * probs[:, None, :], axis=-1)
    sel_total = jnp.sum(selected, axis=1, keepdims=True)
    gates = selected / sel_total
    capacity = 5 * tokens_here * route_picks // (4 * expert_count)
    flat_route = route_here.reshape(-1)
    slot_hits = (flat_route[:, None] == jnp.arange(expert_count, dtype=jnp.int32)[None, :]).astype(
        jnp.int32
    )
    slot_index = jnp.sum((jnp.cumsum(slot_hits, axis=0) - slot_hits) * slot_hits, axis=1)
    target = flat_route * capacity + slot_index
    exp_size = lax.axis_size("exp")
    buffer_shape = (exp_size, local_experts * capacity, model_width)
    arrive_shape = (exp_size, local_experts, capacity, model_width)
    empty_buffer = jnp.zeros((expert_count * capacity, model_width), jnp.bfloat16)
    outgoing = empty_buffer.at[target].set(jnp.repeat(ffn_low, route_picks, axis=0))
    arrived = lax.all_to_all(
        outgoing.reshape(buffer_shape), "exp", split_axis=0, concat_axis=0, tiled=True
    ).reshape(arrive_shape)
    gate_up = jnp.einsum("secd,dekf->seckf", arrived, in_all, preferred_element_type=jnp.float32)
    gate_part = gate_up[:, :, :, 0]
    up_part = gate_up[:, :, :, 1]
    sigmoid_part = jax.nn.sigmoid(gate_part)
    silu_part = jax.nn.silu(gate_part)
    act_low = (silu_part * up_part).astype(jnp.bfloat16)
    made = jnp.einsum(
        "secf,def->secd", act_low, out_all, preferred_element_type=jnp.float32
    ).astype(jnp.bfloat16)
    returned = lax.all_to_all(
        made.reshape(buffer_shape), "exp", split_axis=0, concat_axis=0, tiled=True
    ).reshape(expert_count * capacity, model_width)
    route_out = returned[target].astype(jnp.float32).reshape(tokens_here, route_picks, model_width)
    mixture = jnp.sum(gates[:, :, None] * route_out, axis=1)
    output = (middle + mixture).astype(jnp.bfloat16)[None]
    upstream = out_grad[0].astype(jnp.float32)
    gate_grads = jnp.sum(upstream[:, None, :] * route_out, axis=-1)
    route_grads = (
        (gates[:, :, None] * upstream[:, None, :])
        .astype(jnp.bfloat16)
        .reshape(tokens_here * route_picks, model_width)
    )
    outgoing_grads = empty_buffer.at[target].set(route_grads)
    grads_arrived = lax.all_to_all(
        outgoing_grads.reshape(buffer_shape), "exp", split_axis=0, concat_axis=0, tiled=True
    ).reshape(arrive_shape)
    act_grads = jnp.einsum(
        "secd,def->secf", grads_arrived, out_all, preferred_element_type=jnp.float32
    )
    gate_grad_part = act_grads * up_part * sigmoid_part * (1.0 + gate_part * (1.0 - sigmoid_part))
    gate_up_grads = jnp.stack([gate_grad_part, act_grads * silu_part], axis=3).astype(jnp.bfloat16)
    input_rows = jnp.einsum(
        "seckf,dekf->secd", gate_up_grads, in_all, preferred_element_type=jnp.float32
    ).astype(jnp.bfloat16)
    came_back = lax.all_to_all(
        input_rows.reshape(buffer_shape), "exp", split_axis=0, concat_axis=0, tiled=True
    ).reshape(expert_count * capacity, model_width)
    sent_grads = jnp.sum(
        came_back[target].astype(jnp.float32).reshape(tokens_here, route_picks, model_width), axis=1
    )
    term_in = jnp.einsum(
        "secd,seckf->dekf", arrived, gate_up_grads, preferred_element_type=jnp.float32
    )
    term_out = jnp.einsum(
        "secd,secf->def", grads_arrived, act_low, preferred_element_type=jnp.float32
    )
    expert_local = lax.psum_scatter(
        jnp.concatenate([term_in, term_out[:, :, None, :]], axis=2).astype(jnp.bfloat16),
        "ctx",
        scatter_dimension=0,
        tiled=True,
    )
    weighted = jnp.sum(gate_grads * gates, axis=1, keepdims=True)
    sel_grads = (gate_grads - weighted) / sel_total
    prob_grads = jnp.sum(sel_grads[:, :, None] * route_hits, axis=1)
    logit_grads = probs * (prob_grads - jnp.sum(probs * prob_grads, axis=1, keepdims=True))
    router_float = router_weight.astype(jnp.float32)
    ffn_grads = sent_grads + jnp.dot(logit_grads, router_float.T, precision=lax.Precision.HIGHEST)
    router_grads = jnp.dot(
        ffn_low.astype(jnp.float32).T, logit_grads, precision=lax.Precision.HIGHEST
    )
    middle_grad = upstream + norm_backward(ffn_grads, middle_unit, middle_scale, gain_ffn)
    attn_grad_low = middle_grad.astype(jnp.bfloat16)
    heads_grad_low = jnp.dot(attn_grad_low, weight_out, preferred_element_type=jnp.float32).astype(
        jnp.bfloat16
    )
    grad_rows = (
        heads_grad_low.reshape(tokens_here, kv_heads, query_group_size, head_dim)
        .transpose(1, 2, 0, 3)
        .reshape(kv_heads, query_group_size * tokens_here, head_dim)
    )

    def delta_step(summed, scan_item):
        block_id, key_block = scan_item
        masked, allowed = block_scores(block_id, key_block)
        weights = jnp.where(allowed, jnp.exp(masked - log_total[..., None]), 0.0)
        weight_grads = jnp.einsum(
            "hrd,khd->hrk", grad_rows, key_block[:, 1], preferred_element_type=jnp.float32
        )
        return (summed + jnp.sum(weights * weight_grads, axis=-1), None)

    delta_sum, unused = lax.scan(delta_step, jnp.zeros_like(log_total), (block_ids, key_blocks))

    def grad_step(query_grads, scan_item):
        block_id, key_block = scan_item
        masked, allowed = block_scores(block_id, key_block)
        weights = jnp.where(allowed, jnp.exp(masked - log_total[..., None]), 0.0)
        weight_grads = jnp.einsum(
            "hrd,khd->hrk", grad_rows, key_block[:, 1], preferred_element_type=jnp.float32
        )
        score_grads = (weights * (weight_grads - delta_sum[..., None])).astype(jnp.bfloat16)
        query_grads = (
            query_grads
            + jnp.einsum(
                "hrk,khd->hrd", score_grads, key_block[:, 0], preferred_element_type=jnp.float32
            )
            * score_scale
        )
        key_grads = (
            jnp.einsum("hrk,hrd->khd", score_grads, query_rows, preferred_element_type=jnp.float32)
            * score_scale
        )
        value_grads = jnp.einsum(
            "hrk,hrd->khd",
            weights.astype(jnp.bfloat16),
            grad_rows,
            preferred_element_type=jnp.float32,
        )
        return (query_grads, jnp.stack([key_grads, value_grads], axis=1))

    query_grads, block_grads = lax.scan(grad_step, start_rows, (block_ids, key_blocks))
    key_value_grads = lax.psum_scatter(
        block_grads.reshape(seq_length, 2, kv_width).astype(jnp.bfloat16),
        "ctx",
        scatter_dimension=0,
        tiled=True,
    ).astype(jnp.float32)
    query_grads = (
        query_grads.reshape(kv_heads, query_group_size, tokens_here, head_dim)
        .transpose(2, 0, 1, 3)
        .reshape(tokens_here, head_count, head_dim)
    )
    query_turned = rotate(query_grads, query_rel, -1.0)
    query_proj = norm_backward(query_turned, query_unit, query_scale, gain_query)
    key_turned = rotate(
        key_value_grads[:, 0].reshape(tokens_here, kv_heads, head_dim), query_rel, -1.0
    )
    key_proj = norm_backward(key_turned, key_unit, key_scale, gain_key)
    head_gain_grads = jnp.stack(
        [
            jnp.sum(query_turned * query_unit, axis=(0, 1)),
            jnp.sum(key_turned * key_unit, axis=(0, 1)),
        ],
        axis=1,
    )
    joined_grads = jnp.concatenate(
        [
            query_proj.reshape(tokens_here, query_width),
            key_proj.reshape(tokens_here, kv_width),
            key_value_grads[:, 1],
        ],
        axis=1,
    ).astype(jnp.bfloat16)
    normed_grads = jnp.einsum(
        "rc,dc->rd", joined_grads, weight_in, preferred_element_type=jnp.float32
    )
    input_part = norm_backward(normed_grads, hidden_unit, hidden_scale, gain_attn)
    input_grad = (middle_grad + input_part).astype(jnp.bfloat16)[None]
    norm_gain_grads = jnp.stack(
        [jnp.sum(normed_grads * hidden_unit, axis=0), jnp.sum(ffn_grads * middle_unit, axis=0)],
        axis=1,
    )
    norm_total, head_total, router_total = lax.psum(
        (norm_gain_grads, head_gain_grads, router_grads), ("grp", "ctx", "exp")
    )
    part_in = jnp.einsum("rc,rq->cq", normed_low, joined_grads, preferred_element_type=jnp.float32)
    part_out = jnp.einsum(
        "rc,rq->cq", attn_grad_low, attended_low, preferred_element_type=jnp.float32
    )
    dense_local = lax.psum_scatter(
        jnp.concatenate([part_in, part_out], axis=1),
        ("ctx", "exp"),
        scatter_dimension=0,
        tiled=True,
    )
    dense_total, expert_total = (
        lax.psum(dense_local.astype(jnp.bfloat16), "grp").astype(jnp.float32),
        lax.psum(expert_local, "grp").astype(jnp.float32),
    )
    return (
        output,
        input_grad,
        dense_total[:, :joined_width],
        dense_total[:, joined_width:],
        norm_total,
        head_total,
        router_total,
        expert_total[:, :, :2],
        expert_total[:, :, 2],
    )


def solution(mesh):
    placed = (
        P(("grp", "exp"), "ctx", None),
        P(("grp", "exp"), "ctx", None),
        P(("grp", "exp"), None),
        P(("grp", "exp"), "ctx", None),
        P(("ctx", "exp"), None),
        P(("ctx", "exp"), None),
        P(),
        P(),
        P(),
        P("ctx", "exp", None, None),
        P("ctx", "exp", None),
    )
    return jax.shard_map(
        per_device,
        mesh=mesh,
        in_specs=placed,
        out_specs=(
            P(("grp", "exp"), "ctx", None),
            P(("grp", "exp"), "ctx", None),
            P(("ctx", "exp"), None),
            P(("ctx", "exp"), None),
            P(),
            P(),
            P(),
            P("ctx", "exp", None, None),
            P("ctx", "exp", None),
        ),
        check_vma=False,
    )
```

profile of v0, /device:TPU:20, one launch (start us, length us, event | category | flops | bytes accessed | tf_op | source)
XLA Modules:
  0.0 2978.7 jit_solution(15623752981626158025)
XLA Ops:
  14.4 110.0 %all-gather.6.cloned.1.call-done = bf16[2048,5120]{1,0:T(8,128)(2,1)} async-done(((bf16[128,5120]{1,0:T(8,128)(2,1)}), bf16[2048,5120]{1,0:T(8,128)(2,1)}) %all-gather.6.cloned.1.call-update) | async-done | bytes 20971536 | tf_op jit(solution)/shard_map/all_gather | solution.py:75
  173.7 23.5 while.56
  197.2 31.4 %while.57 = (s32[]{:T(128)}, f32[4,2048,128]{2,1,0:T(8,128)}, s32[2]{0:T(128)S(1)}, s32[1,6]{1,0:T(1,128)S(1)}, s32[256]{0:T(256)S(1)}, /*index=5*/bf16[2,512,2,...) while((s32[]{:T(128)}, f32[4,2048,128]{2,1,0:T(8,128)}, ...), condition=%wide.region_14.15_spmd.clone, body=%wide.region_12.14_spmd.clone.sunk | while | flops 2170955008 | bytes 18134212 | solution.py:155
  237.2 54.2 %all-gather.10.cloned.1.call-done = bf16[2048,4096]{1,0:T(8,128)(2,1)} async-done(((bf16[128,4096]{1,0:T(8,128)(2,1)}), bf16[2048,4096]{1,0:T(8,128)(2,1)}) %all-gather.10.cloned.1.call-update) | async-done | bytes 16777232 | tf_op jit(solution)/shard_map/all_gather | solution.py:76
  353.5 198.4 %all-to-all-done = bf16[4,640,2048]{2,1,0:T(8,128)(2,1)} async-done(((bf16[4,640,2048]{2,1,0:T(8,128)(2,1)}), bf16[4,640,2048]{2,1,0:T(8,128)(2,1)}, u32[]{:S(2)}, u32[]{:S(2)}) %all-to-all-start) | async-done | bytes 10485792 | tf_op jit(solution)/shard_map/all_to_all | solution.py:187
  561.4 25.9 fusion.71
  587.3 198.6 %all-to-all-done.2 = bf16[4,640,2048]{2,1,0:T(8,128)(2,1)} async-done(((bf16[4,640,2048]{2,1,0:T(8,128)(2,1)}), bf16[4,640,2048]{2,1,0:T(8,128)(2,1)}, u32[]{:S(2)}, u32[]{:S(2)}) %all-to-all-start.2) | async-done | bytes 10485792 | tf_op jit(solution)/shard_map/all_to_all | solution.py:213
  786.0 21.8 fusion.94
  842.2 23.7 fusion.50
  876.0 190.3 %all-to-all-done.1 = bf16[4,640,2048]{2,1,0:T(8,128)(2,1)} async-done(((bf16[4,640,2048]{2,1,0:T(8,128)(2,1)}), bf16[4,640,2048]{2,1,0:T(8,128)(2,1)}, u32[]{:S(2)}, u32[]{:S(2)}) %all-to-all-start.1) | async-done | bytes 10485792 | tf_op jit(solution)/shard_map/all_to_all | solution.py:199
  1075.8 21.8 gather_fusion
  1107.4 192.6 %all-to-all-done.3 = bf16[4,640,2048]{2,1,0:T(8,128)(2,1)} async-done(((bf16[4,640,2048]{2,1,0:T(8,128)(2,1)}), bf16[4,640,2048]{2,1,0:T(8,128)(2,1)}, u32[]{:S(2)}, u32[]{:S(2)}) %all-to-all-start.3) | async-done | bytes 10485792 | tf_op jit(solution)/shard_map/all_to_all | solution.py:224
  1300.0 22.0 gather_fusion.1
  1351.3 30.3 %while.58 = (s32[]{:T(128)}, f32[4,2048]{1,0:T(4,128)S(1)}, s32[2]{0:T(128)S(1)}, s32[1,6]{1,0:T(1,128)S(1)}, s32[256]{0:T(256)S(1)}, /*index=5*/bf16[2,512,2,4,...) while((s32[]{:T(128)}, f32[4,2048]{1,0:T(4,128)S(1)}, ...), condition=%wide.region_35.36_spmd.clone, body=%wide.region_32.35_spmd.clone.sunk | while | flops 2173060352 | bytes 53916900 | solution.py:271
  1381.6 90.9 %while.59 = (s32[]{:T(128)}, f32[4,2048,128]{2,1,0:T(8,128)}, bf16[2,512,2,4,128]{4,1,3,2,0:T(8,128)(2,1)}, s32[2]{0:T(128)S(1)}, s32[1,6]{1,0:T(1,128)S(1)}, /*...) while((s32[]{:T(128)}, f32[4,2048,128]{2,1,0:T(8,128)}, ...), condition=%wide.region_38.39_spmd.clone, body=%wide.region_36.38_spmd.clone.sunk | while | flops 5425210368 | bytes 106804480 | solution.py:300
  1544.8 50.2 %pad_maximum_fusion = f32[2048,9216]{1,0:T(8,128)} fusion(f32[2048,4096]{1,0:T(8,128)} %fusion.118, f32[2048,5120]{1,0:T(8,128)} %fusion.110), kind=kLoop, calls=%fused_computation.81 | loop fusion | flops 18874368 | bytes 150994944 | tf_op jit(solution)/shard_map/concatenate | solution.py:350
  1612.8 30.0 %fusion.47 = bf16[2048,4,2,768]{0,3,2,1:T(8,128)(2,1)} fusion(bf16[4,4,160,2048,1]{3,2,1,0,4:T(8,128)(2,1)} %bitcast.25, bf16[4,4,160,1,768]{4,2,0,1,3:T(8,128)(2,1)} %get-tuple-element.971, bf16[4,4,160,1,768]{4,2,0,1,3:T(8,128)(2,1)} %get-tuple-element.970), kind=kOutput, calls=%fused_computation.84 | convolution fusion | flops 16122642432 | bytes 43515904 | tf_op jit(solution)/shard_map/secd,seckf->dekf/dot_general | solution.py:230
  1642.8 32.5 %pad_maximum_fusion.1 = bf16[2048,4,3,768]{0,3,2,1:T(8,128)(2,1)} fusion(bf16[2048,4,1,768]{0,3,2,1:T(8,128)(2,1)} %fusion.55, bf16[2048,4,2,768]{0,3,2,1:T(8,128)(2,1)} %fusion.47), kind=kLoop, calls=%fused_computation.83 | loop fusion | flops 18874368 | bytes 75497472 | tf_op jit(solution)/shard_map/concatenate | solution.py:237
  1675.3 625.6 %reduce-scatter.6.cloned.1.call-done = f32[128,9216]{1,0:T(8,128)} async-done(((f32[2048,9216]{1,0:T(8,128)}), f32[128,9216]{1,0:T(8,128)}) %reduce-scatter.6.cloned.1.call-update) | async-done | bytes 4718608 | tf_op jit(solution)/shard_map/reduce_scatter | solution.py:349
  2305.0 259.2 %reduce-scatter.8.cloned.1.call-done = bf16[512,4,3,768]{0,3,2,1:T(8,128)(2,1)} async-done(((bf16[2048,4,3,768]{0,3,2,1:T(8,128)(2,1)}), bf16[512,4,3,768]{0,3,2,1:T(8,128)(2,1)}) %reduce-scatter.8.cloned.1.call-update) | async-done | bytes 9437200 | tf_op jit(solution)/shard_map/reduce_scatter | solution.py:236
  2579.3 43.2 %all-reduce = (f32[2048,2]{0,1:T(2,128)}, f32[128,2]{0,1:T(2,128)}) all-reduce(f32[2048,2]{0,1:T(2,128)S(1)} %pad_maximum_fusion.11, f32[128,2]{0,1:T(2,128)S(1)} %pad_maximum_fusion.12), channel_id=1, replica_groups=mesh['grp'=2,'ctx'=4,'exp'=4] {'grp','ctx','exp'}, use_global_device_ids=true, to_apply=%region_47.48 | all-reduce | flops 4352 | bytes 34816 | tf_op jit(solution)/shard_map/psum | solution.py:342
  2625.7 216.1 %all-reduce.7.cloned.1.call-done = (bf16[128,9216]{1,0:T(8,128)(2,1)}, bf16[512,4,3,768]{0,3,2,1:T(8,128)(2,1)}) async-done(((bf16[128,9216]{1,0:T(8,128)(2,1)}, bf16[512,4,3,768]{0,3,2,1:T(8,128)(2,1)}), (bf16[128,9216]{1,0:T(8,128)(2,1)}, bf16[512,4,3,768]{0,3,2,1:T(8,128)(2,1)})) %all-reduce.7.cloned.1.call-update) | async-done | bytes 11796496 | tf_op jit(solution)/shard_map/psum | solution.py:356
  2871.0 19.4 copy.157
  2898.0 72.2 %all-reduce.5.cloned.1.call-done = f32[2048,16]{0,1:T(8,128)} async-done(((f32[2048,16]{0,1:T(8,128)}), f32[2048,16]{0,1:T(8,128)}) %all-reduce.5.cloned.1.call-update) | async-done | bytes 131088 | tf_op jit(solution)/shard_map/psum | solution.py:342
  (433 shorter events, 549.1 us)
Async XLA Ops:
  7.2 324.9 %copy-start = (bf16[2048,16]{0,1:T(8,128)(2,1)S(1)}, bf16[2048,16]{0,1:T(8,128)(2,1)}, u32[]{:S(2)}) copy-start(bf16[2048,16]{0,1:T(8,128)(2,1)} %param.27) | copy-start | bytes 196612
  7.2 117.2 %all-gather.6.cloned.1.call-start = ((), (), s32[]{:S(2)}) async-start(), calls=%async_computation.7 | async-start | bytes 22282240 | tf_op jit(solution)/shard_map/all_gather | solution.py:75
  7.9 158.4 %all-gather.8.cloned.1.call-start = ((), (), s32[]{:S(2)}) async-start(), calls=%async_computation.8 | async-start | bytes 2621440 | tf_op jit(solution)/shard_map/all_gather | solution.py:96
  11.8 125.8 %copy-start.80 = (f32[128]{0:T(128)}, f32[128]{0:T(128)S(1)}, u32[]{:S(2)}) copy-start(f32[128]{0:T(128)S(1)} %get-tuple-element.995) | copy-start | bytes 1540
  11.8 148.5 %copy-start.77 = (f32[128]{0:T(128)}, f32[128]{0:T(128)S(1)}, u32[]{:S(2)}) copy-start(f32[128]{0:T(128)S(1)} %get-tuple-element.994) | copy-start | bytes 1540
  11.8 122.8 %copy-start.60 = (f32[256]{0:T(256)}, f32[256]{0:T(256)S(1)}, u32[]{:S(2)}) copy-start(f32[256]{0:T(256)S(1)} %add_rsqrt_fusion.3) | copy-start | bytes 3076
  13.0 148.8 %copy-start.27 = (f32[256,64]{1,0:T(8,128)}, f32[256,64]{1,0:T(8,128)S(1)}, u32[]{:S(2)}) copy-start(f32[256,64]{1,0:T(8,128)S(1)} %get-tuple-element.993) | copy-start | bytes 196612
  14.4 120.2 %copy-start.40 = (f32[2048,1]{0,1:T(1,128)}, f32[2048,1]{0,1:T(1,128)S(1)}, u32[]{:S(2)}) copy-start(f32[2048,1]{0,1:T(1,128)S(1)} %get-tuple-element.990) | copy-start | bytes 24580
  140.4 151.0 %all-gather.10.cloned.1.call-start = ((), (), s32[]{:S(2)}) async-start(), calls=%async_computation.9 | async-start | bytes 17825792 | tf_op jit(solution)/shard_map/all_gather | solution.py:76
  141.2 420.2 %all-gather.12.cloned.1.call-start = ((), (), s32[]{:S(2)}) async-start(), calls=%async_computation.10 | async-start | bytes 31457280 | tf_op jit(solution)/shard_map/all_gather | solution.py:97
  319.2 232.7 %all-to-all-start = ((bf16[4,640,2048]{2,1,0:T(8,128)(2,1)}), bf16[4,640,2048]{2,1,0:T(8,128)(2,1)}, u32[]{:S(2)}, u32[]{:S(2)}) async-start(bf16[4,640,2048]{2,1,0:T(8,128)(2,1)} %bitcast.524), calls=%async_computation | async-start | bytes 20971520 | tf_op jit(solution)/shard_map/all_to_all | solution.py:187
  326.5 260.8 %all-gather.14.cloned.1.call-start = ((), (), s32[]{:S(2)}) async-start(), calls=%async_computation.11 | async-start | bytes 15728640 | tf_op jit(solution)/shard_map/all_gather | solution.py:98
  332.5 219.4 %copy-start.69 = (f32[256]{0:T(256)}, f32[256]{0:T(256)S(1)}, u32[]{:S(2)}) copy-start(f32[256]{0:T(256)S(1)} %get-tuple-element.998) | copy-start | bytes 3076
  551.9 234.1 %all-to-all-start.2 = ((bf16[4,640,2048]{2,1,0:T(8,128)(2,1)}), bf16[4,640,2048]{2,1,0:T(8,128)(2,1)}, u32[]{:S(2)}, u32[]{:S(2)}) async-start(bf16[4,640,2048]{2,1,0:T(8,128)(2,1)} %bitcast.525), calls=%async_computation.2 | async-start | bytes 20971520 | tf_op jit(solution)/shard_map/all_to_all | solution.py:213
  832.8 233.5 %all-to-all-start.1 = ((bf16[4,640,2048]{2,1,0:T(8,128)(2,1)}), bf16[4,640,2048]{2,1,0:T(8,128)(2,1)}, u32[]{:S(2)}, u32[]{:S(2)}) async-start(bf16[4,640,2048]{2,1,0:T(8,128)(2,1)} %bitcast.526), calls=%async_computation.1 | async-start | bytes 20971520 | tf_op jit(solution)/shard_map/all_to_all | solution.py:199
  1066.4 233.6 %all-to-all-start.3 = ((bf16[4,640,2048]{2,1,0:T(8,128)(2,1)}), bf16[4,640,2048]{2,1,0:T(8,128)(2,1)}, u32[]{:S(2)}, u32[]{:S(2)}) async-start(bf16[4,640,2048]{2,1,0:T(8,128)(2,1)} %bitcast.523), calls=%async_computation.3 | async-start | bytes 20971520 | tf_op jit(solution)/shard_map/all_to_all | solution.py:224
  1075.8 442.7 %reduce-scatter.4.cloned.1.call-start = ((), (), s32[]{:S(2)}) async-start(), calls=%async_computation.12 | async-start | bytes 2621440 | tf_op jit(solution)/shard_map/reduce_scatter | solution.py:301
  1107.4 226.1 %copy-start.46 = (f32[256,16]{0,1:T(8,128)}, f32[256,16]{0,1:T(8,128)S(1)}, u32[]{:S(2)}) copy-start(f32[256,16]{0,1:T(8,128)S(1)} %select_reduce_fusion.3) | copy-start | bytes 49156
  1107.4 226.1 %copy-start.75 = (f32[256]{0:T(256)}, f32[256]{0:T(256)S(1)}, u32[]{:S(2)}) copy-start(f32[256]{0:T(256)S(1)} %multiply_reduce_fusion.7) | copy-start | bytes 3076
  1477.9 823.0 %reduce-scatter.6.cloned.1.call-start = ((), (), s32[]{:S(2)}) async-start(), calls=%async_computation.13 | async-start | bytes 80216064 | tf_op jit(solution)/shard_map/reduce_scatter | solution.py:349
  1595.0 969.2 %reduce-scatter.8.cloned.1.call-start = ((), (), s32[]{:S(2)}) async-start(), calls=%async_computation.15 | async-start | bytes 47185920 | tf_op jit(solution)/shard_map/reduce_scatter | solution.py:236
  1675.3 1166.5 %all-reduce.7.cloned.1.call-start = ((), (), s32[]{:S(2)}) async-start(), calls=%async_computation.16 | async-start | bytes 23592960 | tf_op jit(solution)/shard_map/psum | solution.py:356
  2564.3 405.9 %all-reduce.5.cloned.1.call-start = ((), (), s32[]{:S(2)}) async-start(), calls=%async_computation.14 | async-start | bytes 262144 | tf_op jit(solution)/shard_map/psum | solution.py:342
  2871.0 100.7 %copy-start.1 = (bf16[2048,16]{0,1:T(8,128)(2,1)S(1)}, bf16[2048,16]{0,1:T(8,128)(2,1)}, u32[]{:S(2)}) copy-start(bf16[2048,16]{0,1:T(8,128)(2,1)} %param.27) | copy-start | bytes 196612
  (80 other events, 707.4 us)
Sparse Core Ops, SparseCore 0:
  9.6 114.8 all-gather.5
  140.6 22.5 all-gather.7
  165.4 125.9 all-gather.9
  293.4 153.5 all-gather.11
  448.5 82.0 all-gather.13
  1478.0 32.3 reduce-scatter.3
  1595.1 705.7 reduce-scatter.5
  2303.5 260.6 reduce-scatter.7
  2567.4 274.2 all-reduce.6
  2848.6 121.4 all-reduce.4
where the time goes:
time: 2990 us; the launch traced here: 2980 us
  waiting for transfers between devices  2120 us (71%)
  matrix products  338 us (11%)
  other arithmetic  212 us (7%)
  local copies, waits for them, and re-layouts  210 us (7%)
  blocking collectives  43.2 us (1%)
  starting transfers between devices  35.9 us (1%)
    reduce_scatter x1, waiting for transfers between devices, per_device(): lax.psum_scatter(jnp.concatenate([part_in, part_out], axis=1), ('ctx', 'e...  626 us
    reduce_scatter x1, waiting for transfers between devices, per_device(): lax.psum_scatter(jnp.concatenate([term_in, term_out[:, :, None, :]], axis...  259 us
    psum x1, waiting for transfers between devices, per_device(): lax.psum(dense_local.astype(jnp.bfloat16), 'grp').astype(jnp.float32)  216 us
    all_to_all x1, waiting for transfers between devices, per_device(): lax.all_to_all(outgoing_grads.reshape(buffer_shape), 'exp', split_axis=0,...  199 us
    all_to_all x1, waiting for transfers between devices, per_device(): lax.all_to_all(outgoing.reshape(buffer_shape), 'exp', split_axis=0, conca...  198 us
    all_to_all x1, waiting for transfers between devices, per_device(): lax.all_to_all(input_rows.reshape(buffer_shape), 'exp', split_axis=0, con...  193 us
    all_to_all x1, waiting for transfers between devices, per_device(): lax.all_to_all(made.reshape(buffer_shape), 'exp', split_axis=0, concat_ax...  190 us
    all_gather x1, waiting for transfers between devices, per_device(): lax.all_gather(attention_input_weight, ('ctx', 'exp'), axis=0, tiled=True)  110 us
  transfers between devices with their start and end apart: 14, of which 10 were waited for; matrix products, arithmetic and copies ran while one was open for 15% of the time, Pallas kernels for 0%

commit v1 on v0

--- a/solution.py
+++ b/solution.py
@@ -1,6 +1,10 @@
+import functools
+
 import jax
 import jax.numpy as jnp
 from jax import lax
+from jax.experimental import pallas as pl
+from jax.experimental.pallas import tpu as pltpu
 from jax.sharding import PartitionSpec as P
 
 epsilon = 1e-06
@@ -40,7 +44,7 @@
     return scale_vec * (along - unit_vec * jnp.mean(along * unit_vec, axis=-1, keepdims=True))
 
 
-def per_device(
+def per_device_general(
     hidden_in,
     out_grad,
     doc_lengths,
@@ -369,6 +373,517 @@
     )
 
 
+NT = (((1,), (1,)), ((), ()))
+
+def head_norm(raw):
+    scale = lax.rsqrt(jnp.mean(raw * raw, axis=-1, keepdims=True) + epsilon)
+    return raw * scale, scale
+
+def turn(values, cosine, sine):
+    return values * cosine + pltpu.roll(values, values.shape[-1] // 2, 1) * sine
+
+def dots(a, b):
+    return jnp.dot(a, b, preferred_element_type=jnp.float32)
+
+def dots_nt(a, b):
+    return lax.dot_general(a, b, NT, preferred_element_type=jnp.float32)
+
+def allowed_chunk(start, i, j, tile):
+    key_pos = j * tile + lax.broadcasted_iota(jnp.int32, (tile, tile), 0)
+    ok = key_pos >= start
+    if i == j:
+        query_pos = i * tile + lax.broadcasted_iota(jnp.int32, (tile, tile), 1)
+        ok = ok & (key_pos <= query_pos)
+    return ok
+
+def attend_kernel(tile, q_ref, k_ref, v_ref, cos_ref, sin_ref, start_ref, gain_ref,
+                  o_ref, lse_ref, key_s, value_t):
+    length, head_dim = q_ref.shape
+    c = head_dim ** -0.5 * 1.4426950408889634
+    @pl.when(pl.program_id(0) == 0)
+    def _():
+        unit, _ = head_norm(k_ref[...])
+        key_s[...] = turn(unit * gain_ref[1:2], cos_ref[...], sin_ref[...]).astype(jnp.bfloat16)
+        value_t[...] = v_ref[...].T.astype(jnp.bfloat16)
+    unit, _ = head_norm(q_ref[...])
+    query = turn(unit * gain_ref[0:1], cos_ref[...], sin_ref[...]).astype(jnp.bfloat16)
+    for i in range(length // tile):
+        rows = slice(i * tile, (i + 1) * tile)
+        start = start_ref[:, rows]
+        mass = jnp.zeros((1, tile), jnp.float32)
+        total = jnp.zeros((head_dim, tile), jnp.float32)
+        for j in range(i + 1):
+            cols = slice(j * tile, (j + 1) * tile)
+            s = dots_nt(key_s[cols, :], query[rows])
+            p = jnp.where(allowed_chunk(start, i, j, tile), jnp.exp2(s * c), 0.0)
+            mass = mass + jnp.sum(p, axis=0, keepdims=True)
+            total = total + dots(value_t[:, cols], p.astype(jnp.bfloat16))
+        o_ref[rows, :] = (total / mass).T.astype(jnp.bfloat16)
+        lse_ref[0, :, rows] = jnp.log2(mass)
+
+def attend(qkv, cosine, sine, start, gains, heads):
+    length, head_dim = cosine.shape
+    full = lambda shape: pl.BlockSpec(shape, lambda h: (0, 0))
+    col = lambda at: pl.BlockSpec((length, head_dim), lambda h: (0, at))
+    return pl.pallas_call(
+        functools.partial(attend_kernel, min(256, length)),
+        grid=(heads,),
+        in_specs=[
+            pl.BlockSpec((length, head_dim), lambda h: (0, h)), col(heads), col(heads + 1),
+            full((length, head_dim)), full((length, head_dim)), full((1, length)), full(gains.shape),
+        ],
+        out_specs=[
+            pl.BlockSpec((length, head_dim), lambda h: (0, h)),
+            pl.BlockSpec((1, 1, length), lambda h: (h, 0, 0)),
+        ],
+        out_shape=[
+            jax.ShapeDtypeStruct((length, heads * head_dim), jnp.bfloat16),
+            jax.ShapeDtypeStruct((heads, 1, length), jnp.float32),
+        ],
+        scratch_shapes=[
+            pltpu.VMEM((length, head_dim), jnp.bfloat16),
+            pltpu.VMEM((head_dim, length), jnp.bfloat16),
+        ],
+        compiler_params=pltpu.CompilerParams(vmem_limit_bytes=48 * 2**20),
+    )(qkv, qkv, qkv, cosine, sine, start, gains)
+
+def attend_back_kernel(tile, heads, q_ref, k_ref, v_ref, cos_ref, sin_ref, start_ref, gain_ref,
+                       o_ref, go_ref, lse_ref, grad_ref, gain_grad_ref,
+                       key_s, key_t, value_s, key_grad, value_grad, query_grad):
+    length, head_dim = q_ref.shape
+    scale = head_dim ** -0.5
+    c = scale * 1.4426950408889634
+    step = pl.program_id(0)
+
+    def norm_back(turned_grad, raw, row):
+        back = turn(turned_grad, cos_ref[...], -sin_ref[...])
+        unit, unit_scale = head_norm(raw)
+        gain_grad_ref[row:row + 1] += jnp.sum(back * unit, axis=0, keepdims=True)
+        along = back * gain_ref[row:row + 1]
+        return unit_scale * (along - unit * jnp.mean(along * unit, axis=-1, keepdims=True))
+
+    @pl.when(step == 0)
+    def _():
+        unit, _ = head_norm(k_ref[...])
+        key = turn(unit * gain_ref[1:2], cos_ref[...], sin_ref[...])
+        key_s[...] = key.astype(jnp.bfloat16)
+        key_t[...] = key.T.astype(jnp.bfloat16)
+        value_s[...] = v_ref[...].astype(jnp.bfloat16)
+        key_grad[...] = jnp.zeros_like(key_grad)
+        value_grad[...] = jnp.zeros_like(value_grad)
+        gain_grad_ref[...] = jnp.zeros_like(gain_grad_ref)
+
+    @pl.when(step < heads)
+    def _():
+        unit, _ = head_norm(q_ref[...])
+        query = turn(unit * gain_ref[0:1], cos_ref[...], sin_ref[...]).astype(jnp.bfloat16)
+        for i in range(length // tile):
+            rows = slice(i * tile, (i + 1) * tile)
+            start = start_ref[:, rows]
+            lse = lse_ref[0, :, rows]
+            up = go_ref[rows, :]
+            delta = jnp.sum((up.astype(jnp.float32) * o_ref[rows, :].astype(jnp.float32)).T, axis=0, keepdims=True)
+            q_i = query[rows]
+            total = jnp.zeros((head_dim, tile), jnp.float32)
+            for j in range(i + 1):
+                cols = slice(j * tile, (j + 1) * tile)
+                s = dots_nt(key_s[cols, :], q_i)
+                p = jnp.where(allowed_chunk(start, i, j, tile), jnp.exp2(s * c - lse), 0.0)
+                dp = dots_nt(value_s[cols, :], up)
+                ds = (p * (dp - delta)).astype(jnp.bfloat16)
+                value_grad[cols, :] += dots(p.astype(jnp.bfloat16), up)
+                key_grad[cols, :] += dots(ds, q_i)
+                total = total + dots(key_t[:, cols], ds)
+            query_grad[rows, :] = (total * scale).T
+        grad_ref[...] = norm_back(query_grad[...], q_ref[...], 0).astype(jnp.bfloat16)
+
+    @pl.when(step == heads)
+    def _():
+        grad_ref[...] = norm_back(key_grad[...] * scale, k_ref[...], 1).astype(jnp.bfloat16)
+
+    @pl.when(step == heads + 1)
+    def _():
+        grad_ref[...] = value_grad[...].astype(jnp.bfloat16)
+
+def attend_back(qkv, cosine, sine, start, gains, attended, upstream, lse, heads):
+    length, head_dim = cosine.shape
+    full = lambda shape: pl.BlockSpec(shape, lambda h: (0, 0))
+    col = lambda at: pl.BlockSpec((length, head_dim), lambda h: (0, at))
+    per_head = pl.BlockSpec((length, head_dim), lambda h: (0, jnp.minimum(h, heads - 1)))
+    return pl.pallas_call(
+        functools.partial(attend_back_kernel, min(256, length), heads),
+        grid=(heads + 2,),
+        in_specs=[
+            per_head, col(heads), col(heads + 1),
+            full((length, head_dim)), full((length, head_dim)), full((1, length)), full(gains.shape),
+            per_head, per_head,
+            pl.BlockSpec((1, 1, length), lambda h: (jnp.minimum(h, heads - 1), 0, 0)),
+        ],
+        out_specs=[
+            pl.BlockSpec((length, head_dim), lambda h: (0, h)),
+            full((8, head_dim)),
+        ],
+        out_shape=[
+            jax.ShapeDtypeStruct((length, (heads + 2) * head_dim), jnp.bfloat16),
+            jax.ShapeDtypeStruct((8, head_dim), jnp.float32),
+        ],
+        scratch_shapes=[
+            pltpu.VMEM((length, head_dim), jnp.bfloat16),
+            pltpu.VMEM((head_dim, length), jnp.bfloat16),
+            pltpu.VMEM((length, head_dim), jnp.bfloat16),
+            pltpu.VMEM((length, head_dim), jnp.float32),
+            pltpu.VMEM((length, head_dim), jnp.float32),
+            pltpu.VMEM((length, head_dim), jnp.float32),
+        ],
+        compiler_params=pltpu.CompilerParams(vmem_limit_bytes=48 * 2**20),
+    )(qkv, qkv, qkv, cosine, sine, start, gains, attended, upstream, lse)
+
+
+low = jnp.bfloat16
+
+
+def swap_on(value, axis, mask):
+    count = lax.axis_size(axis)
+    return lax.ppermute(value, axis, [(i, i ^ mask) for i in range(count)])
+
+
+def line_gather(block, axis):
+    n = lax.axis_size(axis)
+    rights, lefts = [block], [block]
+    for s in range(1, n):
+        rights.append(lax.ppermute(rights[-1], axis, [(i, i + 1) for i in range(s - 1, n - 1)]))
+        lefts.append(lax.ppermute(lefts[-1], axis, [(i, i - 1) for i in range(1, n - s + 1)]))
+    return [block] + [rights[s] + lefts[n - s] for s in range(1, n)]
+
+
+def line_scatter(parts, axis):
+    n = lax.axis_size(axis)
+    right = left = None
+    for s in range(1, n):
+        to_right = parts[n - s] if right is None else add_low(parts[n - s], right)
+        to_left = parts[s] if left is None else add_low(parts[s], left)
+        right = lax.ppermute(to_right, axis, [(i, i + 1) for i in range(s)])
+        left = lax.ppermute(to_left, axis, [(i, i - 1) for i in range(n - s, n)])
+    return parts[0].astype(jnp.float32) + right.astype(jnp.float32) + left.astype(jnp.float32)
+
+
+def add_low(a, b):
+    return (a.astype(jnp.float32) + b.astype(jnp.float32)).astype(low)
+
+
+def pick(array, index):
+    return lax.dynamic_index_in_dim(array, index, 0, keepdims=False)
+
+
+def per_device(
+    hidden_in,
+    out_grad,
+    doc_lengths,
+    routes,
+    attention_input_weight,
+    attn_out_weight,
+    norm_gains,
+    head_gains,
+    router_weight,
+    expert_in,
+    expert_out,
+):
+    hidden = hidden_in[0].astype(jnp.float32)
+    rows, width = hidden.shape
+    head_dim = head_gains.shape[0]
+    expert_count = router_weight.shape[1]
+    top = routes.shape[2]
+    n_ctx, n_exp = lax.axis_size("ctx"), lax.axis_size("exp")
+    grp, ctx, exp = lax.axis_index("grp"), lax.axis_index("ctx"), lax.axis_index("exp")
+    half, core = ctx // 2, ctx % 2
+    length = rows * n_ctx
+    query_width = attn_out_weight.shape[1]
+    kv_width = (attention_input_weight.shape[1] - query_width) // 2
+    heads = query_width // head_dim // n_ctx
+    shard = attention_input_weight.shape[0]
+    f32 = jnp.float32
+
+    def dot(a, b):
+        return jnp.dot(a, b, preferred_element_type=f32)
+
+    def dot_nt(a, b):
+        return lax.dot_general(a, b, (((1,), (1,)), ((), ())), preferred_element_type=f32)
+
+    def dot_tn(a, b):
+        return lax.dot_general(a, b, (((0,), (0,)), ((), ())), preferred_element_type=f32)
+
+    def by_exp(a):
+        return a.reshape(a.shape[0], n_ctx, n_exp, shard).transpose(0, 2, 1, 3).reshape(a.shape)
+
+    def by_ctx(a):
+        return a.reshape(a.shape[0], n_exp, n_ctx, shard).transpose(0, 2, 1, 3).reshape(a.shape)
+
+    def own_half_first(a):
+        return jnp.where(half == 0, a, jnp.concatenate([a[:, width // 2 :], a[:, : width // 2]], 1))
+
+    def gather_ctx(block):
+        over = swap_on(block, "ctx", 2)
+        blocks = [block, swap_on(block, "ctx", 1), over, swap_on(over, "ctx", 1)]
+        return place_ctx(blocks)
+
+    def place_ctx(blocks):
+        out = jnp.zeros((n_ctx,) + blocks[0].shape, blocks[0].dtype)
+        for m in range(n_ctx):
+            out = lax.dynamic_update_index_in_dim(out, blocks[m], ctx ^ m, 0)
+        return out
+
+    def scatter_ctx(parts):
+        got = swap_on(jnp.stack([pick(parts, ctx ^ 1), pick(parts, ctx ^ 3)]), "ctx", 1)
+        mine = pick(parts, ctx).astype(f32) + got[0].astype(f32)
+        other = add_low(pick(parts, ctx ^ 2), got[1])
+        return mine + swap_on(other, "ctx", 2).astype(f32)
+
+    positions = jnp.arange(length, dtype=jnp.int32)
+    relative = doc_tables(doc_lengths[0], positions)[1]
+    doc_start = (positions - relative)[None, :]
+    freqs = rotary_base ** (-2.0 * jnp.arange(head_dim // 2, dtype=f32) / head_dim)
+    angles = relative.astype(f32)[:, None] * freqs[None, :]
+    cosine = jnp.concatenate([jnp.cos(angles)] * 2, 1)
+    sine = jnp.concatenate([-jnp.sin(angles), jnp.sin(angles)], 1)
+    gains = jnp.pad(head_gains.astype(f32).T, ((0, 6), (0, 0)))
+    gain_attn = norm_gains[:, 0].astype(f32)
+    gain_ffn = norm_gains[:, 1].astype(f32)
+
+    def weight_in_of(at):
+        return jnp.concatenate(
+            [
+                lax.dynamic_slice_in_dim(attention_input_weight, at * heads * head_dim, heads * head_dim, 1),
+                lax.dynamic_slice_in_dim(attention_input_weight, query_width + at * head_dim, head_dim, 1),
+                lax.dynamic_slice_in_dim(
+                    attention_input_weight, query_width + kv_width + at * head_dim, head_dim, 1
+                ),
+            ],
+            1,
+        )
+
+    def weight_out_of(at):
+        return lax.dynamic_slice_in_dim(attn_out_weight, at * heads * head_dim, heads * head_dim, 1)
+
+    def all_rows(piece_of):
+        blocks = [piece_of(ctx)] + [swap_on(piece_of(ctx ^ m), "ctx", m) for m in range(1, n_ctx)]
+        block = place_ctx(blocks)
+        blocks = line_gather(block, "exp")
+        out = jnp.zeros((n_exp,) + block.shape, block.dtype)
+        for s in range(n_exp):
+            out = lax.dynamic_update_index_in_dim(out, blocks[s], (exp - s) % n_exp, 0)
+        return out.reshape(width, block.shape[-1])
+
+    normed, hidden_unit, hidden_scale = norm_forward(hidden, gain_attn)
+    normed_seq = gather_ctx(by_exp(normed.astype(low))).reshape(length, width)
+    weight_in = all_rows(weight_in_of)
+    weight_out = all_rows(weight_out_of)
+
+    capacity = 5 * rows * top // (4 * expert_count)
+    hits = jnp.any(routes[0][:, :, None] == jnp.arange(expert_count, dtype=jnp.int32), axis=1)
+    before = jnp.tril(jnp.ones((rows, rows), low), -1)
+    slots = jnp.where(hits, dot(before, hits.astype(low)), -1.0).T
+    slots_all = lax.all_gather(slots, ("ctx", "exp"), axis=0).reshape(n_ctx, n_exp, expert_count, rows)
+    order = [(s, j) for s in range(n_exp) for j in range(2)]
+    slots_of = jnp.stack([pick(pick(slots_all, ctx ^ j), (exp - s) % n_exp) for s, j in order])
+
+    local_experts = expert_in.shape[1]
+    hidden_units = expert_out.shape[2]
+    quarter = expert_in.shape[0]
+
+    def expert_rows(at):
+        return jnp.concatenate(
+            [
+                lax.dynamic_index_in_dim(expert_in, at, 1, keepdims=False).reshape(quarter, -1),
+                lax.dynamic_index_in_dim(expert_out, at, 1, keepdims=False),
+            ],
+            1,
+        )
+
+    here = [2 * core + (1 - grp), 2 * core + grp]
+    there = [2 * (1 - core) + (1 - grp), 2 * (1 - core) + grp]
+    over_same = swap_on(expert_rows(here[0]), "ctx", 2)
+    over_other = swap_on(expert_rows(there[0]), "ctx", 3)
+    expert_weights = []
+    for j in range(2):
+        same, other = expert_rows(here[j]), swap_on(expert_rows(there[j]), "ctx", 1)
+        if j == 1:
+            over_same, over_other = swap_on(over_same, "grp", 1), swap_on(over_other, "grp", 1)
+        expert_weights.append(
+            jnp.concatenate(
+                [
+                    jnp.where(core == 0, same, other),
+                    jnp.where(core == 0, other, same),
+                    jnp.where(core == 0, over_same, over_other),
+                    jnp.where(core == 0, over_other, over_same),
+                ]
+            )
+        )
+
+    def gather_tokens(block):
+        blocks = line_gather(block, "exp")
+        return jnp.stack([b for own in blocks for b in (own, swap_on(own, "ctx", 1))])
+
+    qkv = dot(normed_seq, weight_in)
+    attended, log_mass = attend(qkv, cosine, sine, doc_start, gains, heads)
+    branch = dot_nt(attended, weight_out).astype(low).reshape(n_ctx, rows, width)
+    middle = hidden + by_ctx(scatter_ctx(branch))
+    ffn_normed, middle_unit, middle_scale = norm_forward(middle, gain_ffn)
+    ffn_low = ffn_normed.astype(low)
+
+    tokens = gather_tokens(own_half_first(ffn_low))
+    upstreams = gather_tokens(own_half_first(out_grad[0]))
+    router_here = jnp.where(
+        half == 0, router_weight, jnp.concatenate([router_weight[width // 2 :], router_weight[: width // 2]])
+    )
+    logits = dot(tokens.reshape(-1, width), router_here)
+    probs_all = jax.nn.softmax(logits, axis=-1).reshape(len(order), rows, expert_count)
+    selected = jnp.where(slots_of.transpose(0, 2, 1) >= 0, probs_all, 0.0)
+    sel_sums = jnp.sum(selected, axis=-1, keepdims=True)
+    gates_all = selected / sel_sums
+    probs, sel_total = probs_all[0], sel_sums[0]
+    gates = gates_all[0]
+
+    mixed, sent, tables, gate_grad_parts, grad_halves = [], [], [], [], []
+    for j in range(2):
+        expert = exp * local_experts + here[j]
+        slot = lax.dynamic_index_in_dim(slots_of, expert, 1, keepdims=False)
+        table = slot[:, None, :] == jnp.arange(capacity, dtype=f32)[None, :, None]
+        gate_rows = lax.dynamic_index_in_dim(gates_all, expert, 2, keepdims=False)
+        gate_slots = jnp.sum(jnp.where(table, gate_rows[:, None, :], 0.0), axis=-1)
+        table_low = table.astype(low)
+        gather = lambda a: jnp.einsum(
+            "bct,btd->bcd", table_low, a, preferred_element_type=f32
+        ).reshape(-1, width)
+        inputs = gather(tokens).astype(low)
+        ups = gather(upstreams)
+        grads = (ups * gate_slots.reshape(-1, 1)).astype(low)
+        weight = expert_weights[j]
+        into, outof = weight[:, : 2 * hidden_units], weight[:, 2 * hidden_units :]
+        gate_up = dot(inputs, into)
+        gate_part, up_part = gate_up[:, :hidden_units], gate_up[:, hidden_units:]
+        sigmoid_part = jax.nn.sigmoid(gate_part)
+        silu_part = gate_part * sigmoid_part
+        act = (silu_part * up_part).astype(low)
+        made = dot_nt(act, outof).astype(low)
+        act_grad = dot(grads, outof)
+        gate_grad = act_grad * up_part * sigmoid_part * (1.0 + gate_part * (1.0 - sigmoid_part))
+        gate_up_grad = jnp.concatenate([gate_grad, act_grad * silu_part], 1).astype(low)
+        sent.append(dot_nt(gate_up_grad, into).astype(low).reshape(len(order), capacity, width))
+        gate_grad_slots = jnp.sum(ups * made.astype(f32), axis=-1).reshape(len(order), capacity)
+        gate_grad_parts.append(jnp.sum(jnp.where(table, gate_grad_slots[:, :, None], 0.0), axis=1))
+        mixed.append(
+            (made.astype(f32) * gate_slots.reshape(-1, 1)).astype(low).reshape(len(order), capacity, width)
+        )
+        tables.append(table_low)
+        grad = jnp.concatenate([dot_tn(inputs, gate_up_grad), dot_tn(grads, act)], 1).astype(low)
+        grad_halves.append(
+            grad[: width // 2].astype(f32) + swap_on(grad[width // 2 :], "ctx", 2).astype(f32)
+        )
+
+    both = jnp.concatenate(tables, 1)
+
+    def back_to_tokens(parts):
+        summed = jnp.einsum(
+            "bct,bcd->btd", both, jnp.concatenate(parts, 1), preferred_element_type=f32
+        ).astype(low)
+        summed = summed.reshape(n_exp, 2, rows, width)
+        mine = add_low(summed[:, 0], swap_on(summed[:, 1], "ctx", 1))
+        return own_half_first(line_scatter([mine[(-o) % n_exp] for o in range(n_exp)], "exp"))
+
+    sent_grads = back_to_tokens(sent)
+    gate_parts = lax.all_gather(jnp.stack(gate_grad_parts, 1), ("ctx", "exp"), axis=0).reshape(
+        n_ctx, n_exp, len(order), 2, rows
+    )
+    expert_ids = jnp.arange(expert_count, dtype=jnp.int32)
+    gate_grads = jnp.zeros((rows, expert_count), f32)
+    for at, (s, j) in enumerate(order):
+        owner = (exp + s) % n_exp
+        piece = pick(pick(gate_parts, ctx ^ j), owner)[at]
+        there_core = core ^ j
+        for i, first in enumerate((1 - grp, grp)):
+            expert = owner * local_experts + 2 * there_core + first
+            gate_grads = gate_grads + jnp.where(expert_ids[None, :] == expert, piece[i][:, None], 0.0)
+
+    weighted = jnp.sum(gate_grads * gates, axis=1, keepdims=True)
+    prob_grads = jnp.where(hits, (gate_grads - weighted) / sel_total, 0.0)
+    logit_grads = probs * (prob_grads - jnp.sum(probs * prob_grads, axis=1, keepdims=True))
+    router_float = router_weight.astype(f32)
+    ffn_grads = sent_grads + jnp.dot(logit_grads, router_float.T, precision=lax.Precision.HIGHEST)
+    router_grads = jnp.dot(ffn_low.astype(f32).T, logit_grads, precision=lax.Precision.HIGHEST)
+    middle_grad = out_grad[0].astype(f32) + norm_backward(ffn_grads, middle_unit, middle_scale, gain_ffn)
+
+    branch_grad = gather_ctx(by_exp(middle_grad.astype(low))).reshape(length, width)
+    heads_grad = dot(branch_grad, weight_out).astype(low)
+    joined_grads, gain_grads = attend_back(
+        qkv, cosine, sine, doc_start, gains, attended, heads_grad, log_mass, heads
+    )
+    part_out = dot_tn(branch_grad, attended).astype(low)
+    part_in = dot_tn(normed_seq, joined_grads).astype(low)
+    normed_parts = dot_nt(joined_grads, weight_in).astype(low).reshape(n_ctx, rows, width)
+    normed_grads = by_ctx(scatter_ctx(normed_parts))
+    input_part = norm_backward(normed_grads, hidden_unit, hidden_scale, gain_attn)
+    input_grad = (middle_grad + input_part).astype(low)[None]
+
+    mixture = back_to_tokens(mixed)
+    output = (middle + mixture).astype(low)[None]
+
+    kept = add_low(grad_halves[1], swap_on(grad_halves[0].astype(low), "grp", 1)).reshape(2, quarter, -1)
+    mine = pick(kept, core)
+    sibling = swap_on(pick(kept, 1 - core), "ctx", 1)
+    mine_x, sibling_x = swap_on(mine, "grp", 1), swap_on(sibling, "grp", 1)
+    totals = []
+    for at in range(local_experts):
+        same_core = at // 2 == core
+        same_grp = at % 2 == grp
+        totals.append(
+            jnp.where(
+                same_core, jnp.where(same_grp, mine, mine_x), jnp.where(same_grp, sibling, sibling_x)
+            ).astype(f32)
+        )
+    total = jnp.stack(totals, 1)
+    expert_in_grad = total[:, :, : 2 * hidden_units].reshape(expert_in.shape)
+    expert_out_grad = total[:, :, 2 * hidden_units :]
+
+    def to_rows(part):
+        blocks = part.reshape(n_exp, n_ctx * shard, part.shape[1])
+        own = line_scatter([pick(blocks, (exp + o) % n_exp) for o in range(n_exp)], "exp")
+        own = own.astype(low).reshape(n_ctx, shard, part.shape[1])
+        pieces = [pick(own, ctx)] + [swap_on(pick(own, ctx ^ m), "ctx", m) for m in range(1, n_ctx)]
+        placed = place_ctx(pieces)
+        return placed.astype(f32) + swap_on(placed, "grp", 1).astype(f32)
+
+    rows_out = to_rows(part_out)
+    rows_in = to_rows(part_in)
+    attn_out_grad = rows_out.transpose(1, 0, 2).reshape(shard, query_width)
+    wide = heads * head_dim
+    attn_in_grad = jnp.concatenate(
+        [
+            rows_in[:, :, :wide].transpose(1, 0, 2).reshape(shard, query_width),
+            rows_in[:, :, wide : wide + head_dim].transpose(1, 0, 2).reshape(shard, kv_width),
+            rows_in[:, :, wide + head_dim :].transpose(1, 0, 2).reshape(shard, kv_width),
+        ],
+        1,
+    )
+
+    norm_gain_grads = jnp.stack(
+        [jnp.sum(normed_grads * hidden_unit, axis=0), jnp.sum(ffn_grads * middle_unit, axis=0)], axis=1
+    )
+    norm_total, head_total, router_total = lax.psum(
+        (norm_gain_grads, gain_grads[:2].T, router_grads), ("grp", "ctx", "exp")
+    )
+    return (
+        output,
+        input_grad,
+        attn_in_grad,
+        attn_out_grad,
+        norm_total,
+        head_total,
+        router_total,
+        expert_in_grad,
+        expert_out_grad,
+    )
+
+
 def solution(mesh):
     placed = (
         P(("grp", "exp"), "ctx", None),
@@ -383,8 +898,10 @@
         P("ctx", "exp", None, None),
         P("ctx", "exp", None),
     )
+    sizes = dict(mesh.shape)
+    body = per_device if sizes == {"grp": 2, "ctx": 4, "exp": 4} else per_device_general
     return jax.shard_map(
-        per_device,
+        body,
         mesh=mesh,
         in_specs=placed,
         out_specs=(

time: 2990 us -> 1510 us (0.51)
  waiting for transfers between devices: 2120 us -> 382 us
  starting transfers between devices: 35.9 us -> 176 us
  matrix products: 338 us -> 221 us
  blocking collectives: 43.2 us -> 141 us
  local copies, waits for them, and re-layouts: 210 us -> 268 us
  Pallas kernels: 0 us -> 44.4 us
  other arithmetic: 212 us -> 245 us
    reduce_scatter x3 -> x0, waiting for transfers between devices: 885 us -> none  [the longest x1 626 us: per_device(): lax.psum_scatter(jnp.concatenate([part_in, part_out], axis=1), ('ctx', 'e...]
    all_to_all x4 -> x0, waiting for transfers between devices: 780 us -> none  [the longest x1 199 us: per_device(): lax.all_to_all(outgoing_grads.reshape(buffer_shape), 'exp', split_axis=0,...]
    ppermute x0 -> x94, waiting for transfers between devices: none -> 382 us  [the longest x46 132 us: swap_on(): return lax.ppermute(value, axis, [(i, i ^ mask) for i in range(count)])]
    psum x2 -> x1, waiting for transfers between devices: 288 us -> 0.01 us  [per_device(): lax.psum((norm_gain_grads, gain_grads[:2].T, router_grads), ('grp', 'ctx'...]
    ppermute x0 -> x94, starting transfers between devices: none -> 176 us  [the longest x12 47.4 us: line_scatter(): left = lax.ppermute(to_left, axis, [(i, i - 1) for i in range(n - s, n)])]
    all_gather x5 -> x0, waiting for transfers between devices: 164 us -> none  [the longest x1 110 us: per_device(): lax.all_gather(attention_input_weight, ('ctx', 'exp'), axis=0, tiled=True)]
    dot_general x32 -> x27, matrix products: 334 us -> 218 us  [the longest x6 65.4 us: dot_nt(): lax.dot_general(a, b, (((1,), (1,)), ((), ())), preferred_element_type=f32)]
    all_gather x0 -> x2, blocking collectives: none -> 81.1 us  [the longest x1 46.1 us: per_device(): lax.all_gather(jnp.stack(gate_grad_parts, 1), ('ctx', 'exp'), axis=0)]
  transfers between devices with their start and end apart: 14 -> 95, of which waited for: 10 -> 26; matrix products, arithmetic and copies ran while one was open for 15% -> 37% of each run, Pallas kernels for 0% -> 3%
where the time goes in v1:
time: 1510 us; the launch traced here: 1500 us
  waiting for transfers between devices  382 us (25%)
  local copies, waits for them, and re-layouts  268 us (18%)
  other arithmetic  245 us (16%)
  matrix products  221 us (15%)
  starting transfers between devices  176 us (12%)
  blocking collectives  141 us (9%)
  Pallas kernels  44.4 us (3%)
  between operations  17.2 us (1%)
    ppermute x46, waiting for transfers between devices, swap_on(): return lax.ppermute(value, axis, [(i, i ^ mask) for i in range(count)])  132 us
    ppermute x12, waiting for transfers between devices, line_gather(): lax.ppermute(rights[-1], axis, [(i, i + 1) for i in range(s - 1, n - 1)])  111 us
    unnamed x311, local copies, waits for them, and re-layouts  73.6 us
    dot_general x6, matrix products, dot_nt(): lax.dot_general(a, b, (((1,), (1,)), ((), ())), preferred_element_type=f32)  65.4 us
    dot_general x8, matrix products, dot(): return jnp.dot(a, b, preferred_element_type=f32)  62.6 us
    psum x1, blocking collectives, per_device(): lax.psum((norm_gain_grads, gain_grads[:2].T, router_grads), ('grp', 'ctx'...  60.3 us
    convert_element_type x17, other arithmetic, add_low(): return (a.astype(jnp.float32) + b.astype(jnp.float32)).astype(low)  54.4 us
    ppermute x12, waiting for transfers between devices, line_scatter(): left = lax.ppermute(to_left, axis, [(i, i - 1) for i in range(n - s, n)])  52.9 us
  transfers between devices with their start and end apart: 95, of which 26 were waited for; matrix products, arithmetic and copies ran while one was open for 37% of the time, Pallas kernels for 3%

profile of v1, /device:TPU:20, one launch (start us, length us, event | category | flops | bytes accessed | tf_op | source)
XLA Modules:
  0.0 1496.1 jit_solution(2746883649937339776)
XLA Ops:
  37.6 35.0 %all-gather = f32[256,256]{1,0:T(8,128)} all-gather(f32[16,256]{1,0:T(8,128)S(1)} %convolution_select_fusion), channel_id=2, replica_groups=mesh['grp'=2,'ctx'=4,'exp'=4] {'ctx','exp'}, dimensions={0}, use_global_device_ids=true | all-gather | bytes 278528 | tf_op jit(solution)/shard_map/all_gather | solution.py:685
  148.6 17.5 %collective-permute-done.7 = bf16[4,128,1280]{2,1,0:T(8,128)(2,1)} collective-permute-done((bf16[4,128,1280]{2,1,0:T(8,128)(2,1)}, bf16[4,128,1280]{2,1,0:T(8,128)(2,1)}, u32[]{:S(2)}, u32[]{:S(2)}) %collective-permute-start.7) | collective-permute-done | bytes 1310752 | tf_op jit(solution)/shard_map/ppermute | solution.py:555
  235.2 13.9 collective-permute-start.48
  272.7 38.0 %collective-permute-done.47 = bf16[256,2048]{1,0:T(8,128)(2,1)} collective-permute-done((bf16[256,2048]{1,0:T(8,128)(2,1)S(1)}, bf16[256,2048]{1,0:T(8,128)(2,1)}, u32[]{:S(2)}, u32[]{:S(2)}) %collective-permute-start.47) | collective-permute-done | bytes 1048608 | tf_op jit(solution)/shard_map/ppermute | solution.py:554
  329.4 14.4 shard_map.178
  373.7 65.6 %collective-permute-done.22 = bf16[256,2048]{1,0:T(8,128)(2,1)S(1)} collective-permute-done((bf16[256,2048]{1,0:T(8,128)(2,1)S(1)}, bf16[256,2048]{1,0:T(8,128)(2,1)S(1)}, u32[]{:S(2)}, u32[]{:S(2)}) %collective-permute-start.22) | collective-permute-done | bytes 1048608 | tf_op jit(solution)/shard_map/ppermute | solution.py:547
  463.9 18.3 %collective-permute-done.25 = bf16[256,2048]{1,0:T(8,128)(2,1)} collective-permute-done((bf16[256,2048]{1,0:T(8,128)(2,1)}, bf16[256,2048]{1,0:T(8,128)(2,1)}, u32[]{:S(2)}, u32[]{:S(2)}) %collective-permute-start.25) | collective-permute-done | bytes 1048608 | tf_op jit(solution)/shard_map/ppermute | solution.py:555
  486.3 20.1 %pad_maximum_fusion = bf16[2048,2304]{1,0:T(8,128)(2,1)} fusion(bf16[512,2304]{1,0:T(8,128)(2,1)S(1)} %get-tuple-element.116, bf16[512,2304]{1,0:T(8,128)(2,1)S(1)} %get-tuple-element.115, bf16[512,2304]{1,0:T(8,128)(2,1)S(1)} %copy-done.29, bf16[512,2304]{1,0:T(8,128)(2,1)S(1)} %copy-done.27), kind=kLoop, calls=%fused_computation.20 | loop fusion | flops 37748736 | bytes 18874368 | tf_op jit(solution)/shard_map/concatenate | solution.py:712
  522.0 19.4 %collective-permute-done.24 = bf16[256,2048]{1,0:T(8,128)(2,1)S(1)} collective-permute-done((bf16[256,2048]{1,0:T(8,128)(2,1)}, bf16[256,2048]{1,0:T(8,128)(2,1)S(1)}, u32[]{:S(2)}, u32[]{:S(2)}) %collective-permute-start.24) | collective-permute-done | bytes 1048608 | tf_op jit(solution)/shard_map/ppermute | solution.py:554
  555.5 16.2 %collective-permute-done.29 = bf16[256,2048]{1,0:T(8,128)(2,1)S(1)} collective-permute-done((bf16[256,2048]{1,0:T(8,128)(2,1)S(1)}, bf16[256,2048]{1,0:T(8,128)(2,1)S(1)}, u32[]{:S(2)}, u32[]{:S(2)}) %collective-permute-start.29) | collective-permute-done | bytes 1048608 | tf_op jit(solution)/shard_map/ppermute | solution.py:554
  586.6 20.9 %collective-permute-done.31 = bf16[256,2048]{1,0:T(8,128)(2,1)S(1)} collective-permute-done((bf16[256,2048]{1,0:T(8,128)(2,1)S(1)}, bf16[256,2048]{1,0:T(8,128)(2,1)S(1)}, u32[]{:S(2)}, u32[]{:S(2)}) %collective-permute-start.31) | collective-permute-done | bytes 1048608 | tf_op jit(solution)/shard_map/ppermute | solution.py:554
  609.2 20.0 %pad_maximum_fusion.1 = bf16[2048,2304]{1,0:T(8,128)(2,1)} fusion(bf16[512,2304]{1,0:T(8,128)(2,1)S(1)} %get-tuple-element.120, bf16[512,2304]{1,0:T(8,128)(2,1)S(1)} %get-tuple-element.119, bf16[512,2304]{1,0:T(8,128)(2,1)S(1)} %copy-done.33, bf16[512,2304]{1,0:T(8,128)(2,1)S(1)} %copy-done.32), kind=kLoop, calls=%fused_computation.21 | loop fusion | flops 37748736 | bytes 18874368 | tf_op jit(solution)/shard_map/concatenate | solution.py:712
  702.4 13.1 convolution_convert_fusion.3
  846.4 46.1 %all-gather.1 = f32[128,2,256]{2,0,1:T(8,128)S(1)} all-gather(f32[8,2,256]{2,0,1:T(8,128)S(1)} %pad_maximum_fusion.24), channel_id=3, replica_groups=mesh['grp'=2,'ctx'=4,'exp'=4] {'ctx','exp'}, dimensions={0}, use_global_device_ids=true | all-gather | bytes 278528 | tf_op jit(solution)/shard_map/all_gather | solution.py:794
  910.0 13.1 collective-permute-done.58
  956.8 17.7 %collective-permute-start.44 = (bf16[256,2048]{1,0:T(8,128)(2,1)}, bf16[256,2048]{1,0:T(8,128)(2,1)}, u32[]{:S(2)}, u32[]{:S(2)}) collective-permute-start(bf16[256,2048]{1,0:T(8,128)(2,1)} %get-tuple-element.134), channel_id=1, source_target_pairs={{2,1},{3,2},{6,5},{7,6},{10,9},{11,10},{14,13},{15,14},{18,17},{19... | collective-permute-start | bytes 3145736 | tf_op jit(solution)/shard_map/ppermute | solution.py:566
  1010.6 43.4 %collective-permute-done.64 = bf16[256,2048]{1,0:T(8,128)(2,1)} collective-permute-done((bf16[256,2048]{1,0:T(8,128)(2,1)}, bf16[256,2048]{1,0:T(8,128)(2,1)}, u32[]{:S(2)}, u32[]{:S(2)}) %collective-permute-start.64) | collective-permute-done | bytes 1048608 | tf_op jit(solution)/shard_map/ppermute | solution.py:547
  1092.2 29.9 %shard_map.179 = (bf16[1024,1280]{1,0:T(8,128)(2,1)}, f32[8,128]{1,0:T(8,128)S(1)}) custom-call(f32[1024,1280]{1,0:T(8,128)} %fusion.118.q_ref.k_ref.v_ref, f32[1024,1280]{1,0:T(8,128)} %fusion.118.q_ref.k_ref.v_ref, f32[1024,1280]{1,0:T(8,128)} %fusion.118.q_ref.k_ref.v_ref, f32[1024,128]{1,0:T(8,128)S(1)} %get-tuple-element.221.cos_ref, ...), custom_call_target="tpu_custom_call" | custom-call | tf_op jit(solution)/shard_map/pallas_call | solution.py:513
  1153.1 12.4 constant_dynamic-slice_fusion.8
  1213.6 21.7 %collective-permute-done.69 = bf16[512,1280]{1,0:T(8,128)(2,1)} collective-permute-done((bf16[512,1280]{1,0:T(8,128)(2,1)}, bf16[512,1280]{1,0:T(8,128)(2,1)}, u32[]{:S(2)}, u32[]{:S(2)}) %collective-permute-start.69) | collective-permute-done | bytes 1310752 | tf_op jit(solution)/shard_map/ppermute | solution.py:565
  1257.0 15.7 %collective-permute-done.71 = bf16[512,1280]{1,0:T(8,128)(2,1)} collective-permute-done((bf16[512,1280]{1,0:T(8,128)(2,1)}, bf16[512,1280]{1,0:T(8,128)(2,1)}, u32[]{:S(2)}, u32[]{:S(2)}) %collective-permute-start.71) | collective-permute-done | bytes 1310752 | tf_op jit(solution)/shard_map/ppermute | solution.py:566
  1283.9 60.3 %all-reduce.1 = (f32[2048,2]{0,1:T(2,128)}, f32[128,2]{0,1:T(2,128)}) all-reduce(f32[2048,2]{0,1:T(2,128)S(1)} %pad_maximum_fusion.25, f32[128,2]{0,1:T(2,128)S(1)} %slice_bitcast_fusion.16), channel_id=1, replica_groups=mesh['grp'=2,'ctx'=4,'exp'=4] {'grp','ctx','exp'}, use_global_device_ids=true, to_apply=%region_20.21 | all-reduce | flops 4352 | bytes 34816 | tf_op jit(solution)/shard_map/psum | solution.py:871
  1365.6 16.5 %collective-permute-done.83 = bf16[512,1024]{1,0:T(8,128)(2,1)S(1)} collective-permute-done((bf16[512,1024]{1,0:T(8,128)(2,1)S(1)}, bf16[512,1024]{1,0:T(8,128)(2,1)S(1)}, u32[]{:S(2)}, u32[]{:S(2)}) %collective-permute-start.83) | collective-permute-done | bytes 1048608 | tf_op jit(solution)/shard_map/ppermute | solution.py:566
  1446.6 15.3 %reshape.546 = f32[512,4,2,768]{3,2,0,1:T(2,128)} reshape(f32[512,4,1536]{2,0,1:T(8,128)} %slice.350) | data formatting | bytes 25165824 | tf_op jit(solution)/shard_map/reshape | solution.py:844
  (719 shorter events, 874.3 us)
Async XLA Ops:
  7.2 1480.1 %all-reduce.4.cloned.1.call-start = ((), (), s32[]{:S(2)}) async-start(), calls=%async_computation | async-start | bytes 262144 | tf_op jit(solution)/shard_map/psum | solution.py:871
  15.3 130.5 %collective-permute-start = (bf16[256,2048]{0,1:T(8,128)(2,1)}, bf16[256,2048]{0,1:T(8,128)(2,1)}, u32[]{:S(2)}, u32[]{:S(2)}) collective-permute-start(bf16[256,2048]{0,1:T(8,128)(2,1)} %bitcast.4), channel_id=1, source_target_pairs={{0,4},{4,0},{8,12},{12,8},{1,5},{5,1},{9,13},{13,9},{2,6},{6,2},{1... | collective-permute-start | bytes 3145736 | tf_op jit(solution)/shard_map/ppermute | solution.py:547
  15.3 165.1 %collective-permute-start.1 = (bf16[256,2048]{0,1:T(8,128)(2,1)}, bf16[256,2048]{0,1:T(8,128)(2,1)}, u32[]{:S(2)}, u32[]{:S(2)}) collective-permute-start(bf16[256,2048]{0,1:T(8,128)(2,1)} %bitcast.4), channel_id=1, source_target_pairs={{0,8},{4,12},{8,0},{12,4},{1,9},{5,13},{9,1},{13,5},{2,10},{6,14},... | collective-permute-start | bytes 3145736 | tf_op jit(solution)/shard_map/ppermute | solution.py:547
  16.8 86.7 %collective-permute-start.12 = (bf16[128,1024]{1,0:T(8,128)(2,1)}, bf16[128,1024]{1,0:T(8,128)(2,1)}, u32[]{:S(2)}, u32[]{:S(2)}) collective-permute-start(bf16[128,1024]{1,0:T(8,128)(2,1)} %get-tuple-element.181), channel_id=1, source_target_pairs={{0,4},{4,0},{8,12},{12,8},{1,5},{5,1},{9,13},{13,9},{2,6},{6,2},{1... | collective-permute-start | bytes 786440 | tf_op jit(solution)/shard_map/ppermute | solution.py:547
  17.0 88.3 %collective-permute-start.13 = (bf16[128,1024]{1,0:T(8,128)(2,1)}, bf16[128,1024]{1,0:T(8,128)(2,1)}, u32[]{:S(2)}, u32[]{:S(2)}) collective-permute-start(bf16[128,1024]{1,0:T(8,128)(2,1)} %get-tuple-element.182), channel_id=1, source_target_pairs={{0,8},{4,12},{8,0},{12,4},{1,9},{5,13},{9,1},{13,5},{2,10},{6,14},... | collective-permute-start | bytes 786440 | tf_op jit(solution)/shard_map/ppermute | solution.py:547
  18.5 89.3 %collective-permute-start.14 = (bf16[128,1024]{1,0:T(8,128)(2,1)}, bf16[128,1024]{1,0:T(8,128)(2,1)}, u32[]{:S(2)}, u32[]{:S(2)}) collective-permute-start(bf16[128,1024]{1,0:T(8,128)(2,1)} %get-tuple-element.180), channel_id=1, source_target_pairs={{0,12},{4,8},{8,4},{12,0},{1,13},{5,9},{9,5},{13,1},{2,14},{6,10},... | collective-permute-start | bytes 786440 | tf_op jit(solution)/shard_map/ppermute | solution.py:547
  218.6 136.7 %collective-permute-start.33 = (bf16[512,2304]{1,0:T(8,128)(2,1)}, bf16[512,2304]{1,0:T(8,128)(2,1)}, u32[]{:S(2)}, u32[]{:S(2)}) collective-permute-start(bf16[512,2304]{1,0:T(8,128)(2,1)} %pad_maximum_fusion.14), channel_id=1, source_target_pairs={{0,4},{4,0},{8,12},{12,8},{1,5},{5,1},{9,13},{13,9},{2,6},{6,2},{1... | collective-permute-start | bytes 7077896 | tf_op jit(solution)/shard_map/ppermute | solution.py:547
  223.2 139.8 %collective-permute-start.35 = (bf16[512,2304]{1,0:T(8,128)(2,1)}, bf16[512,2304]{1,0:T(8,128)(2,1)}, u32[]{:S(2)}, u32[]{:S(2)}) collective-permute-start(bf16[512,2304]{1,0:T(8,128)(2,1)} %pad_maximum_fusion.14), channel_id=1, source_target_pairs={{0,12},{4,8},{8,4},{12,0},{1,13},{5,9},{9,5},{13,1},{2,14},{6,10},... | collective-permute-start | bytes 7077896 | tf_op jit(solution)/shard_map/ppermute | solution.py:547
  272.7 79.3 %collective-permute-start.46 = (bf16[256,2048]{1,0:T(8,128)(2,1)S(1)}, bf16[256,2048]{1,0:T(8,128)(2,1)S(1)}, u32[]{:S(2)}, u32[]{:S(2)}) collective-permute-start(bf16[256,2048]{1,0:T(8,128)(2,1)S(1)} %copy-done.74), channel_id=1, source_target_pairs={{0,4},{4,0},{8,12},{12,8},{1,5},{5,1},{9,13},{13,9},{2,6},{6,2},{1... | collective-permute-start | bytes 3145736 | tf_op jit(solution)/shard_map/ppermute | solution.py:547
  355.3 152.2 %collective-permute-start.54 = (bf16[256,2048]{1,0:T(8,128)(2,1)}, bf16[256,2048]{1,0:T(8,128)(2,1)}, u32[]{:S(2)}, u32[]{:S(2)}) collective-permute-start(bf16[256,2048]{1,0:T(8,128)(2,1)} %collective-permute-done.52), channel_id=1, source_target_pairs={{2,3},{6,7},{10,11},{14,15},{18,19},{22,23},{26,27},{30,31}} | collective-permute-start | bytes 3145736 | tf_op jit(solution)/shard_map/ppermute | solution.py:554
  363.0 98.1 %collective-permute-start.34 = (bf16[512,2304]{1,0:T(8,128)(2,1)}, bf16[512,2304]{1,0:T(8,128)(2,1)}, u32[]{:S(2)}, u32[]{:S(2)}) collective-permute-start(bf16[512,2304]{1,0:T(8,128)(2,1)} %get-tuple-element.147), channel_id=1, source_target_pairs={{0,8},{4,12},{8,0},{12,4},{1,9},{5,13},{9,1},{13,5},{2,10},{6,14},... | collective-permute-start | bytes 7077896 | tf_op jit(solution)/shard_map/ppermute | solution.py:547
  363.8 220.7 %collective-permute-start.38 = (bf16[512,2304]{1,0:T(8,128)(2,1)}, bf16[512,2304]{1,0:T(8,128)(2,1)}, u32[]{:S(2)}, u32[]{:S(2)}) collective-permute-start(bf16[512,2304]{1,0:T(8,128)(2,1)} %collective-permute-done.35), channel_id=1, source_target_pairs={{0,16},{16,0},{1,17},{17,1},{2,18},{18,2},{3,19},{19,3},{4,20},{20... | collective-permute-start | bytes 7077896 | tf_op jit(solution)/shard_map/ppermute | solution.py:547
  368.3 71.0 %collective-permute-start.22 = (bf16[256,2048]{1,0:T(8,128)(2,1)S(1)}, bf16[256,2048]{1,0:T(8,128)(2,1)S(1)}, u32[]{:S(2)}, u32[]{:S(2)}) collective-permute-start(bf16[256,2048]{1,0:T(8,128)(2,1)S(1)} %fusion.60), channel_id=1, source_target_pairs={{0,8},{4,12},{8,0},{12,4},{1,9},{5,13},{9,1},{13,5},{2,10},{6,14},... | collective-permute-start | bytes 3145736 | tf_op jit(solution)/shard_map/ppermute | solution.py:547
  802.6 101.0 %collective-permute-start.39 = (bf16[4,256,2048]{2,1,0:T(8,128)(2,1)}, bf16[4,256,2048]{2,1,0:T(8,128)(2,1)}, u32[]{:S(2)}, u32[]{:S(2)}) collective-permute-start(bf16[4,256,2048]{2,1,0:T(8,128)(2,1)} %slice_bitcast_fusion.2), channel_id=1, source_target_pairs={{0,4},{4,0},{8,12},{12,8},{1,5},{5,1},{9,13},{13,9},{2,6},{6,2},{1... | collective-permute-start | bytes 12582920 | tf_op jit(solution)/shard_map/ppermute | solution.py:547
  825.5 105.9 %collective-permute-start.89 = (bf16[1024,2304]{0,1:T(8,128)(2,1)}, bf16[1024,2304]{0,1:T(8,128)(2,1)}, u32[]{:S(2)}, u32[]{:S(2)}) collective-permute-start(bf16[1024,2304]{0,1:T(8,128)(2,1)} %pad_maximum_fusion.2), channel_id=1, source_target_pairs={{0,8},{4,12},{8,0},{12,4},{1,9},{5,13},{9,1},{13,5},{2,10},{6,14},... | collective-permute-start | bytes 14155784 | tf_op jit(solution)/shard_map/ppermute | solution.py:547
  845.4 213.2 %collective-permute-start.88 = (bf16[1024,2304]{0,1:T(8,128)(2,1)}, bf16[1024,2304]{0,1:T(8,128)(2,1)}, u32[]{:S(2)}, u32[]{:S(2)}) collective-permute-start(bf16[1024,2304]{0,1:T(8,128)(2,1)} %pad_maximum_fusion.3), channel_id=1, source_target_pairs={{0,8},{4,12},{8,0},{12,4},{1,9},{5,13},{9,1},{13,5},{2,10},{6,14},... | collective-permute-start | bytes 14155784 | tf_op jit(solution)/shard_map/ppermute | solution.py:547
  939.8 118.8 %collective-permute-start.90 = (bf16[1024,2304]{0,1:T(8,128)(2,1)}, bf16[1024,2304]{0,1:T(8,128)(2,1)}, u32[]{:S(2)}, u32[]{:S(2)}) collective-permute-start(bf16[1024,2304]{0,1:T(8,128)(2,1)} %add_convert_fusion.1), channel_id=1, source_target_pairs={{0,16},{16,0},{1,17},{17,1},{2,18},{18,2},{3,19},{19,3},{4,20},{20... | collective-permute-start | bytes 14155784 | tf_op jit(solution)/shard_map/ppermute | solution.py:547
  998.4 185.4 %collective-permute-start.42 = (bf16[256,2048]{1,0:T(8,128)(2,1)}, bf16[256,2048]{1,0:T(8,128)(2,1)}, u32[]{:S(2)}, u32[]{:S(2)}) collective-permute-start(bf16[256,2048]{1,0:T(8,128)(2,1)} %get-tuple-element.131), channel_id=1, source_target_pairs={{0,1},{1,2},{2,3},{4,5},{5,6},{6,7},{8,9},{9,10},{10,11},{12,13},{... | collective-permute-start | bytes 3145736 | tf_op jit(solution)/shard_map/ppermute | solution.py:565
  1006.1 178.9 %collective-permute-start.45 = (bf16[256,2048]{1,0:T(8,128)(2,1)}, bf16[256,2048]{1,0:T(8,128)(2,1)}, u32[]{:S(2)}, u32[]{:S(2)}) collective-permute-start(bf16[256,2048]{1,0:T(8,128)(2,1)} %get-tuple-element.132), channel_id=1, source_target_pairs={{1,0},{2,1},{3,2},{5,4},{6,5},{7,6},{9,8},{10,9},{11,10},{13,12},{... | collective-permute-start | bytes 3145736 | tf_op jit(solution)/shard_map/ppermute | solution.py:566
  1201.3 157.8 %collective-permute-start.91 = (bf16[512,2304]{1,0:T(8,128)(2,1)}, bf16[512,2304]{1,0:T(8,128)(2,1)}, u32[]{:S(2)}, u32[]{:S(2)}) collective-permute-start(bf16[512,2304]{1,0:T(8,128)(2,1)} %bitcast.501), channel_id=1, source_target_pairs={{0,16},{16,0},{1,17},{17,1},{2,18},{18,2},{3,19},{19,3},{4,20},{20... | collective-permute-start | bytes 7077896 | tf_op jit(solution)/shard_map/ppermute | solution.py:547
  1241.4 124.2 %collective-permute-start.80 = (bf16[512,1024]{1,0:T(8,128)(2,1)}, bf16[512,1024]{1,0:T(8,128)(2,1)}, u32[]{:S(2)}, u32[]{:S(2)}) collective-permute-start(bf16[512,1024]{1,0:T(8,128)(2,1)} %get-tuple-element.81), channel_id=1, source_target_pairs={{0,1},{1,2},{2,3},{4,5},{5,6},{6,7},{8,9},{9,10},{10,11},{12,13},{... | collective-permute-start | bytes 3145736 | tf_op jit(solution)/shard_map/ppermute | solution.py:565
  1247.2 114.8 %collective-permute-start.93 = (bf16[512,2304]{1,0:T(8,128)(2,1)}, bf16[512,2304]{1,0:T(8,128)(2,1)}, u32[]{:S(2)}, u32[]{:S(2)}) collective-permute-start(bf16[512,2304]{1,0:T(8,128)(2,1)} %collective-permute-done.92), channel_id=1, source_target_pairs={{0,16},{16,0},{1,17},{17,1},{2,18},{18,2},{3,19},{19,3},{4,20},{20... | collective-permute-start | bytes 7077896 | tf_op jit(solution)/shard_map/ppermute | solution.py:547
  1255.1 94.3 %collective-permute-start.82 = (bf16[512,1024]{1,0:T(8,128)(2,1)}, bf16[512,1024]{1,0:T(8,128)(2,1)}, u32[]{:S(2)}, u32[]{:S(2)}) collective-permute-start(bf16[512,1024]{1,0:T(8,128)(2,1)} %fusion.41), channel_id=1, source_target_pairs={{2,1},{3,2},{6,5},{7,6},{10,9},{11,10},{14,13},{15,14},{18,17},{19... | collective-permute-start | bytes 3145736 | tf_op jit(solution)/shard_map/ppermute | solution.py:566
  1275.8 78.3 %collective-permute-start.72 = (bf16[512,1280]{1,0:T(8,128)(2,1)}, bf16[512,1280]{1,0:T(8,128)(2,1)}, u32[]{:S(2)}, u32[]{:S(2)}) collective-permute-start(bf16[512,1280]{1,0:T(8,128)(2,1)} %fusion.33), channel_id=1, source_target_pairs={{2,1},{3,2},{6,5},{7,6},{10,9},{11,10},{14,13},{15,14},{18,17},{19... | collective-permute-start | bytes 3932168 | tf_op jit(solution)/shard_map/ppermute | solution.py:566
  (211 other events, 5503.7 us)
Sparse Core Ops, SparseCore 0:
  994.0 122.6 all-reduce.3

commit v2 on v1

--- a/solution.py
+++ b/solution.py
@@ -539,6 +539,186 @@
     )(qkv, qkv, qkv, cosine, sine, start, gains, attended, upstream, lse)
 
 
+def expert_kernel(blocks, capacity, piece_count, *refs):
+    tok0, tok1, up0, up1, router_ref = refs[:5]
+    weights = refs[5 : 5 + 6 * piece_count]
+    x_out, up_out, gug_out, act_out, sent0, sent1, mix0, mix1 = refs[-18:-10]
+    x_s, up_s, table_s, gate_s, y_acc, sent_acc, gg_acc, gate_tab0, gate_tab1, gg_rows = refs[-10:]
+    tokens, ups = (tok0, tok1), (up0, up1)
+    rows = tok0.shape[0]
+    span = tok0.shape[1] // piece_count
+    half = capacity
+    ctx, grp, exp = lax.axis_index("ctx"), lax.axis_index("grp"), lax.axis_index("exp")
+    core = ctx % 2
+    step_e, step_f = pl.program_id(0), pl.program_id(1)
+    experts = router_ref.shape[0]
+    expert = exp * 4 + 2 * core + jnp.where(step_e == 0, 1 - grp, grp)
+    order = [pl.ds(pl.multiple_of((q ^ core) * span, span), span) for q in range(piece_count)]
+
+    @pl.when((step_e == 0) & (step_f == 0))
+    def _():
+        gg_rows[...] = jnp.zeros_like(gg_rows)
+        for kk, tab in enumerate((gate_tab0, gate_tab1)):
+            logits = dots_nt(router_ref[...], tokens[kk][...])
+            powers = jnp.exp(logits - jnp.max(logits, axis=0, keepdims=True))
+            probs = powers / jnp.sum(powers, axis=0, keepdims=True)
+            slot = ups[kk][rows:, :rows].astype(jnp.float32)
+            chosen = jnp.where(slot >= 0, probs, 0.0)
+            tab[...] = chosen / jnp.sum(chosen, axis=0, keepdims=True)
+
+    @pl.when(step_f == 0)
+    def _():
+        y_acc[...] = jnp.zeros_like(y_acc)
+        sent_acc[...] = jnp.zeros_like(sent_acc)
+        gg_acc[...] = jnp.zeros_like(gg_acc)
+        which = lax.broadcasted_iota(jnp.int32, (experts, rows), 0) == expert
+        for kk, tab in enumerate((gate_tab0, gate_tab1)):
+            slots = ups[kk][rows:, :rows].astype(jnp.float32)
+            slot = jnp.sum(jnp.where(which, slots, 0.0), axis=0, keepdims=True)
+            gate = jnp.sum(jnp.where(which, tab[...], 0.0), axis=0, keepdims=True)
+            table = slot == lax.broadcasted_iota(jnp.int32, (capacity, rows), 0).astype(jnp.float32)
+            table_low = jnp.where(table, 1.0, 0.0).astype(jnp.bfloat16)
+            table_s[kk] = table_low
+            at = slice(kk * half, (kk + 1) * half)
+            gate_s[at, :] = jnp.sum(jnp.where(table, gate, 0.0), axis=1, keepdims=True)
+            for q in range(piece_count):
+                cols = slice(q * span, (q + 1) * span)
+                x_s[at, cols] = dots(table_low, tokens[kk][:, order[q]]).astype(jnp.bfloat16)
+                up_s[at, cols] = dots(table_low, ups[kk][:rows, order[q]]).astype(jnp.bfloat16)
+        x_out[0] = x_s[...]
+        up_out[0] = up_s[...]
+
+    def body(parts):
+        gates, upw, outs = parts[0::3], parts[1::3], parts[2::3]
+        wide = gates[0].shape[1]
+        cut = [slice(q * span, (q + 1) * span) for q in range(piece_count)]
+        a = sum(dots(x_s[:, cut[q]], gates[q][...]) for q in range(piece_count))
+        u = sum(dots(x_s[:, cut[q]], upw[q][...]) for q in range(piece_count))
+        back = sum(dots(up_s[:, cut[q]], outs[q][...]) for q in range(piece_count))
+        s = 1.0 / (1.0 + jnp.exp(-a))
+        silu = a * s
+        act = (silu * u).astype(jnp.bfloat16).astype(jnp.float32)
+        gg_acc[...] += jnp.sum(act * back, axis=1, keepdims=True)
+        gate = gate_s[...]
+        act_low = (act * gate).astype(jnp.bfloat16)
+        back = back * gate
+        gate_grad = (back * u * s * (1.0 + a * (1.0 - s))).astype(jnp.bfloat16)
+        up_grad = (back * silu).astype(jnp.bfloat16)
+        at = pl.multiple_of(step_f * wide, wide)
+        total = gug_out.shape[2] // 2
+        gug_out[0, :, pl.ds(at, wide)] = gate_grad
+        gug_out[0, :, pl.ds(pl.multiple_of(total + at, wide), wide)] = up_grad
+        act_out[0, :, pl.ds(at, wide)] = act_low
+        for q in range(piece_count):
+            y_acc[:, cut[q]] += dots_nt(act_low, outs[q][...])
+            sent_acc[:, cut[q]] += dots_nt(gate_grad, gates[q][...]) + dots_nt(up_grad, upw[q][...])
+
+    @pl.when(step_e == 0)
+    def _():
+        body(weights[: 3 * piece_count])
+
+    @pl.when(step_e == 1)
+    def _():
+        body(weights[3 * piece_count :])
+
+    def finish(first):
+        which = lax.broadcasted_iota(jnp.int32, (experts, rows), 0) == expert
+        for kk, (sent, mix) in enumerate(((sent0, mix0), (sent1, mix1))):
+            table = table_s[kk]
+            at = slice(kk * half, (kk + 1) * half)
+            for q in range(piece_count):
+                cols = slice(q * span, (q + 1) * span)
+                for out, acc, size in ((sent, sent_acc, rows), (mix, y_acc, rows)):
+                    part = lax.dot_general(
+                        table, acc[at, cols].astype(jnp.bfloat16), (((0,), (0,)), ((), ())),
+                        preferred_element_type=jnp.float32,
+                    )
+                    if not first:
+                        part = part + out[:rows, order[q]].astype(jnp.float32)
+                    out[:rows, order[q]] = part.astype(jnp.bfloat16)
+            gg = jnp.sum(jnp.where(table > 0, gg_acc[at, :], 0.0), axis=0, keepdims=True)
+            gg_rows[kk] += jnp.where(which, gg, 0.0)
+            if not first:
+                high = gg_rows[kk].astype(jnp.bfloat16)
+                sent[rows:, :] = jnp.zeros((sent.shape[0] - rows, sent.shape[1]), jnp.bfloat16)
+                sent[rows:, :rows] = high
+                sent[rows:, rows : 2 * rows] = (gg_rows[kk] - high.astype(jnp.float32)).astype(jnp.bfloat16)
+
+    last = pl.num_programs(1) - 1
+
+    @pl.when((step_f == last) & (step_e == 0))
+    def _():
+        finish(True)
+
+    @pl.when((step_f == last) & (step_e == 1))
+    def _():
+        finish(False)
+
+
+def run_experts(block, blocks, tok, ups, router_t, pieces, capacity, held):
+    rows, width = tok[0].shape
+    count = len(pieces[0])
+    quarter, wide3 = pieces[0][0].shape
+    units = wide3 // 3
+    tile = min(256, units)
+    steps = units // tile
+    cap2 = 2 * capacity
+    low = jnp.bfloat16
+    once = pl.Buffered(1)
+    whole = lambda a: pl.BlockSpec(a.shape, lambda e, f: (0, 0), pipeline_mode=once)
+    in_specs = [whole(a) for a in (*tok, *ups, router_t)]
+    operands = [*tok, *ups, router_t]
+    for j in range(2):
+        for piece in pieces[j]:
+            for part in range(3):
+                def at(e, f, j=j, part=part):
+                    return (0, part * steps + (jnp.where(e == 0, f, steps - 1) if j == 0 else jnp.where(e == 1, f, 0)))
+                in_specs.append(pl.BlockSpec((quarter, tile), at))
+                operands.append(piece)
+    aliases = {}
+    if held is not None:
+        for i, a in enumerate(held):
+            aliases[len(operands)] = i
+            operands.append(a)
+            in_specs.append(pl.BlockSpec(memory_space=pl.ANY))
+    store = lambda cols: pl.BlockSpec((1, cap2, cols), lambda e, f: (e, block, 0))
+    whole_out = lambda r: pl.BlockSpec((r, width), lambda e, f: (0, 0), pipeline_mode=once)
+    ext = ups[0].shape[0]
+    struct = jax.ShapeDtypeStruct
+    experts = router_t.shape[0]
+
+    def kernel(*refs):
+        n_in = 5 + 6 * count
+        held_n = 4 if held is not None else 0
+        expert_kernel(blocks, capacity, count, *refs[:n_in], *refs[n_in + held_n :])
+
+    return pl.pallas_call(
+        kernel,
+        grid=(2, steps),
+        in_specs=in_specs,
+        out_specs=[
+            store(width), store(width), store(2 * units), store(units),
+            whole_out(ext), whole_out(ext), whole_out(rows), whole_out(rows),
+        ],
+        out_shape=[
+            struct((2, blocks * cap2, width), low), struct((2, blocks * cap2, width), low),
+            struct((2, blocks * cap2, 2 * units), low), struct((2, blocks * cap2, units), low),
+            struct((ext, width), low), struct((ext, width), low),
+            struct((rows, width), low), struct((rows, width), low),
+        ],
+        scratch_shapes=[
+            pltpu.VMEM((cap2, width), low), pltpu.VMEM((cap2, width), low),
+            pltpu.VMEM((2, capacity, rows), low), pltpu.VMEM((cap2, 1), jnp.float32),
+            pltpu.VMEM((cap2, width), jnp.float32), pltpu.VMEM((cap2, width), jnp.float32),
+            pltpu.VMEM((cap2, 1), jnp.float32),
+            pltpu.VMEM((experts, rows), jnp.float32), pltpu.VMEM((experts, rows), jnp.float32),
+            pltpu.VMEM((2, experts, rows), jnp.float32),
+        ],
+        input_output_aliases=aliases,
+        compiler_params=pltpu.CompilerParams(vmem_limit_bytes=60 * 2**20),
+    )(*operands)
+
+
 low = jnp.bfloat16
 
 
@@ -547,24 +727,33 @@
     return lax.ppermute(value, axis, [(i, i ^ mask) for i in range(count)])
 
 
-def line_gather(block, axis):
+def after(value, *others):
+    return lax.optimization_barrier((value, *others))[0]
+
+
+def line_chain(block, axis, then=None):
     n = lax.axis_size(axis)
     rights, lefts = [block], [block]
     for s in range(1, n):
+        if s == 2 and then is not None:
+            rights[1], lefts[1] = after(rights[1], then), after(lefts[1], then)
         rights.append(lax.ppermute(rights[-1], axis, [(i, i + 1) for i in range(s - 1, n - 1)]))
         lefts.append(lax.ppermute(lefts[-1], axis, [(i, i - 1) for i in range(1, n - s + 1)]))
-    return [block] + [rights[s] + lefts[n - s] for s in range(1, n)]
-
-
-def line_scatter(parts, axis):
+    return rights, lefts
+
+
+def shift_back(value, axis, s):
     n = lax.axis_size(axis)
-    right = left = None
-    for s in range(1, n):
-        to_right = parts[n - s] if right is None else add_low(parts[n - s], right)
-        to_left = parts[s] if left is None else add_low(parts[s], left)
-        right = lax.ppermute(to_right, axis, [(i, i + 1) for i in range(s)])
-        left = lax.ppermute(to_left, axis, [(i, i - 1) for i in range(n - s, n)])
-    return parts[0].astype(jnp.float32) + right.astype(jnp.float32) + left.astype(jnp.float32)
+    return lax.ppermute(value, axis, [(i, (i - s) % n) for i in range(n)])
+
+
+def sum_all(value):
+    for axis in ("grp", "ctx", "exp"):
+        mask = 1
+        while mask < lax.axis_size(axis):
+            value = value + swap_on(value, axis, mask)
+            mask *= 2
+    return value
 
 
 def add_low(a, b):
@@ -664,27 +853,47 @@
     def weight_out_of(at):
         return lax.dynamic_slice_in_dim(attn_out_weight, at * heads * head_dim, heads * head_dim, 1)
 
-    def all_rows(piece_of):
-        blocks = [piece_of(ctx)] + [swap_on(piece_of(ctx ^ m), "ctx", m) for m in range(1, n_ctx)]
-        block = place_ctx(blocks)
-        blocks = line_gather(block, "exp")
-        out = jnp.zeros((n_exp,) + block.shape, block.dtype)
-        for s in range(n_exp):
-            out = lax.dynamic_update_index_in_dim(out, blocks[s], (exp - s) % n_exp, 0)
-        return out.reshape(width, block.shape[-1])
+    def to_ctx(piece_of, then=None):
+        pieces = [piece_of(ctx ^ m) for m in range(n_ctx)]
+        if then is not None:
+            pieces = [after(p, then) for p in pieces]
+        return place_ctx([pieces[0]] + [swap_on(pieces[m], "ctx", m) for m in range(1, n_ctx)])
+
+    def all_rows(block, then=None):
+        halves = block.reshape((2, n_ctx // 2) + block.shape[1:])
+        half_block = pick(halves, grp)
+        if then is not None:
+            half_block = after(half_block, then)
+        rights, lefts = line_chain(half_block, "exp")
+        cross = lambda value, held: lax.ppermute(
+            value, ("grp", "exp"), [(g * n_exp + i, (1 - g) * n_exp + i) for g in range(2) for i in held]
+        )
+        rights_x, lefts_x = [None], [None]
+        for s in range(1, n_exp):
+            rights_x.append(cross(rights[s], range(s, n_exp)))
+            lefts_x.append(cross(lefts[s], range(n_exp - s)))
+        out = jnp.zeros((n_exp,) + halves.shape, block.dtype)
+        out = lax.dynamic_update_index_in_dim(out, halves, exp, 0)
+        for s in range(1, n_exp):
+            for which, r, l in ((grp, rights, lefts), (1 - grp, rights_x, lefts_x)):
+                got = (r[s] + l[n_exp - s])[None, None]
+                out = lax.dynamic_update_slice(out, got, ((exp - s) % n_exp, which, 0, 0, 0))
+        return out.reshape(width, block.shape[-1]), rights[n_exp - 1]
 
     normed, hidden_unit, hidden_scale = norm_forward(hidden, gain_attn)
     normed_seq = gather_ctx(by_exp(normed.astype(low))).reshape(length, width)
-    weight_in = all_rows(weight_in_of)
-    weight_out = all_rows(weight_out_of)
-
     capacity = 5 * rows * top // (4 * expert_count)
     hits = jnp.any(routes[0][:, :, None] == jnp.arange(expert_count, dtype=jnp.int32), axis=1)
     before = jnp.tril(jnp.ones((rows, rows), low), -1)
-    slots = jnp.where(hits, dot(before, hits.astype(low)), -1.0).T
-    slots_all = lax.all_gather(slots, ("ctx", "exp"), axis=0).reshape(n_ctx, n_exp, expert_count, rows)
-    order = [(s, j) for s in range(n_exp) for j in range(2)]
-    slots_of = jnp.stack([pick(pick(slots_all, ctx ^ j), (exp - s) % n_exp) for s, j in order])
+    slots = jnp.where(hits, dot(before, hits.astype(low)), -1.0).T.astype(low)
+    upstream_block = jnp.concatenate(
+        [own_half_first(out_grad[0]), jnp.pad(slots, ((0, 0), (0, width - rows)))]
+    )
+    block_in = to_ctx(weight_in_of)
+    block_out = to_ctx(weight_out_of, block_in)
+    weight_in, in_done = all_rows(block_in)
+    weight_out, out_done = all_rows(block_out, in_done)
+    up_rights, up_lefts = line_chain(upstream_block, "exp", out_done)
 
     local_experts = expert_in.shape[1]
     hidden_units = expert_out.shape[2]
@@ -701,27 +910,14 @@
 
     here = [2 * core + (1 - grp), 2 * core + grp]
     there = [2 * (1 - core) + (1 - grp), 2 * (1 - core) + grp]
-    over_same = swap_on(expert_rows(here[0]), "ctx", 2)
-    over_other = swap_on(expert_rows(there[0]), "ctx", 3)
+    over_same = swap_on(after(expert_rows(here[0]), block_out), "ctx", 2)
+    over_other = swap_on(after(expert_rows(there[0]), block_out), "ctx", 3)
     expert_weights = []
     for j in range(2):
         same, other = expert_rows(here[j]), swap_on(expert_rows(there[j]), "ctx", 1)
         if j == 1:
             over_same, over_other = swap_on(over_same, "grp", 1), swap_on(over_other, "grp", 1)
-        expert_weights.append(
-            jnp.concatenate(
-                [
-                    jnp.where(core == 0, same, other),
-                    jnp.where(core == 0, other, same),
-                    jnp.where(core == 0, over_same, over_other),
-                    jnp.where(core == 0, over_other, over_same),
-                ]
-            )
-        )
-
-    def gather_tokens(block):
-        blocks = line_gather(block, "exp")
-        return jnp.stack([b for own in blocks for b in (own, swap_on(own, "ctx", 1))])
+        expert_weights.append([same, other, over_same, over_other])
 
     qkv = dot(normed_seq, weight_in)
     attended, log_mass = attend(qkv, cosine, sine, doc_start, gains, heads)
@@ -730,79 +926,40 @@
     ffn_normed, middle_unit, middle_scale = norm_forward(middle, gain_ffn)
     ffn_low = ffn_normed.astype(low)
 
-    tokens = gather_tokens(own_half_first(ffn_low))
-    upstreams = gather_tokens(own_half_first(out_grad[0]))
-    router_here = jnp.where(
-        half == 0, router_weight, jnp.concatenate([router_weight[width // 2 :], router_weight[: width // 2]])
-    )
-    logits = dot(tokens.reshape(-1, width), router_here)
-    probs_all = jax.nn.softmax(logits, axis=-1).reshape(len(order), rows, expert_count)
-    selected = jnp.where(slots_of.transpose(0, 2, 1) >= 0, probs_all, 0.0)
-    sel_sums = jnp.sum(selected, axis=-1, keepdims=True)
-    gates_all = selected / sel_sums
-    probs, sel_total = probs_all[0], sel_sums[0]
-    gates = gates_all[0]
-
-    mixed, sent, tables, gate_grad_parts, grad_halves = [], [], [], [], []
+    logits = dot(ffn_low, router_weight)
+    probs = jax.nn.softmax(logits, axis=-1)
+    selected = jnp.where(hits, probs, 0.0)
+    sel_total = jnp.sum(selected, axis=-1, keepdims=True)
+    gates = selected / sel_total
+
+    tok_rights, tok_lefts = line_chain(own_half_first(ffn_low), "exp")
+    router_here = own_half_first(router_weight.T)
+    held, backs, mixes = None, [], []
+    for s in range(n_exp):
+        if s == 0:
+            tok, ups = tok_rights[0], up_rights[0]
+        else:
+            tok, ups = tok_rights[s] + tok_lefts[n_exp - s], up_rights[s] + up_lefts[n_exp - s]
+        tok, ups = (tok, swap_on(tok, "ctx", 1)), (ups, swap_on(ups, "ctx", 1))
+        *held, back0, back1, mix0, mix1 = run_experts(
+            s, n_exp, tok, ups, router_here, expert_weights, capacity, held
+        )
+        back = add_low(back0, swap_on(back1, "ctx", 1))
+        backs.append(back if s == 0 else shift_back(back, "exp", s))
+        mixes.append((mix0, mix1))
+    back_total = sum(b.astype(f32) for b in backs)
+    sent_grads = own_half_first(back_total[:rows])
+    gate_grads = (back_total[rows:, :rows] + back_total[rows:, rows : 2 * rows]).T
+
+    inputs_all, ups_all, gate_up_all, act_all = held
+    grad_halves = []
     for j in range(2):
-        expert = exp * local_experts + here[j]
-        slot = lax.dynamic_index_in_dim(slots_of, expert, 1, keepdims=False)
-        table = slot[:, None, :] == jnp.arange(capacity, dtype=f32)[None, :, None]
-        gate_rows = lax.dynamic_index_in_dim(gates_all, expert, 2, keepdims=False)
-        gate_slots = jnp.sum(jnp.where(table, gate_rows[:, None, :], 0.0), axis=-1)
-        table_low = table.astype(low)
-        gather = lambda a: jnp.einsum(
-            "bct,btd->bcd", table_low, a, preferred_element_type=f32
-        ).reshape(-1, width)
-        inputs = gather(tokens).astype(low)
-        ups = gather(upstreams)
-        grads = (ups * gate_slots.reshape(-1, 1)).astype(low)
-        weight = expert_weights[j]
-        into, outof = weight[:, : 2 * hidden_units], weight[:, 2 * hidden_units :]
-        gate_up = dot(inputs, into)
-        gate_part, up_part = gate_up[:, :hidden_units], gate_up[:, hidden_units:]
-        sigmoid_part = jax.nn.sigmoid(gate_part)
-        silu_part = gate_part * sigmoid_part
-        act = (silu_part * up_part).astype(low)
-        made = dot_nt(act, outof).astype(low)
-        act_grad = dot(grads, outof)
-        gate_grad = act_grad * up_part * sigmoid_part * (1.0 + gate_part * (1.0 - sigmoid_part))
-        gate_up_grad = jnp.concatenate([gate_grad, act_grad * silu_part], 1).astype(low)
-        sent.append(dot_nt(gate_up_grad, into).astype(low).reshape(len(order), capacity, width))
-        gate_grad_slots = jnp.sum(ups * made.astype(f32), axis=-1).reshape(len(order), capacity)
-        gate_grad_parts.append(jnp.sum(jnp.where(table, gate_grad_slots[:, :, None], 0.0), axis=1))
-        mixed.append(
-            (made.astype(f32) * gate_slots.reshape(-1, 1)).astype(low).reshape(len(order), capacity, width)
-        )
-        tables.append(table_low)
-        grad = jnp.concatenate([dot_tn(inputs, gate_up_grad), dot_tn(grads, act)], 1).astype(low)
+        grad = jnp.concatenate(
+            [dot_tn(inputs_all[j], gate_up_all[j]), dot_tn(ups_all[j], act_all[j])], 1
+        ).astype(low)
         grad_halves.append(
             grad[: width // 2].astype(f32) + swap_on(grad[width // 2 :], "ctx", 2).astype(f32)
         )
-
-    both = jnp.concatenate(tables, 1)
-
-    def back_to_tokens(parts):
-        summed = jnp.einsum(
-            "bct,bcd->btd", both, jnp.concatenate(parts, 1), preferred_element_type=f32
-        ).astype(low)
-        summed = summed.reshape(n_exp, 2, rows, width)
-        mine = add_low(summed[:, 0], swap_on(summed[:, 1], "ctx", 1))
-        return own_half_first(line_scatter([mine[(-o) % n_exp] for o in range(n_exp)], "exp"))
-
-    sent_grads = back_to_tokens(sent)
-    gate_parts = lax.all_gather(jnp.stack(gate_grad_parts, 1), ("ctx", "exp"), axis=0).reshape(
-        n_ctx, n_exp, len(order), 2, rows
-    )
-    expert_ids = jnp.arange(expert_count, dtype=jnp.int32)
-    gate_grads = jnp.zeros((rows, expert_count), f32)
-    for at, (s, j) in enumerate(order):
-        owner = (exp + s) % n_exp
-        piece = pick(pick(gate_parts, ctx ^ j), owner)[at]
-        there_core = core ^ j
-        for i, first in enumerate((1 - grp, grp)):
-            expert = owner * local_experts + 2 * there_core + first
-            gate_grads = gate_grads + jnp.where(expert_ids[None, :] == expert, piece[i][:, None], 0.0)
 
     weighted = jnp.sum(gate_grads * gates, axis=1, keepdims=True)
     prob_grads = jnp.where(hits, (gate_grads - weighted) / sel_total, 0.0)
@@ -824,12 +981,15 @@
     input_part = norm_backward(normed_grads, hidden_unit, hidden_scale, gain_attn)
     input_grad = (middle_grad + input_part).astype(low)[None]
 
-    mixture = back_to_tokens(mixed)
+    mixture = 0.0
+    for s, (own, other) in enumerate(mixes):
+        mix = add_low(own, swap_on(after(other, back_total), "ctx", 1))
+        mixture = mixture + (mix if s == 0 else shift_back(mix, "exp", s)).astype(f32)
+    mixture = own_half_first(mixture)
     output = (middle + mixture).astype(low)[None]
 
     kept = add_low(grad_halves[1], swap_on(grad_halves[0].astype(low), "grp", 1)).reshape(2, quarter, -1)
-    mine = pick(kept, core)
-    sibling = swap_on(pick(kept, 1 - core), "ctx", 1)
+    mine, sibling = kept[0], swap_on(kept[1], "ctx", 1)
     mine_x, sibling_x = swap_on(mine, "grp", 1), swap_on(sibling, "grp", 1)
     totals = []
     for at in range(local_experts):
@@ -846,7 +1006,9 @@
 
     def to_rows(part):
         blocks = part.reshape(n_exp, n_ctx * shard, part.shape[1])
-        own = line_scatter([pick(blocks, (exp + o) % n_exp) for o in range(n_exp)], "exp")
+        own = pick(blocks, exp).astype(f32)
+        for s in range(1, n_exp):
+            own = own + shift_back(pick(blocks, (exp - s) % n_exp), "exp", s).astype(f32)
         own = own.astype(low).reshape(n_ctx, shard, part.shape[1])
         pieces = [pick(own, ctx)] + [swap_on(pick(own, ctx ^ m), "ctx", m) for m in range(1, n_ctx)]
         placed = place_ctx(pieces)
@@ -868,8 +1030,13 @@
     norm_gain_grads = jnp.stack(
         [jnp.sum(normed_grads * hidden_unit, axis=0), jnp.sum(ffn_grads * middle_unit, axis=0)], axis=1
     )
-    norm_total, head_total, router_total = lax.psum(
-        (norm_gain_grads, gain_grads[:2].T, router_grads), ("grp", "ctx", "exp")
+    small = [norm_gain_grads, gain_grads[:2].T, router_grads]
+    summed = sum_all(jnp.concatenate([a.reshape(-1, head_dim) for a in small]))
+    norm_total, head_total, router_total = (
+        part.reshape(a.shape)
+        for a, part in zip(
+            small, jnp.split(summed, [norm_gain_grads.size // head_dim, norm_gain_grads.size // head_dim + 2])
+        )
     )
     return (
         output,

time: 1510 us -> 1350 us (0.89)
  waiting for transfers between devices: 382 us -> 621 us
  blocking collectives: 141 us -> 0 us
  matrix products: 221 us -> 90.4 us
  Pallas kernels: 44.4 us -> 174 us
  other arithmetic: 245 us -> 134 us
  local copies, waits for them, and re-layouts: 268 us -> 174 us
  starting transfers between devices: 176 us -> 145 us
    ppermute x46 -> x57, waiting for transfers between devices: 132 us -> 270 us  [swap_on(): return lax.ppermute(value, axis, [(i, i ^ mask) for i in range(count)])]
    pallas_call x0 -> x4, Pallas kernels: none -> 131 us  [run_experts(): pl.pallas_call(kernel, grid=(2, steps), in_specs=in_specs, out_specs=[sto...]
    ppermute x48, waiting for transfers between devices: 250 us -> 350 us  [the longest x12 264 us: shift_back(): return lax.ppermute(value, axis, [(i, (i - s) % n) for i in range(n)])]
    all_gather x2 -> x0, blocking collectives: 81.1 us -> none  [the longest x1 46.1 us: per_device(): lax.all_gather(jnp.stack(gate_grad_parts, 1), ('ctx', 'exp'), axis=0)]
    psum x1 -> x0, blocking collectives: 60.3 us -> none  [per_device(): lax.psum((norm_gain_grads, gain_grads[:2].T, router_grads), ('grp', 'ctx'...]
    dot_general x6 -> x2, matrix products: 65.4 us -> 14.3 us  [dot_nt(): lax.dot_general(a, b, (((1,), (1,)), ((), ())), preferred_element_type=f32)]
    dot_general x8 -> x4, matrix products: 62.6 us -> 17.6 us  [dot(): return jnp.dot(a, b, preferred_element_type=f32)]
    dot_general x6 -> x0, matrix products: 38.5 us -> none  [the longest x4 23.4 us: per_device(): jnp.einsum('bct,btd->bcd', table_low, a, preferred_element_type=f32)]
  transfers between devices with their start and end apart: 95 -> 105, of which waited for: 26 -> 39; matrix products, arithmetic and copies ran while one was open for 37% -> 23% of each run, Pallas kernels for 3% -> 13%
where the time goes in v2:
time: 1350 us; the launch traced here: 1340 us
  waiting for transfers between devices  621 us (46%)
  local copies, waits for them, and re-layouts  174 us (13%)
  Pallas kernels  174 us (13%)
  starting transfers between devices  145 us (11%)
  other arithmetic  134 us (10%)
  matrix products  90.4 us (7%)
    ppermute x57, waiting for transfers between devices, swap_on(): return lax.ppermute(value, axis, [(i, i ^ mask) for i in range(count)])  270 us
    ppermute x12, waiting for transfers between devices, shift_back(): return lax.ppermute(value, axis, [(i, (i - s) % n) for i in range(n)])  264 us
    pallas_call x4, Pallas kernels, run_experts(): pl.pallas_call(kernel, grid=(2, steps), in_specs=in_specs, out_specs=[sto...  131 us
    unnamed x255, local copies, waits for them, and re-layouts  67.1 us
    ppermute x12, waiting for transfers between devices, line_chain(): lax.ppermute(rights[-1], axis, [(i, i + 1) for i in range(s - 1, n - 1)])  55.1 us
    dot_general x6, matrix products, dot_tn(): lax.dot_general(a, b, (((0,), (0,)), ((), ())), preferred_element_type=f32)  53.2 us
    ppermute x12, starting transfers between devices, line_chain(): lax.ppermute(lefts[-1], axis, [(i, i - 1) for i in range(1, n - s + 1)])  46.8 us
    ppermute x12, starting transfers between devices, line_chain(): lax.ppermute(rights[-1], axis, [(i, i + 1) for i in range(s - 1, n - 1)])  29.7 us
  transfers between devices with their start and end apart: 105, of which 39 were waited for; matrix products, arithmetic and copies ran while one was open for 23% of the time, Pallas kernels for 13%

profile of v2, /device:TPU:20, one launch (start us, length us, event | category | flops | bytes accessed | tf_op | source)
XLA Modules:
  0.0 1342.0 jit_solution(3155637275348106839)
XLA Ops:
  34.9 15.1 %collective-permute-done.19 = bf16[128,1024]{1,0:T(8,128)(2,1)S(1)} collective-permute-done((bf16[128,1024]{1,0:T(8,128)(2,1)S(1)}, bf16[128,1024]{1,0:T(8,128)(2,1)S(1)}, u32[]{:S(2)}, u32[]{:S(2)}) %collective-permute-start.19) | collective-permute-done | bytes 262176 | tf_op jit(solution)/shard_map/ppermute | solution.py:727
  240.4 16.2 %collective-permute-done.34 = bf16[256,2048]{0,1:T(8,128)(2,1)} collective-permute-done((bf16[256,2048]{0,1:T(8,128)(2,1)}, bf16[256,2048]{0,1:T(8,128)(2,1)}, u32[]{:S(2)}, u32[]{:S(2)}) %collective-permute-start.34) | collective-permute-done | bytes 1048608 | tf_op jit(solution)/shard_map/ppermute | solution.py:727
  284.0 23.2 %collective-permute-done.38.refs_11_.refs_12_.refs_13_ = bf16[512,2304]{1,0:T(8,128)(2,1)} collective-permute-done((bf16[512,2304]{1,0:T(8,128)(2,1)S(1)}, bf16[512,2304]{1,0:T(8,128)(2,1)}, u32[]{:S(2)}, u32[]{:S(2)}) %collective-permute-start.38) | collective-permute-done | bytes 2359328 | tf_op jit(solution)/shard_map/ppermute | solution.py:727
  320.3 15.3 %collective-permute-done.44 = bf16[256,2048]{1,0:T(8,128)(2,1)S(1)} collective-permute-done((bf16[256,2048]{1,0:T(8,128)(2,1)}, bf16[256,2048]{1,0:T(8,128)(2,1)S(1)}, u32[]{:S(2)}, u32[]{:S(2)}) %collective-permute-start.44) | collective-permute-done | bytes 1048608 | tf_op jit(solution)/shard_map/ppermute | solution.py:740
  339.4 17.2 %collective-permute-done.39.refs_14_.refs_15_.refs_16_ = bf16[512,2304]{1,0:T(8,128)(2,1)} collective-permute-done((bf16[512,2304]{1,0:T(8,128)(2,1)}, bf16[512,2304]{1,0:T(8,128)(2,1)}, u32[]{:S(2)}, u32[]{:S(2)}) %collective-permute-start.39) | collective-permute-done | bytes 2359328 | tf_op jit(solution)/shard_map/ppermute | solution.py:727
  361.0 16.5 %collective-permute-done.56 = bf16[256,2048]{1,0:T(8,128)(2,1)S(1)} collective-permute-done((bf16[256,2048]{1,0:T(8,128)(2,1)S(1)}, bf16[256,2048]{1,0:T(8,128)(2,1)S(1)}, u32[]{:S(2)}, u32[]{:S(2)}) %collective-permute-start.56) | collective-permute-done | bytes 1048608 | tf_op jit(solution)/shard_map/ppermute | solution.py:740
  384.9 18.0 %collective-permute-done.62 = bf16[256,2048]{1,0:T(8,128)(2,1)S(1)} collective-permute-done((bf16[256,2048]{1,0:T(8,128)(2,1)S(1)}, bf16[256,2048]{1,0:T(8,128)(2,1)S(1)}, u32[]{:S(2)}, u32[]{:S(2)}) %collective-permute-start.62) | collective-permute-done | bytes 1048608 | tf_op jit(solution)/shard_map/ppermute | solution.py:740
  418.8 42.5 %collective-permute-done.42.refs_26_.refs_27_.refs_28_ = bf16[512,2304]{1,0:T(8,128)(2,1)} collective-permute-done((bf16[512,2304]{1,0:T(8,128)(2,1)}, bf16[512,2304]{1,0:T(8,128)(2,1)}, u32[]{:S(2)}, u32[]{:S(2)}) %collective-permute-start.42) | collective-permute-done | bytes 2359328 | tf_op jit(solution)/shard_map/ppermute | solution.py:727
  464.1 32.5 %shard_map.179 = (bf16[2,1280,2048]{2,1,0:T(8,128)(2,1)}, bf16[2,1280,2048]{2,1,0:T(8,128)(2,1)}, bf16[2,1280,1536]{2,1,0:T(8,128)(2,1)}, bf16[2,1280,768]{2,1,0...) custom-call(bf16[256,2048]{1,0:T(8,128)(2,1)} %maximum_select_fusion, ...), custom_call_target="tpu_custom_call" | custom-call | tf_op jit(solution)/shard_map/pallas_call | solution.py:695
  497.2 32.9 %shard_map.180 = (bf16[2,1280,2048]{2,1,0:T(8,128)(2,1)}, bf16[2,1280,2048]{2,1,0:T(8,128)(2,1)}, bf16[2,1280,1536]{2,1,0:T(8,128)(2,1)}, bf16[2,1280,768]{2,1,0...) custom-call(bf16[256,2048]{1,0:T(8,128)(2,1)} %add.552.refs_0_, ...), custom_call_target="tpu_custom_call", output_to_operand_aliasing={{0}: (29, {}), {1}: (30, {}), {2}: (31, {}), {3}: (32, {})} | custom-call | tf_op jit(solution)/shard_map/pallas_call | solution.py:695
  530.1 33.0 %shard_map.181 = (bf16[2,1280,2048]{2,1,0:T(8,128)(2,1)}, bf16[2,1280,2048]{2,1,0:T(8,128)(2,1)}, bf16[2,1280,1536]{2,1,0:T(8,128)(2,1)}, bf16[2,1280,768]{2,1,0...) custom-call(bf16[256,2048]{1,0:T(8,128)(2,1)} %add.556.refs_0_, ...), custom_call_target="tpu_custom_call", output_to_operand_aliasing={{0}: (29, {}), {1}: (30, {}), {2}: (31, {}), {3}: (32, {})} | custom-call | tf_op jit(solution)/shard_map/pallas_call | solution.py:695
  563.1 32.6 %shard_map.182 = (bf16[2,1280,2048]{2,1,0:T(8,128)(2,1)}, bf16[2,1280,2048]{2,1,0:T(8,128)(2,1)}, bf16[2,1280,1536]{2,1,0:T(8,128)(2,1)}, bf16[2,1280,768]{2,1,0...) custom-call(bf16[256,2048]{1,0:T(8,128)(2,1)} %add.560.refs_0_, ...), custom_call_target="tpu_custom_call", output_to_operand_aliasing={{0}: (29, {}), {1}: (30, {}), {2}: (31, {}), {3}: (32, {})} | custom-call | tf_op jit(solution)/shard_map/pallas_call | solution.py:695
  661.6 53.6 %collective-permute-done.55 = bf16[272,2048]{1,0:T(8,128)(2,1)} collective-permute-done((bf16[272,2048]{1,0:T(8,128)(2,1)S(1)}, bf16[272,2048]{1,0:T(8,128)(2,1)}, u32[]{:S(2)}, u32[]{:S(2)}) %collective-permute-start.55) | collective-permute-done | bytes 1114144 | tf_op jit(solution)/shard_map/ppermute | solution.py:747
  715.3 23.2 %collective-permute-done.61 = bf16[272,2048]{1,0:T(8,128)(2,1)} collective-permute-done((bf16[272,2048]{1,0:T(8,128)(2,1)}, bf16[272,2048]{1,0:T(8,128)(2,1)}, u32[]{:S(2)}, u32[]{:S(2)}) %collective-permute-start.61) | collective-permute-done | bytes 1114144 | tf_op jit(solution)/shard_map/ppermute | solution.py:747
  800.1 28.6 %shard_map.183 = (bf16[1024,1280]{1,0:T(8,128)(2,1)}, f32[8,128]{1,0:T(8,128)S(1)}) custom-call(f32[1024,1280]{1,0:T(8,128)} %fusion.75.q_ref.k_ref.v_ref, f32[1024,1280]{1,0:T(8,128)} %fusion.75.q_ref.k_ref.v_ref, f32[1024,1280]{1,0:T(8,128)} %fusion.75.q_ref.k_ref.v_ref, f32[1024,128]{1,0:T(8,128)S(1)} %get-tuple-element.234.cos_ref, ...), custom_call_target="tpu_custom_call" | custom-call | tf_op jit(solution)/shard_map/pallas_call | solution.py:513
  841.2 35.1 %collective-permute-done.72 = bf16[256,2048]{1,0:T(8,128)(2,1)} collective-permute-done((bf16[256,2048]{1,0:T(8,128)(2,1)}, bf16[256,2048]{1,0:T(8,128)(2,1)}, u32[]{:S(2)}, u32[]{:S(2)}) %collective-permute-start.72) | collective-permute-done | bytes 1048608 | tf_op jit(solution)/shard_map/ppermute | solution.py:747
  880.2 40.4 %collective-permute-done.74 = bf16[256,2048]{1,0:T(8,128)(2,1)} collective-permute-done((bf16[256,2048]{1,0:T(8,128)(2,1)}, bf16[256,2048]{1,0:T(8,128)(2,1)}, u32[]{:S(2)}, u32[]{:S(2)}) %collective-permute-start.74) | collective-permute-done | bytes 1048608 | tf_op jit(solution)/shard_map/ppermute | solution.py:747
  950.1 15.5 %collective-permute-done.88 = bf16[512,1024]{1,0:T(8,128)(2,1)S(1)} collective-permute-done((bf16[512,1024]{1,0:T(8,128)(2,1)}, bf16[512,1024]{1,0:T(8,128)(2,1)S(1)}, u32[]{:S(2)}, u32[]{:S(2)}) %collective-permute-start.88) | collective-permute-done | bytes 1048608 | tf_op jit(solution)/shard_map/ppermute | solution.py:747
  965.6 56.0 %collective-permute-done.89 = bf16[512,1024]{1,0:T(8,128)(2,1)S(1)} collective-permute-done((bf16[512,1024]{1,0:T(8,128)(2,1)}, bf16[512,1024]{1,0:T(8,128)(2,1)S(1)}, u32[]{:S(2)}, u32[]{:S(2)}) %collective-permute-start.89) | collective-permute-done | bytes 1048608 | tf_op jit(solution)/shard_map/ppermute | solution.py:747
  1049.9 27.1 %collective-permute-done.81 = bf16[512,1280]{1,0:T(8,128)(2,1)} collective-permute-done((bf16[512,1280]{1,0:T(8,128)(2,1)}, bf16[512,1280]{1,0:T(8,128)(2,1)}, u32[]{:S(2)}, u32[]{:S(2)}) %collective-permute-start.81) | collective-permute-done | bytes 1310752 | tf_op jit(solution)/shard_map/ppermute | solution.py:747
  1152.5 23.8 %collective-permute-done.86 = bf16[4,128,1280]{2,1,0:T(8,128)(2,1)} collective-permute-done((bf16[4,128,1280]{2,1,0:T(8,128)(2,1)}, bf16[4,128,1280]{2,1,0:T(8,128)(2,1)}, u32[]{:S(2)}, u32[]{:S(2)}) %collective-permute-start.86) | collective-permute-done | bytes 1310752 | tf_op jit(solution)/shard_map/ppermute | solution.py:727
  1216.6 24.6 %collective-permute-done.102 = bf16[512,2304]{0,1:T(8,128)(2,1)} collective-permute-done((bf16[512,2304]{0,1:T(8,128)(2,1)}, bf16[512,2304]{0,1:T(8,128)(2,1)}, u32[]{:S(2)}, u32[]{:S(2)}) %collective-permute-start.102) | collective-permute-done | bytes 2359328 | tf_op jit(solution)/shard_map/ppermute | solution.py:727
  1241.2 48.7 %collective-permute-done.104 = bf16[512,2304]{0,1:T(8,128)(2,1)} collective-permute-done((bf16[512,2304]{0,1:T(8,128)(2,1)}, bf16[512,2304]{0,1:T(8,128)(2,1)}, u32[]{:S(2)}, u32[]{:S(2)}) %collective-permute-start.104) | collective-permute-done | bytes 2359328 | tf_op jit(solution)/shard_map/ppermute | solution.py:727
  1322.2 19.3 %copy.200 = f32[512,4,2,768]{3,2,1,0:T(2,128)} copy(f32[512,4,2,768]{0,3,2,1:T(8,128)} %bitcast.307) | data formatting | bytes 25165824
  (636 shorter events, 647.7 us)
Async XLA Ops:
  235.6 71.6 %collective-permute-start.38 = (bf16[512,2304]{1,0:T(8,128)(2,1)S(1)}, bf16[512,2304]{1,0:T(8,128)(2,1)}, u32[]{:S(2)}, u32[]{:S(2)}) collective-permute-start(bf16[512,2304]{1,0:T(8,128)(2,1)S(1)} %pad_maximum_fusion.3.refs_5_.refs_6_.refs_7_), channel_id=1, source_target_pairs={{0,8},{4,12},{8,0},{12,4},{1,9},{5,13},{9,1},{13,5},{2,10},{6,14},... | collective-permute-start | bytes 7077896 | tf_op jit(solution)/shard_map/ppermute | solution.py:727
  236.9 119.7 %collective-permute-start.39 = (bf16[512,2304]{1,0:T(8,128)(2,1)}, bf16[512,2304]{1,0:T(8,128)(2,1)}, u32[]{:S(2)}, u32[]{:S(2)}) collective-permute-start(bf16[512,2304]{1,0:T(8,128)(2,1)} %pad_maximum_fusion.4), channel_id=1, source_target_pairs={{0,12},{4,8},{8,4},{12,0},{1,13},{5,9},{9,5},{13,1},{2,14},{6,10},... | collective-permute-start | bytes 7077896 | tf_op jit(solution)/shard_map/ppermute | solution.py:727
  358.7 102.5 %collective-permute-start.42 = (bf16[512,2304]{1,0:T(8,128)(2,1)}, bf16[512,2304]{1,0:T(8,128)(2,1)}, u32[]{:S(2)}, u32[]{:S(2)}) collective-permute-start(bf16[512,2304]{1,0:T(8,128)(2,1)} %collective-permute-done.39.refs_14_.refs_15_.refs_16_), channel_id=1, source_target_pairs={{0,16},{16,0},{1,17},{17,1},{2,18},{18,2},{3,19},{19,3},{4,20},{20... | collective-permute-start | bytes 7077896 | tf_op jit(solution)/shard_map/ppermute | solution.py:727
  384.8 76.4 %collective-permute-start.53 = (bf16[272,2048]{1,0:T(8,128)(2,1)}, bf16[272,2048]{1,0:T(8,128)(2,1)}, u32[]{:S(2)}, u32[]{:S(2)}) collective-permute-start(bf16[272,2048]{1,0:T(8,128)(2,1)} %add.553.refs_2_), channel_id=1, source_target_pairs={{0,4},{4,0},{8,12},{12,8},{1,5},{5,1},{9,13},{13,9},{2,6},{6,2},{1... | collective-permute-start | bytes 3342344 | tf_op jit(solution)/shard_map/ppermute | solution.py:727
  418.2 111.9 %collective-permute-start.59 = (bf16[272,2048]{1,0:T(8,128)(2,1)}, bf16[272,2048]{1,0:T(8,128)(2,1)}, u32[]{:S(2)}, u32[]{:S(2)}) collective-permute-start(bf16[272,2048]{1,0:T(8,128)(2,1)} %add.557.refs_2_), channel_id=1, source_target_pairs={{0,4},{4,0},{8,12},{12,8},{1,5},{5,1},{9,13},{13,9},{2,6},{6,2},{1... | collective-permute-start | bytes 3342344 | tf_op jit(solution)/shard_map/ppermute | solution.py:727
  418.7 144.4 %collective-permute-start.65 = (bf16[272,2048]{1,0:T(8,128)(2,1)}, bf16[272,2048]{1,0:T(8,128)(2,1)}, u32[]{:S(2)}, u32[]{:S(2)}) collective-permute-start(bf16[272,2048]{1,0:T(8,128)(2,1)} %add.561.refs_2_), channel_id=1, source_target_pairs={{0,4},{4,0},{8,12},{12,8},{1,5},{5,1},{9,13},{13,9},{2,6},{6,2},{1... | collective-permute-start | bytes 3342344 | tf_op jit(solution)/shard_map/ppermute | solution.py:727
  461.8 101.3 %collective-permute-start.63 = (bf16[256,2048]{1,0:T(8,128)(2,1)}, bf16[256,2048]{1,0:T(8,128)(2,1)}, u32[]{:S(2)}, u32[]{:S(2)}) collective-permute-start(bf16[256,2048]{1,0:T(8,128)(2,1)} %add.560.refs_0_), channel_id=1, source_target_pairs={{0,4},{4,0},{8,12},{12,8},{1,5},{5,1},{9,13},{13,9},{2,6},{6,2},{1... | collective-permute-start | bytes 3145736 | tf_op jit(solution)/shard_map/ppermute | solution.py:727
  496.7 164.9 %collective-permute-start.43 = (bf16[272,2048]{1,0:T(8,128)(2,1)}, bf16[272,2048]{1,0:T(8,128)(2,1)}, u32[]{:S(2)}, u32[]{:S(2)}) collective-permute-start(bf16[272,2048]{1,0:T(8,128)(2,1)} %get-tuple-element.69), channel_id=1, source_target_pairs={{0,4},{4,0},{8,12},{12,8},{1,5},{5,1},{9,13},{13,9},{2,6},{6,2},{1... | collective-permute-start | bytes 3342344 | tf_op jit(solution)/shard_map/ppermute | solution.py:727
  634.4 308.5 %collective-permute-start.100 = (bf16[1024,2304]{0,1:T(8,128)(2,1)}, bf16[1024,2304]{0,1:T(8,128)(2,1)}, u32[]{:S(2)}, u32[]{:S(2)}) collective-permute-start(bf16[1024,2304]{0,1:T(8,128)(2,1)} %pad_maximum_fusion), channel_id=1, source_target_pairs={{0,8},{4,12},{8,0},{12,4},{1,9},{5,13},{9,1},{13,5},{2,10},{6,14},... | collective-permute-start | bytes 14155784 | tf_op jit(solution)/shard_map/ppermute | solution.py:727
  638.8 76.5 %collective-permute-start.55 = (bf16[272,2048]{1,0:T(8,128)(2,1)S(1)}, bf16[272,2048]{1,0:T(8,128)(2,1)}, u32[]{:S(2)}, u32[]{:S(2)}) collective-permute-start(bf16[272,2048]{1,0:T(8,128)(2,1)S(1)} %add_convert_fusion.4), channel_id=1, source_target_pairs={{0,3},{1,0},{2,1},{3,2},{4,7},{5,4},{6,5},{7,6},{8,11},{9,8},{10,9... | collective-permute-start | bytes 3342344 | tf_op jit(solution)/shard_map/ppermute | solution.py:747
  645.3 93.2 %collective-permute-start.61 = (bf16[272,2048]{1,0:T(8,128)(2,1)}, bf16[272,2048]{1,0:T(8,128)(2,1)}, u32[]{:S(2)}, u32[]{:S(2)}) collective-permute-start(bf16[272,2048]{1,0:T(8,128)(2,1)} %add_convert_fusion.3), channel_id=1, source_target_pairs={{0,2},{1,3},{2,0},{3,1},{4,6},{5,7},{6,4},{7,5},{8,10},{9,11},{10,... | collective-permute-start | bytes 3342344 | tf_op jit(solution)/shard_map/ppermute | solution.py:747
  649.1 92.4 %collective-permute-start.67 = (bf16[272,2048]{1,0:T(8,128)(2,1)}, bf16[272,2048]{1,0:T(8,128)(2,1)S(1)}, u32[]{:S(2)}, u32[]{:S(2)}) collective-permute-start(bf16[272,2048]{1,0:T(8,128)(2,1)} %add_convert_fusion.2), channel_id=1, source_target_pairs={{0,1},{1,2},{2,3},{3,0},{4,5},{5,6},{6,7},{7,4},{8,9},{9,10},{10,1... | collective-permute-start | bytes 3342344 | tf_op jit(solution)/shard_map/ppermute | solution.py:747
  769.6 69.8 %collective-permute-start.68 = (bf16[256,2048]{1,0:T(8,128)(2,1)}, bf16[256,2048]{1,0:T(8,128)(2,1)}, u32[]{:S(2)}, u32[]{:S(2)}) collective-permute-start(bf16[256,2048]{1,0:T(8,128)(2,1)} %get-tuple-element.90), channel_id=1, source_target_pairs={{0,4},{4,0},{8,12},{12,8},{1,5},{5,1},{9,13},{13,9},{2,6},{6,2},{1... | collective-permute-start | bytes 3145736 | tf_op jit(solution)/shard_map/ppermute | solution.py:727
  788.1 88.2 %collective-permute-start.72 = (bf16[256,2048]{1,0:T(8,128)(2,1)}, bf16[256,2048]{1,0:T(8,128)(2,1)}, u32[]{:S(2)}, u32[]{:S(2)}) collective-permute-start(bf16[256,2048]{1,0:T(8,128)(2,1)} %add_convert_fusion.8), channel_id=1, source_target_pairs={{0,2},{1,3},{2,0},{3,1},{4,6},{5,7},{6,4},{7,5},{8,10},{9,11},{10,... | collective-permute-start | bytes 3145736 | tf_op jit(solution)/shard_map/ppermute | solution.py:747
  789.8 130.7 %collective-permute-start.74 = (bf16[256,2048]{1,0:T(8,128)(2,1)}, bf16[256,2048]{1,0:T(8,128)(2,1)}, u32[]{:S(2)}, u32[]{:S(2)}) collective-permute-start(bf16[256,2048]{1,0:T(8,128)(2,1)} %add_convert_fusion.7), channel_id=1, source_target_pairs={{0,1},{1,2},{2,3},{3,0},{4,5},{5,6},{6,7},{7,4},{8,9},{9,10},{10,1... | collective-permute-start | bytes 3145736 | tf_op jit(solution)/shard_map/ppermute | solution.py:747
  839.4 278.3 %collective-permute-start.99 = (bf16[1024,2304]{0,1:T(8,128)(2,1)}, bf16[1024,2304]{0,1:T(8,128)(2,1)}, u32[]{:S(2)}, u32[]{:S(2)}) collective-permute-start(bf16[1024,2304]{0,1:T(8,128)(2,1)} %pad_maximum_fusion.1), channel_id=1, source_target_pairs={{0,8},{4,12},{8,0},{12,4},{1,9},{5,13},{9,1},{13,5},{2,10},{6,14},... | collective-permute-start | bytes 14155784 | tf_op jit(solution)/shard_map/ppermute | solution.py:727
  839.8 110.2 %collective-permute-start.87 = (bf16[512,1024]{1,0:T(8,128)(2,1)}, bf16[512,1024]{1,0:T(8,128)(2,1)S(1)}, u32[]{:S(2)}, u32[]{:S(2)}) collective-permute-start(bf16[512,1024]{1,0:T(8,128)(2,1)} %get-tuple-element.173), channel_id=1, source_target_pairs={{0,3},{1,0},{2,1},{3,2},{4,7},{5,4},{6,5},{7,6},{8,11},{9,8},{10,9... | collective-permute-start | bytes 3145736 | tf_op jit(solution)/shard_map/ppermute | solution.py:747
  876.3 89.3 %collective-permute-start.88 = (bf16[512,1024]{1,0:T(8,128)(2,1)}, bf16[512,1024]{1,0:T(8,128)(2,1)S(1)}, u32[]{:S(2)}, u32[]{:S(2)}) collective-permute-start(bf16[512,1024]{1,0:T(8,128)(2,1)} %get-tuple-element.175), channel_id=1, source_target_pairs={{0,2},{1,3},{2,0},{3,1},{4,6},{5,7},{6,4},{7,5},{8,10},{9,11},{10,... | collective-permute-start | bytes 3145736 | tf_op jit(solution)/shard_map/ppermute | solution.py:747
  920.5 101.1 %collective-permute-start.89 = (bf16[512,1024]{1,0:T(8,128)(2,1)}, bf16[512,1024]{1,0:T(8,128)(2,1)S(1)}, u32[]{:S(2)}, u32[]{:S(2)}) collective-permute-start(bf16[512,1024]{1,0:T(8,128)(2,1)} %get-tuple-element.174), channel_id=1, source_target_pairs={{0,1},{1,2},{2,3},{3,0},{4,5},{5,6},{6,7},{7,4},{8,9},{9,10},{10,1... | collective-permute-start | bytes 3145736 | tf_op jit(solution)/shard_map/ppermute | solution.py:747
  942.8 107.0 %collective-permute-start.80 = (bf16[512,1280]{1,0:T(8,128)(2,1)}, bf16[512,1280]{1,0:T(8,128)(2,1)}, u32[]{:S(2)}, u32[]{:S(2)}) collective-permute-start(bf16[512,1280]{1,0:T(8,128)(2,1)} %get-tuple-element.168), channel_id=1, source_target_pairs={{0,3},{1,0},{2,1},{3,2},{4,7},{5,4},{6,5},{7,6},{8,11},{9,8},{10,9... | collective-permute-start | bytes 3932168 | tf_op jit(solution)/shard_map/ppermute | solution.py:747
  950.0 127.0 %collective-permute-start.81 = (bf16[512,1280]{1,0:T(8,128)(2,1)}, bf16[512,1280]{1,0:T(8,128)(2,1)}, u32[]{:S(2)}, u32[]{:S(2)}) collective-permute-start(bf16[512,1280]{1,0:T(8,128)(2,1)} %get-tuple-element.170), channel_id=1, source_target_pairs={{0,2},{1,3},{2,0},{3,1},{4,6},{5,7},{6,4},{7,5},{8,10},{9,11},{10,... | collective-permute-start | bytes 3932168 | tf_op jit(solution)/shard_map/ppermute | solution.py:747
  965.6 112.2 %collective-permute-start.82 = (bf16[512,1280]{1,0:T(8,128)(2,1)}, bf16[512,1280]{1,0:T(8,128)(2,1)}, u32[]{:S(2)}, u32[]{:S(2)}) collective-permute-start(bf16[512,1280]{1,0:T(8,128)(2,1)} %get-tuple-element.169), channel_id=1, source_target_pairs={{0,1},{1,2},{2,3},{3,0},{4,5},{5,6},{6,7},{7,4},{8,9},{9,10},{10,1... | collective-permute-start | bytes 3932168 | tf_op jit(solution)/shard_map/ppermute | solution.py:747
  1021.6 105.0 %collective-permute-start.101 = (bf16[1024,2304]{0,1:T(8,128)(2,1)}, bf16[1024,2304]{0,1:T(8,128)(2,1)}, u32[]{:S(2)}, u32[]{:S(2)}) collective-permute-start(bf16[1024,2304]{0,1:T(8,128)(2,1)} %add_convert_fusion.1), channel_id=1, source_target_pairs={{0,16},{16,0},{1,17},{17,1},{2,18},{18,2},{3,19},{19,3},{4,20},{20... | collective-permute-start | bytes 14155784 | tf_op jit(solution)/shard_map/ppermute | solution.py:727
  1185.7 104.2 %collective-permute-start.104 = (bf16[512,2304]{0,1:T(8,128)(2,1)}, bf16[512,2304]{0,1:T(8,128)(2,1)}, u32[]{:S(2)}, u32[]{:S(2)}) collective-permute-start(bf16[512,2304]{0,1:T(8,128)(2,1)} %collective-permute-done.103), channel_id=1, source_target_pairs={{0,16},{16,0},{1,17},{17,1},{2,18},{18,2},{3,19},{19,3},{4,20},{20... | collective-permute-start | bytes 7077896 | tf_op jit(solution)/shard_map/ppermute | solution.py:727
  (197 other events, 4589.2 us)

commit v3 on v2

--- a/solution.py
+++ b/solution.py
@@ -539,6 +539,340 @@
     )(qkv, qkv, qkv, cosine, sine, start, gains, attended, upstream, lse)
 
 
+def front_kernel(
+    n_ctx, n_exp, heads,
+    win, wout, normed, expert_rows, ups, hidden, gain2, cos_ref, sin_ref, start_ref, gain_ref,
+    wi_out, wo_out, xn_out, qkv_out, att_out, pieces, upb, tokb, lse_ref, middle_ref,
+    wi, wo, xn, qkv, att, part, got_core, got_over, hn, key_s, value_t, send, recv, local,
+):
+    grp, ctx, exp = lax.axis_index("grp"), lax.axis_index("ctx"), lax.axis_index("exp")
+    core = ctx % 2
+    shard = win.shape[0] // n_ctx
+    rows = normed.shape[0]
+    head_dim = cos_ref.shape[1]
+    block = n_ctx * shard
+    half = block // 2
+    names = {}
+
+    def place(name):
+        return names.setdefault(name, len(names))
+
+    waits = []
+
+    def move(name, src, dst, to, landed, ok=True, landed_ok=True):
+        i = place(name)
+        out = pltpu.make_async_remote_copy(src, dst, send.at[i], recv.at[i], device_id=to)
+        come = pltpu.make_async_remote_copy(src, landed, send.at[i], recv.at[i], device_id=to)
+        def start():
+            when(ok, out.start)
+        def arrive():
+            when(landed_ok, come.wait_recv)
+        waits.append(lambda: when(ok, out.wait_send))
+        return start, arrive
+
+    def when(ok, f):
+        if ok is True:
+            f()
+        else:
+            pl.when(ok)(lambda: f())
+
+    def keep(i, src, dst):
+        return pltpu.make_async_copy(src, dst, local.at[i])
+
+    mates = {1: {"ctx": ctx ^ 1}, 2: {"ctx": ctx ^ 2}, 3: {"ctx": ctx ^ 3}}
+    other_grp, right, left = {"grp": 1 - grp}, {"exp": exp + 1}, {"exp": exp - 1}
+    has_right, has_left = exp < n_exp - 1, exp > 0
+
+    barrier = pltpu.get_barrier_semaphore()
+    for to in (mates[1], mates[2], mates[3], other_grp):
+        pl.semaphore_signal(barrier, inc=1, device_id=to)
+    pl.when(has_right)(lambda: pl.semaphore_signal(barrier, inc=1, device_id=right))
+    pl.when(has_left)(lambda: pl.semaphore_signal(barrier, inc=1, device_id=left))
+    pl.semaphore_wait(barrier, 4 + has_right.astype(jnp.int32) + has_left.astype(jnp.int32))
+
+    def rows_of(ref, index, size):
+        return ref.at[pl.ds(pl.multiple_of(index * size, size), size)]
+
+    owns = [
+        keep(0, rows_of(win, ctx, shard), rows_of(wi, exp * n_ctx + ctx, shard)),
+        keep(1, rows_of(wout, ctx, shard), rows_of(wo, exp * n_ctx + ctx, shard)),
+        keep(2, normed, rows_of(xn, ctx, rows)),
+        keep(3, ups, upb.at[0, 0]),
+    ]
+    here = [2 * core + 1 - grp, 2 * core + grp]
+    there = [2 * (1 - core) + 1 - grp, 2 * (1 - core) + grp]
+    owns += [keep(4 + j, expert_rows.at[here[j]], pieces.at[j, 0]) for j in range(2)]
+
+    def exchange(name, src, buf):
+        return [
+            move(name + str(m), rows_of(src, ctx ^ m, shard), rows_of(buf, exp * n_ctx + ctx, shard),
+                 mates[m], rows_of(buf, exp * n_ctx + (ctx ^ m), shard))
+            for m in (2, 3, 1)
+        ]
+
+    give_in, give_out = exchange("in", win, wi), exchange("out", wout, wo)
+
+    def line(name, buf):
+        at = lambda b, g: rows_of(buf, b * 2 + g, half)
+        steps = []
+        for s in range(1, n_exp):
+            r = move(name + "r" + str(s), at(exp - s + 1, grp), at(exp - s + 1, grp), right, at(exp - s, grp),
+                     has_right & (exp >= s - 1), exp >= s)
+            l = move(name + "l" + str(s), at(exp + s - 1, grp), at(exp + s - 1, grp), left, at(exp + s, grp),
+                     has_left & (exp + s - 1 < n_exp), exp + s < n_exp)
+            rx = move(name + "rx" + str(s), at(exp - s, grp), at(exp - s, grp), other_grp, at(exp - s, 1 - grp),
+                      exp >= s, exp >= s)
+            lx = move(name + "lx" + str(s), at(exp + s, grp), at(exp + s, grp), other_grp, at(exp + s, 1 - grp),
+                      exp + s < n_exp, exp + s < n_exp)
+            steps.append((r, l, rx, lx))
+        return steps
+
+    line_in, line_out = line("in", wi), line("out", wo)
+
+    def begin(steps, s):
+        steps[s - 1][0][0]()
+        steps[s - 1][1][0]()
+
+    def relay(steps, s):
+        for way in (0, 1):
+            steps[s - 1][way][1]()
+            if s < n_exp - 1:
+                steps[s][way][0]()
+            steps[s - 1][2 + way][0]()
+
+    def crossed(steps):
+        for s in range(1, n_exp):
+            steps[s - 1][2][1]()
+            steps[s - 1][3][1]()
+
+    def tokens(name, own, buf):
+        steps = []
+        for s in range(1, n_exp):
+            r = move(name + "r" + str(s), own if s == 1 else buf.at[s - 1, 0], buf.at[s, 0], right, buf.at[s, 0],
+                     has_right & (exp >= s - 1), exp >= s)
+            l = move(name + "l" + str(s), own if s == 1 else buf.at[n_exp - s + 1, 0], buf.at[n_exp - s, 0], left,
+                     buf.at[n_exp - s, 0], has_left & (exp + s - 1 < n_exp), exp + s < n_exp)
+            steps.append((r, l))
+        own_core = move(name + "c", own, buf.at[0, 1], mates[1], buf.at[0, 1])
+        rc = {}
+        for s in range(1, n_exp):
+            rc[s] = (
+                move(name + "rc" + str(s), buf.at[s, 0], buf.at[s, 1], mates[1], buf.at[s, 1], exp >= s, exp >= s),
+                move(name + "lc" + str(s), buf.at[n_exp - s, 0], buf.at[n_exp - s, 1], mates[1],
+                     buf.at[n_exp - s, 1], exp + s < n_exp, exp + s < n_exp),
+            )
+        return steps, own_core, rc
+
+    def token_begin(t, s):
+        t[0][s - 1][0][0]()
+        t[0][s - 1][1][0]()
+
+    def token_arrive(t, s):
+        for way in (0, 1):
+            t[0][s - 1][way][1]()
+            t[2][s][way][0]()
+
+    def token_end(t):
+        t[1][1]()
+        for s in range(1, n_exp):
+            t[2][s][0][1]()
+            t[2][s][1][1]()
+
+    up_line = tokens("up", ups, upb)
+    tok_line = tokens("tok", hn, tokb)
+
+    xn_over = move("xo", normed, rows_of(xn, ctx, rows), mates[2], rows_of(xn, ctx ^ 2, rows))
+    xn_core = move("xc", normed, rows_of(xn, ctx, rows), mates[1], rows_of(xn, ctx ^ 1, rows))
+    xn_both = move("xb", rows_of(xn, ctx ^ 2, rows), rows_of(xn, ctx ^ 2, rows), mates[1], rows_of(xn, ctx ^ 3, rows))
+
+    sib = [move("es" + str(j), expert_rows.at[there[j]], pieces.at[j, 1], mates[1], pieces.at[j, 1]) for j in range(2)]
+    over_same = move("eo", expert_rows.at[here[0]], pieces.at[0, 2], mates[2], pieces.at[0, 2])
+    over_other = move("ep", expert_rows.at[there[0]], pieces.at[0, 3], mates[3], pieces.at[0, 3])
+    cross_same = move("ex", pieces.at[0, 2], pieces.at[1, 2], other_grp, pieces.at[1, 2])
+    cross_other = move("ey", pieces.at[0, 3], pieces.at[1, 3], other_grp, pieces.at[1, 3])
+
+    part_of = lambda m: rows_of(part, ctx ^ m, rows)
+    core_sums = [move("p" + str(m), part_of(m), got_core.at[i], mates[1], got_core.at[i]) for i, m in enumerate((1, 3))]
+    over_sum = move("po", part_of(2), got_over, mates[2], got_over)
+
+    for c in owns:
+        c.start()
+    for start, _ in give_in:
+        start()
+    token_begin(up_line, 1)
+    up_line[1][0]()
+    owns[0].wait()
+    for _, arrive in give_in:
+        arrive()
+    begin(line_in, 1)
+    xn_over[0]()
+    xn_core[0]()
+    for start, _ in give_out:
+        start()
+    relay(line_in, 1)
+    relay(line_in, 2)
+    owns[1].wait()
+    for _, arrive in give_out:
+        arrive()
+    xn_over[1]()
+    xn_both[0]()
+    over_same[0]()
+    sib[0][0]()
+    sib[1][0]()
+    relay(line_in, 3)
+    begin(line_out, 1)
+    token_arrive(up_line, 1)
+    crossed(line_in)
+    owns[2].wait()
+    xn_core[1]()
+    xn_both[1]()
+
+    c = head_dim ** -0.5 * 1.4426950408889634
+    length = xn.shape[0]
+    tile = min(256, length)
+    wide = heads * head_dim
+    kv = dots(xn[...], wi[:, wide:])
+    qkv[:, wide:] = kv
+    unit, _ = head_norm(kv[:, :head_dim])
+    key_s[...] = turn(unit * gain_ref[1:2], cos_ref[...], sin_ref[...]).astype(jnp.bfloat16)
+    value_t[...] = kv[:, head_dim:].T.astype(jnp.bfloat16)
+
+    def pair(p, carry):
+        cols = pl.ds(pl.multiple_of(p * 2 * head_dim, 2 * head_dim), 2 * head_dim)
+        raw2 = dots(xn[...], wi[:, cols])
+        qkv[:, cols] = raw2
+        for hh in range(2):
+            unit, _ = head_norm(raw2[:, hh * head_dim : (hh + 1) * head_dim])
+            query = turn(unit * gain_ref[0:1], cos_ref[...], sin_ref[...]).astype(jnp.bfloat16)
+            for i in range(length // tile):
+                at = slice(i * tile, (i + 1) * tile)
+                start = start_ref[:, at]
+                mass = jnp.zeros((1, tile), jnp.float32)
+                total = jnp.zeros((head_dim, tile), jnp.float32)
+                for j in range(i + 1):
+                    keys = slice(j * tile, (j + 1) * tile)
+                    s = dots_nt(key_s[keys, :], query[at])
+                    w = jnp.where(allowed_chunk(start, i, j, tile), jnp.exp2(s * c), 0.0)
+                    mass = mass + jnp.sum(w, axis=0, keepdims=True)
+                    total = total + dots(value_t[:, keys], w.astype(jnp.bfloat16))
+                att[at, pl.ds(pl.multiple_of((2 * p + hh) * head_dim, head_dim), head_dim)] = (
+                    (total / mass).T.astype(jnp.bfloat16)
+                )
+                lse_ref[2 * p + hh, :, at] = jnp.log2(mass)
+        return carry
+
+    relay(line_out, 1)
+    lax.fori_loop(0, heads // 4, pair, 0)
+    relay(line_out, 2)
+    lax.fori_loop(heads // 4, heads // 2, pair, 0)
+    relay(line_out, 3)
+    token_begin(up_line, 2)
+    over_same[1]()
+    cross_same[0]()
+    over_other[0]()
+    crossed(line_out)
+    keeps = [
+        keep(6, wi, wi_out), keep(7, wo, wo_out), keep(8, xn, xn_out), keep(9, qkv, qkv_out), keep(10, att, att_out)
+    ]
+    for k in keeps:
+        k.start()
+
+    def project(m):
+        at = pl.ds(pl.multiple_of((ctx ^ m) * rows, rows), rows)
+        def columns(n, carry):
+            cols = pl.ds(pl.multiple_of(n * 2 * tile, 2 * tile), 2 * tile)
+            part[at, cols] = dots_nt(att[at, :], wo[cols, :]).astype(jnp.bfloat16)
+            return carry
+        lax.fori_loop(0, part.shape[1] // (2 * tile), columns, 0)
+
+    project(1)
+    core_sums[0][0]()
+    project(3)
+    core_sums[1][0]()
+    project(2)
+    core_sums[1][1]()
+    two = pl.ds(pl.multiple_of((ctx ^ 2) * rows, rows), rows)
+    part[two, :] = (part[two, :].astype(jnp.float32) + got_core[1].astype(jnp.float32)).astype(jnp.bfloat16)
+    over_sum[0]()
+    project(0)
+    core_sums[0][1]()
+    token_arrive(up_line, 2)
+    token_begin(up_line, 3)
+    own = pl.ds(pl.multiple_of(ctx * rows, rows), rows)
+    middle_ref[...] = hidden[...].astype(jnp.float32) + part[own, :].astype(jnp.float32) + got_core[0].astype(jnp.float32)
+    over_sum[1]()
+    middle = middle_ref[...] + got_over[...].astype(jnp.float32)
+    middle_ref[...] = middle
+    scale = lax.rsqrt(jnp.mean(middle * middle, axis=-1, keepdims=True) + epsilon)
+    normed2 = (middle * scale * gain2[...]).astype(jnp.bfloat16)
+    for b in range(n_exp):
+        for a in range(n_ctx):
+            to = (a * n_exp + b) * shard
+            at = pl.multiple_of((to + (ctx // 2) * (block * n_exp // 2)) % (block * n_exp), shard)
+            hn[:, pl.ds(at, shard)] = normed2[:, (b * n_ctx + a) * shard : (b * n_ctx + a + 1) * shard]
+    token_begin(tok_line, 1)
+    tok_line[1][0]()
+    mine = keep(11, hn, tokb.at[0, 0])
+    mine.start()
+    token_arrive(up_line, 3)
+    token_arrive(tok_line, 1)
+    token_begin(tok_line, 2)
+    over_other[1]()
+    cross_other[0]()
+    token_arrive(tok_line, 2)
+    token_begin(tok_line, 3)
+    token_arrive(tok_line, 3)
+    token_end(up_line)
+    token_end(tok_line)
+    sib[0][1]()
+    sib[1][1]()
+    cross_same[1]()
+    cross_other[1]()
+    for k in owns[3:] + keeps + [mine]:
+        k.wait()
+    for w in waits:
+        w()
+
+
+def front_count(n_exp):
+    return 3 + 3 + 8 * (n_exp - 1) + 2 * (4 * (n_exp - 1) + 1) + 3 + 2 + 4 + 3
+
+
+def front(win, wout, normed, expert_rows, ups, hidden, gain2, cosine, sine, start, gains, heads, n_ctx, n_exp):
+    rows, width = normed.shape
+    length, head_dim = cosine.shape
+    low, f32 = jnp.bfloat16, jnp.float32
+    struct = jax.ShapeDtypeStruct
+    anywhere = pl.BlockSpec(memory_space=pl.ANY)
+    vmem = pl.BlockSpec(memory_space=pltpu.VMEM)
+    cols_in, cols_out = win.shape[1], wout.shape[1]
+    quarter, wide3 = expert_rows.shape[1:]
+    ext = ups.shape[0]
+    count = front_count(n_exp)
+    return pl.pallas_call(
+        functools.partial(front_kernel, n_ctx, n_exp, heads),
+        in_specs=[anywhere] * 5 + [vmem] * 6,
+        out_specs=[anywhere] * 8 + [vmem] * 2,
+        out_shape=[
+            struct((width, cols_in), low), struct((width, cols_out), low), struct((length, width), low),
+            struct((length, cols_in), f32), struct((length, cols_out), low),
+            struct((2, n_ctx, quarter, wide3), low),
+            struct((n_exp, 2, ext, width), low), struct((n_exp, 2, rows, width), low),
+            struct((heads, 1, length), f32), struct((rows, width), f32),
+        ],
+        scratch_shapes=[
+            pltpu.VMEM((width, cols_in), low), pltpu.VMEM((width, cols_out), low), pltpu.VMEM((length, width), low),
+            pltpu.VMEM((length, cols_in), f32), pltpu.VMEM((length, cols_out), low), pltpu.VMEM((length, width), low),
+            pltpu.VMEM((2, rows, width), low), pltpu.VMEM((rows, width), low), pltpu.VMEM((rows, width), low),
+            pltpu.VMEM((length, head_dim), low), pltpu.VMEM((head_dim, length), low),
+            pltpu.SemaphoreType.DMA((count,)), pltpu.SemaphoreType.DMA((count,)), pltpu.SemaphoreType.DMA((12,)),
+        ],
+        compiler_params=pltpu.CompilerParams(
+            collective_id=0, has_side_effects=True, vmem_limit_bytes=60 * 2**20
+        ),
+    )(win, wout, normed, expert_rows, ups, hidden, gain2, cosine, sine, start, gains)
+
+
 def expert_kernel(blocks, capacity, piece_count, *refs):
     tok0, tok1, up0, up1, router_ref = refs[:5]
     weights = refs[5 : 5 + 6 * piece_count]
@@ -655,26 +989,29 @@
         finish(False)
 
 
-def run_experts(block, blocks, tok, ups, router_t, pieces, capacity, held):
-    rows, width = tok[0].shape
-    count = len(pieces[0])
-    quarter, wide3 = pieces[0][0].shape
+def run_experts(block, tok, ups, router_t, pieces, capacity, held):
+    blocks, _, rows, width = tok.shape
+    count, quarter, wide3 = pieces.shape[1:]
     units = wide3 // 3
     tile = min(256, units)
     steps = units // tile
     cap2 = 2 * capacity
     low = jnp.bfloat16
     once = pl.Buffered(1)
-    whole = lambda a: pl.BlockSpec(a.shape, lambda e, f: (0, 0), pipeline_mode=once)
-    in_specs = [whole(a) for a in (*tok, *ups, router_t)]
-    operands = [*tok, *ups, router_t]
+    block_of = lambda a, j: pl.BlockSpec(
+        (None, None) + a.shape[2:], lambda e, f: (block, j, 0, 0), pipeline_mode=once
+    )
+    in_specs = [block_of(tok, 0), block_of(tok, 1), block_of(ups, 0), block_of(ups, 1)]
+    in_specs.append(pl.BlockSpec(router_t.shape, lambda e, f: (0, 0), pipeline_mode=once))
+    operands = [tok, tok, ups, ups, router_t]
     for j in range(2):
-        for piece in pieces[j]:
+        for q in range(count):
             for part in range(3):
-                def at(e, f, j=j, part=part):
-                    return (0, part * steps + (jnp.where(e == 0, f, steps - 1) if j == 0 else jnp.where(e == 1, f, 0)))
-                in_specs.append(pl.BlockSpec((quarter, tile), at))
-                operands.append(piece)
+                def at(e, f, j=j, q=q, part=part):
+                    step = jnp.where(e == 0, f, steps - 1) if j == 0 else jnp.where(e == 1, f, 0)
+                    return (j, q, 0, part * steps + step)
+                in_specs.append(pl.BlockSpec((None, None, quarter, tile), at))
+                operands.append(pieces)
     aliases = {}
     if held is not None:
         for i, a in enumerate(held):
@@ -683,7 +1020,7 @@
             in_specs.append(pl.BlockSpec(memory_space=pl.ANY))
     store = lambda cols: pl.BlockSpec((1, cap2, cols), lambda e, f: (e, block, 0))
     whole_out = lambda r: pl.BlockSpec((r, width), lambda e, f: (0, 0), pipeline_mode=once)
-    ext = ups[0].shape[0]
+    ext = ups.shape[2]
     struct = jax.ShapeDtypeStruct
     experts = router_t.shape[0]
 
@@ -838,50 +1175,19 @@
     gain_attn = norm_gains[:, 0].astype(f32)
     gain_ffn = norm_gains[:, 1].astype(f32)
 
-    def weight_in_of(at):
-        return jnp.concatenate(
-            [
-                lax.dynamic_slice_in_dim(attention_input_weight, at * heads * head_dim, heads * head_dim, 1),
-                lax.dynamic_slice_in_dim(attention_input_weight, query_width + at * head_dim, head_dim, 1),
-                lax.dynamic_slice_in_dim(
-                    attention_input_weight, query_width + kv_width + at * head_dim, head_dim, 1
-                ),
-            ],
-            1,
-        )
-
-    def weight_out_of(at):
-        return lax.dynamic_slice_in_dim(attn_out_weight, at * heads * head_dim, heads * head_dim, 1)
-
-    def to_ctx(piece_of, then=None):
-        pieces = [piece_of(ctx ^ m) for m in range(n_ctx)]
-        if then is not None:
-            pieces = [after(p, then) for p in pieces]
-        return place_ctx([pieces[0]] + [swap_on(pieces[m], "ctx", m) for m in range(1, n_ctx)])
-
-    def all_rows(block, then=None):
-        halves = block.reshape((2, n_ctx // 2) + block.shape[1:])
-        half_block = pick(halves, grp)
-        if then is not None:
-            half_block = after(half_block, then)
-        rights, lefts = line_chain(half_block, "exp")
-        cross = lambda value, held: lax.ppermute(
-            value, ("grp", "exp"), [(g * n_exp + i, (1 - g) * n_exp + i) for g in range(2) for i in held]
-        )
-        rights_x, lefts_x = [None], [None]
-        for s in range(1, n_exp):
-            rights_x.append(cross(rights[s], range(s, n_exp)))
-            lefts_x.append(cross(lefts[s], range(n_exp - s)))
-        out = jnp.zeros((n_exp,) + halves.shape, block.dtype)
-        out = lax.dynamic_update_index_in_dim(out, halves, exp, 0)
-        for s in range(1, n_exp):
-            for which, r, l in ((grp, rights, lefts), (1 - grp, rights_x, lefts_x)):
-                got = (r[s] + l[n_exp - s])[None, None]
-                out = lax.dynamic_update_slice(out, got, ((exp - s) % n_exp, which, 0, 0, 0))
-        return out.reshape(width, block.shape[-1]), rights[n_exp - 1]
+    by_head = lambda a, at, size: a[:, at : at + n_ctx * size].reshape(shard, n_ctx, size).transpose(1, 0, 2)
+    wide = heads * head_dim
+    weight_in_block = jnp.concatenate(
+        [
+            by_head(attention_input_weight, 0, wide),
+            by_head(attention_input_weight, query_width, head_dim),
+            by_head(attention_input_weight, query_width + kv_width, head_dim),
+        ],
+        2,
+    ).reshape(n_ctx * shard, wide + 2 * head_dim)
+    weight_out_block = by_head(attn_out_weight, 0, wide).reshape(n_ctx * shard, wide)
 
     normed, hidden_unit, hidden_scale = norm_forward(hidden, gain_attn)
-    normed_seq = gather_ctx(by_exp(normed.astype(low))).reshape(length, width)
     capacity = 5 * rows * top // (4 * expert_count)
     hits = jnp.any(routes[0][:, :, None] == jnp.arange(expert_count, dtype=jnp.int32), axis=1)
     before = jnp.tril(jnp.ones((rows, rows), low), -1)
@@ -889,40 +1195,17 @@
     upstream_block = jnp.concatenate(
         [own_half_first(out_grad[0]), jnp.pad(slots, ((0, 0), (0, width - rows)))]
     )
-    block_in = to_ctx(weight_in_of)
-    block_out = to_ctx(weight_out_of, block_in)
-    weight_in, in_done = all_rows(block_in)
-    weight_out, out_done = all_rows(block_out, in_done)
-    up_rights, up_lefts = line_chain(upstream_block, "exp", out_done)
-
-    local_experts = expert_in.shape[1]
-    hidden_units = expert_out.shape[2]
-    quarter = expert_in.shape[0]
-
-    def expert_rows(at):
-        return jnp.concatenate(
-            [
-                lax.dynamic_index_in_dim(expert_in, at, 1, keepdims=False).reshape(quarter, -1),
-                lax.dynamic_index_in_dim(expert_out, at, 1, keepdims=False),
-            ],
-            1,
-        )
-
-    here = [2 * core + (1 - grp), 2 * core + grp]
-    there = [2 * (1 - core) + (1 - grp), 2 * (1 - core) + grp]
-    over_same = swap_on(after(expert_rows(here[0]), block_out), "ctx", 2)
-    over_other = swap_on(after(expert_rows(there[0]), block_out), "ctx", 3)
-    expert_weights = []
-    for j in range(2):
-        same, other = expert_rows(here[j]), swap_on(expert_rows(there[j]), "ctx", 1)
-        if j == 1:
-            over_same, over_other = swap_on(over_same, "grp", 1), swap_on(over_other, "grp", 1)
-        expert_weights.append([same, other, over_same, over_other])
-
-    qkv = dot(normed_seq, weight_in)
-    attended, log_mass = attend(qkv, cosine, sine, doc_start, gains, heads)
-    branch = dot_nt(attended, weight_out).astype(low).reshape(n_ctx, rows, width)
-    middle = hidden + by_ctx(scatter_ctx(branch))
+    local_experts, quarter, hidden_units = expert_in.shape[1], expert_in.shape[0], expert_out.shape[2]
+    expert_rows = jnp.concatenate(
+        [expert_in.transpose(1, 0, 2, 3).reshape(local_experts, quarter, -1), expert_out.transpose(1, 0, 2)], 2
+    )
+    (
+        weight_in, weight_out, normed_seq, qkv, attended, expert_weights, upstreams, tokens, log_mass, middle,
+    ) = front(
+        weight_in_block, weight_out_block, by_exp(normed.astype(low)), expert_rows, upstream_block,
+        by_exp(hidden_in[0]), by_exp(gain_ffn[None]), cosine, sine, doc_start, gains, heads, n_ctx, n_exp,
+    )
+    middle = by_ctx(middle)
     ffn_normed, middle_unit, middle_scale = norm_forward(middle, gain_ffn)
     ffn_low = ffn_normed.astype(low)
 
@@ -932,17 +1215,11 @@
     sel_total = jnp.sum(selected, axis=-1, keepdims=True)
     gates = selected / sel_total
 
-    tok_rights, tok_lefts = line_chain(own_half_first(ffn_low), "exp")
     router_here = own_half_first(router_weight.T)
     held, backs, mixes = None, [], []
     for s in range(n_exp):
-        if s == 0:
-            tok, ups = tok_rights[0], up_rights[0]
-        else:
-            tok, ups = tok_rights[s] + tok_lefts[n_exp - s], up_rights[s] + up_lefts[n_exp - s]
-        tok, ups = (tok, swap_on(tok, "ctx", 1)), (ups, swap_on(ups, "ctx", 1))
         *held, back0, back1, mix0, mix1 = run_experts(
-            s, n_exp, tok, ups, router_here, expert_weights, capacity, held
+            s, tokens, upstreams, router_here, expert_weights, capacity, held
         )
         back = add_low(back0, swap_on(back1, "ctx", 1))
         backs.append(back if s == 0 else shift_back(back, "exp", s))
@@ -1017,7 +1294,6 @@
     rows_out = to_rows(part_out)
     rows_in = to_rows(part_in)
     attn_out_grad = rows_out.transpose(1, 0, 2).reshape(shard, query_width)
-    wide = heads * head_dim
     attn_in_grad = jnp.concatenate(
         [
             rows_in[:, :, :wide].transpose(1, 0, 2).reshape(shard, query_width),

time: 1350 us -> 1250 us (0.926)
  Pallas kernels: 174 us -> 422 us
  waiting for transfers between devices: 621 us -> 389 us
  starting transfers between devices: 145 us -> 34.5 us
  local copies, waits for them, and re-layouts: 174 us -> 224 us
  other arithmetic: 134 us -> 89.9 us
  matrix products: 90.4 us -> 68.4 us
    pallas_call x1, Pallas kernels: 14.6 us -> 264 us  [front(): pl.pallas_call(functools.partial(front_kernel, n_ctx, n_exp, heads), in_s...]
    ppermute x57 -> x32, waiting for transfers between devices: 270 us -> 160 us  [swap_on(): return lax.ppermute(value, axis, [(i, i ^ mask) for i in range(count)])]
    ppermute x36 -> x0, starting transfers between devices: 98.5 us -> none  [the longest x12 46.8 us: line_chain(): lax.ppermute(lefts[-1], axis, [(i, i - 1) for i in range(1, n - s + 1)])]
    ppermute x36 -> x0, waiting for transfers between devices: 86.2 us -> none  [the longest x12 55.1 us: line_chain(): lax.ppermute(rights[-1], axis, [(i, i + 1) for i in range(s - 1, n - 1)])]
    dynamic_update_slice x21 -> x12, local copies, waits for them, and re-layouts: 18.3 us -> 72.9 us  [place_ctx(): out = lax.dynamic_update_index_in_dim(out, blocks[m], ctx ^ m, 0)]
    ppermute x12, waiting for transfers between devices: 264 us -> 229 us  [shift_back(): return lax.ppermute(value, axis, [(i, (i - s) % n) for i in range(n)])]
    reshape x4, local copies, waits for them, and re-layouts: 1.73 us -> 21.9 us  [the longest x2 19.6 us: per_device(): expert_in.transpose(1, 0, 2, 3).reshape(local_experts, quarter, -1)]
    dynamic_slice x5 -> x0, local copies, waits for them, and re-layouts: 17.5 us -> none  [the longest x1 7.63 us: expert_rows(): lax.dynamic_index_in_dim(expert_in, at, 1, keepdims=False)]
  transfers between devices with their start and end apart: 105 -> 44, of which waited for: 39 -> 21; matrix products, arithmetic and copies ran while one was open for 23% -> 22% of each run, Pallas kernels for 13% -> 8%
where the time goes in v3:
time: 1250 us; the launch traced here: 1230 us
  Pallas kernels  422 us (34%)
  waiting for transfers between devices  389 us (31%)
  local copies, waits for them, and re-layouts  224 us (18%)
  other arithmetic  89.9 us (7%)
  matrix products  68.4 us (5%)
  starting transfers between devices  34.5 us (3%)
    pallas_call x1, Pallas kernels, front(): pl.pallas_call(functools.partial(front_kernel, n_ctx, n_exp, heads), in_s...  264 us
    ppermute x12, waiting for transfers between devices, shift_back(): return lax.ppermute(value, axis, [(i, (i - s) % n) for i in range(n)])  229 us
    ppermute x32, waiting for transfers between devices, swap_on(): return lax.ppermute(value, axis, [(i, i ^ mask) for i in range(count)])  160 us
    pallas_call x4, Pallas kernels, run_experts(): pl.pallas_call(kernel, grid=(2, steps), in_specs=in_specs, out_specs=[sto...  129 us
    dynamic_update_slice x12, local copies, waits for them, and re-layouts, place_ctx(): out = lax.dynamic_update_index_in_dim(out, blocks[m], ctx ^ m, 0)  72.9 us
    unnamed x172, local copies, waits for them, and re-layouts  56.9 us
    dot_general x6, matrix products, dot_tn(): lax.dot_general(a, b, (((0,), (0,)), ((), ())), preferred_element_type=f32)  52.7 us
    pallas_call x1, Pallas kernels, attend_back(): pl.pallas_call(functools.partial(attend_back_kernel, min(256, length), he...  28.3 us
  transfers between devices with their start and end apart: 44, of which 21 were waited for; matrix products, arithmetic and copies ran while one was open for 22% of the time, Pallas kernels for 8%

profile of v3, /device:TPU:20, one launch (start us, length us, event | category | flops | bytes accessed | tf_op | source)
XLA Modules:
  0.0 1229.6 jit_solution(10955100051090005512)
XLA Ops:
  20.1 15.4 %reshape.311 = bf16[4,512,1536]{2,0,1:T(4,128)(2,1)} reshape(bf16[4,512,2,768]{3,2,0,1:T(2,128)(2,1)} %bitcast.240) | data formatting | bytes 12582912 | tf_op jit(solution)/shard_map/reshape | solution.py:1200
  53.1 264.2 %shard_map.178 = (bf16[2048,1280]{1,0:T(8,128)(2,1)}, bf16[2048,1024]{1,0:T(8,128)(2,1)}, bf16[1024,2048]{1,0:T(8,128)(2,1)}, f32[1024,1280]{1,0:T(8,128)}, bf16...) custom-call(bf16[512,1280]{1,0:T(8,128)(2,1)} %bitcast.241, ...), custom_call_target="tpu_custom_call" | custom-call | tf_op jit(solution)/shard_map/pallas_call | solution.py:852
  317.3 32.3 %shard_map.179 = (bf16[2,1280,2048]{2,1,0:T(8,128)(2,1)}, bf16[2,1280,2048]{2,1,0:T(8,128)(2,1)}, bf16[2,1280,1536]{2,1,0:T(8,128)(2,1)}, bf16[2,1280,768]{2,1,0...) custom-call(bf16[4,2,256,2048]{3,2,1,0:T(8,128)(2,1)} %get-tuple-ele, ...), custom_call_target="tpu_custom_call" | custom-call | tf_op jit(solution)/shard_map/pallas_call | solution.py:1032
  349.6 32.2 %shard_map.180 = (bf16[2,1280,2048]{2,1,0:T(8,128)(2,1)}, bf16[2,1280,2048]{2,1,0:T(8,128)(2,1)}, bf16[2,1280,1536]{2,1,0:T(8,128)(2,1)}, bf16[2,1280,768]{2,1,0...) custom-call(bf16[4,2,256,2048]{3,2,1,0:T(8,128)(2,1)} %get-tuple-ele, ...), custom_call_target="tpu_custom_call", output_to_operand_aliasing={{0}: (29, {}), {1}: (30, {}), {2}: (31, {}), {3}: (32, {})} | custom-call | tf_op jit(solution)/shard_map/pallas_call | solution.py:1032
  381.9 32.2 %shard_map.181 = (bf16[2,1280,2048]{2,1,0:T(8,128)(2,1)}, bf16[2,1280,2048]{2,1,0:T(8,128)(2,1)}, bf16[2,1280,1536]{2,1,0:T(8,128)(2,1)}, bf16[2,1280,768]{2,1,0...) custom-call(bf16[4,2,256,2048]{3,2,1,0:T(8,128)(2,1)} %get-tuple-ele, ...), custom_call_target="tpu_custom_call", output_to_operand_aliasing={{0}: (29, {}), {1}: (30, {}), {2}: (31, {}), {3}: (32, {})} | custom-call | tf_op jit(solution)/shard_map/pallas_call | solution.py:1032
  414.1 32.3 %shard_map.182 = (bf16[2,1280,2048]{2,1,0:T(8,128)(2,1)}, bf16[2,1280,2048]{2,1,0:T(8,128)(2,1)}, bf16[2,1280,1536]{2,1,0:T(8,128)(2,1)}, bf16[2,1280,768]{2,1,0...) custom-call(bf16[4,2,256,2048]{3,2,1,0:T(8,128)(2,1)} %get-tuple-ele, ...), custom_call_target="tpu_custom_call", output_to_operand_aliasing={{0}: (29, {}), {1}: (30, {}), {2}: (31, {}), {3}: (32, {})} | custom-call | tf_op jit(solution)/shard_map/pallas_call | solution.py:1032
  446.4 12.0 convolution_convert_fusion
  486.0 13.6 %convolution_convert_fusion.1 = bf16[2048,1536]{0,1:T(8,128)(2,1)} fusion(bf16[2,1280,2048]{2,1,0:T(8,128)(2,1)} %get-tuple-element.101, bf16[2,1280,1536]{2,1,0:T(8,128)(2,1)} %get-tuple-element.102), kind=kOutput, calls=%fused_computation.9 | convolution fusion | flops 8056209408 | bytes 15466496 | tf_op jit(solution)/shard_map/dot_general | solution.py:1139
  499.6 53.2 %collective-permute-done.2 = bf16[272,2048]{1,0:T(8,128)(2,1)S(1)} collective-permute-done((bf16[272,2048]{1,0:T(8,128)(2,1)S(1)}, bf16[272,2048]{1,0:T(8,128)(2,1)S(1)}, u32[]{:S(2)}, u32[]{:S(2)}) %collective-permute-start.2) | collective-permute-done | bytes 1114144 | tf_op jit(solution)/shard_map/ppermute | solution.py:1084
  552.8 23.0 %collective-permute-done.4 = bf16[272,2048]{1,0:T(8,128)(2,1)S(1)} collective-permute-done((bf16[272,2048]{1,0:T(8,128)(2,1)S(1)}, bf16[272,2048]{1,0:T(8,128)(2,1)S(1)}, u32[]{:S(2)}, u32[]{:S(2)}) %collective-permute-start.4) | collective-permute-done | bytes 1114144 | tf_op jit(solution)/shard_map/ppermute | solution.py:1084
  650.0 28.3 %shard_map.183 = (bf16[1024,1280]{1,0:T(8,128)(2,1)}, f32[8,128]{1,0:T(8,128)S(1)}) custom-call(f32[1024,1280]{1,0:T(8,128)} %get-tuple-element.93.q_ref.k_ref.v_ref, f32[1024,1280]{1,0:T(8,128)} %get-tuple-element.93.q_ref.k_ref.v_ref, f32[1024,1280]{1,0:T(8,128)} %get-tuple-element.93.q_ref.k_ref.v_ref, f32[1024,128]{1,0:T(8,128)S(1)} %copy-done, ...), custom_call_target="tpu_custom_call" | custom-call | tf_op jit(solution)/shard_map/pallas_call | solution.py:513
  698.6 35.4 %collective-permute-done.27 = bf16[512,1024]{1,0:T(8,128)(2,1)} collective-permute-done((bf16[512,1024]{1,0:T(8,128)(2,1)}, bf16[512,1024]{1,0:T(8,128)(2,1)}, u32[]{:S(2)}, u32[]{:S(2)}) %collective-permute-start.27) | collective-permute-done | bytes 1048608 | tf_op jit(solution)/shard_map/ppermute | solution.py:1084
  757.2 44.2 %collective-permute-done.30 = bf16[128,1024]{1,0:T(8,128)(2,1)S(1)} collective-permute-done((bf16[128,1024]{1,0:T(8,128)(2,1)}, bf16[128,1024]{1,0:T(8,128)(2,1)S(1)}, u32[]{:S(2)}, u32[]{:S(2)}) %collective-permute-start.30) | collective-permute-done | bytes 262176 | tf_op jit(solution)/shard_map/ppermute | solution.py:1064
  820.3 9.8 dynamic_update_slice.48
  849.8 43.5 %collective-permute-done.20 = bf16[512,1280]{1,0:T(8,128)(2,1)} collective-permute-done((bf16[512,1280]{1,0:T(8,128)(2,1)}, bf16[512,1280]{1,0:T(8,128)(2,1)}, u32[]{:S(2)}, u32[]{:S(2)}) %collective-permute-start.20) | collective-permute-done | bytes 1310752 | tf_op jit(solution)/shard_map/ppermute | solution.py:1084
  922.1 62.9 %collective-permute-done.11 = bf16[256,2048]{1,0:T(8,128)(2,1)S(1)} collective-permute-done((bf16[256,2048]{1,0:T(8,128)(2,1)S(1)}, bf16[256,2048]{1,0:T(8,128)(2,1)S(1)}, u32[]{:S(2)}, u32[]{:S(2)}) %collective-permute-start.11) | collective-permute-done | bytes 1048608 | tf_op jit(solution)/shard_map/ppermute | solution.py:1084
  1006.6 11.7 dynamic_update_slice.44
  1018.2 11.6 dynamic_update_slice.45
  1029.9 11.8 dynamic_update_slice.46
  1056.8 16.9 %collective-permute-done.25 = bf16[4,128,1280]{2,0,1:T(4,128)(2,1)} collective-permute-done((bf16[4,128,1280]{2,0,1:T(4,128)(2,1)}, bf16[4,128,1280]{2,0,1:T(4,128)(2,1)}, u32[]{:S(2)}, u32[]{:S(2)}) %collective-permute-start.25) | collective-permute-done | bytes 1310752 | tf_op jit(solution)/shard_map/ppermute | solution.py:1064
  1104.4 23.1 %collective-permute-done.41 = bf16[512,2304]{0,1:T(8,128)(2,1)} collective-permute-done((bf16[512,2304]{0,1:T(8,128)(2,1)}, bf16[512,2304]{0,1:T(8,128)(2,1)}, u32[]{:S(2)}, u32[]{:S(2)}) %collective-permute-start.41) | collective-permute-done | bytes 2359328 | tf_op jit(solution)/shard_map/ppermute | solution.py:1064
  1127.5 50.4 %collective-permute-done.43 = bf16[512,2304]{0,1:T(8,128)(2,1)} collective-permute-done((bf16[512,2304]{0,1:T(8,128)(2,1)}, bf16[512,2304]{0,1:T(8,128)(2,1)}, u32[]{:S(2)}, u32[]{:S(2)}) %collective-permute-start.43) | collective-permute-done | bytes 2359328 | tf_op jit(solution)/shard_map/ppermute | solution.py:1064
  1199.5 10.6 slice.178
  1210.1 19.3 %copy.155 = f32[512,4,2,768]{3,2,1,0:T(2,128)} copy(f32[512,4,2,768]{0,3,2,1:T(8,128)} %bitcast.224) | data formatting | bytes 25165824
  (383 shorter events, 337.4 us)
Async XLA Ops:
  381.8 93.7 %collective-permute-start.1 = (bf16[272,2048]{1,0:T(8,128)(2,1)}, bf16[272,2048]{1,0:T(8,128)(2,1)}, u32[]{:S(2)}, u32[]{:S(2)}) collective-permute-start(bf16[272,2048]{1,0:T(8,128)(2,1)} %get-tuple-element.70), channel_id=1, source_target_pairs={{0,4},{4,0},{8,12},{12,8},{1,5},{5,1},{9,13},{13,9},{2,6},{6,2},{1... | collective-permute-start | bytes 3342344 | tf_op jit(solution)/shard_map/ppermute | solution.py:1064
  466.1 224.7 %collective-permute-start.39 = (bf16[1024,2304]{0,1:T(8,128)(2,1)}, bf16[1024,2304]{0,1:T(8,128)(2,1)}, u32[]{:S(2)}, u32[]{:S(2)}) collective-permute-start(bf16[1024,2304]{0,1:T(8,128)(2,1)} %pad_maximum_fusion.1), channel_id=1, source_target_pairs={{0,8},{4,12},{8,0},{12,4},{1,9},{5,13},{9,1},{13,5},{2,10},{6,14},... | collective-permute-start | bytes 14155784 | tf_op jit(solution)/shard_map/ppermute | solution.py:1064
  478.5 74.3 %collective-permute-start.2 = (bf16[272,2048]{1,0:T(8,128)(2,1)S(1)}, bf16[272,2048]{1,0:T(8,128)(2,1)S(1)}, u32[]{:S(2)}, u32[]{:S(2)}) collective-permute-start(bf16[272,2048]{1,0:T(8,128)(2,1)S(1)} %add_convert_fusion.4), channel_id=1, source_target_pairs={{0,3},{1,0},{2,1},{3,2},{4,7},{5,4},{6,5},{7,6},{8,11},{9,8},{10,9... | collective-permute-start | bytes 3342344 | tf_op jit(solution)/shard_map/ppermute | solution.py:1084
  481.8 94.0 %collective-permute-start.4 = (bf16[272,2048]{1,0:T(8,128)(2,1)S(1)}, bf16[272,2048]{1,0:T(8,128)(2,1)S(1)}, u32[]{:S(2)}, u32[]{:S(2)}) collective-permute-start(bf16[272,2048]{1,0:T(8,128)(2,1)S(1)} %add_convert_fusion.3), channel_id=1, source_target_pairs={{0,2},{1,3},{2,0},{3,1},{4,6},{5,7},{6,4},{7,5},{8,10},{9,11},{10,... | collective-permute-start | bytes 3342344 | tf_op jit(solution)/shard_map/ppermute | solution.py:1084
  485.9 92.7 %collective-permute-start.6 = (bf16[272,2048]{1,0:T(8,128)(2,1)S(1)}, bf16[272,2048]{1,0:T(8,128)(2,1)S(1)}, u32[]{:S(2)}, u32[]{:S(2)}) collective-permute-start(bf16[272,2048]{1,0:T(8,128)(2,1)S(1)} %add_convert_fusion.2), channel_id=1, source_target_pairs={{0,1},{1,2},{2,3},{3,0},{4,5},{5,6},{6,7},{7,4},{8,9},{9,10},{10,1... | collective-permute-start | bytes 3342344 | tf_op jit(solution)/shard_map/ppermute | solution.py:1084
  620.9 77.2 %collective-permute-start.8 = (bf16[256,2048]{1,0:T(8,128)(2,1)}, bf16[256,2048]{1,0:T(8,128)(2,1)}, u32[]{:S(2)}, u32[]{:S(2)}) collective-permute-start(bf16[256,2048]{1,0:T(8,128)(2,1)} %get-tuple-element.86), channel_id=1, source_target_pairs={{0,4},{4,0},{8,12},{12,8},{1,5},{5,1},{9,13},{13,9},{2,6},{6,2},{1... | collective-permute-start | bytes 3145736 | tf_op jit(solution)/shard_map/ppermute | solution.py:1064
  642.9 55.2 %collective-permute-start.26 = (bf16[512,1024]{1,0:T(8,128)(2,1)}, bf16[512,1024]{1,0:T(8,128)(2,1)}, u32[]{:S(2)}, u32[]{:S(2)}) collective-permute-start(bf16[512,1024]{1,0:T(8,128)(2,1)} %get-tuple-element.156), channel_id=1, source_target_pairs={{0,3},{1,0},{2,1},{3,2},{4,7},{5,4},{6,5},{7,6},{8,11},{9,8},{10,9... | collective-permute-start | bytes 3145736 | tf_op jit(solution)/shard_map/ppermute | solution.py:1084
  643.0 91.1 %collective-permute-start.27 = (bf16[512,1024]{1,0:T(8,128)(2,1)}, bf16[512,1024]{1,0:T(8,128)(2,1)}, u32[]{:S(2)}, u32[]{:S(2)}) collective-permute-start(bf16[512,1024]{1,0:T(8,128)(2,1)} %get-tuple-element.158), channel_id=1, source_target_pairs={{0,2},{1,3},{2,0},{3,1},{4,6},{5,7},{6,4},{7,5},{8,10},{9,11},{10,... | collective-permute-start | bytes 3145736 | tf_op jit(solution)/shard_map/ppermute | solution.py:1084
  643.0 91.6 %collective-permute-start.28 = (bf16[512,1024]{1,0:T(8,128)(2,1)}, bf16[512,1024]{1,0:T(8,128)(2,1)}, u32[]{:S(2)}, u32[]{:S(2)}) collective-permute-start(bf16[512,1024]{1,0:T(8,128)(2,1)} %get-tuple-element.157), channel_id=1, source_target_pairs={{0,1},{1,2},{2,3},{3,0},{4,5},{5,6},{6,7},{7,4},{8,9},{9,10},{10,1... | collective-permute-start | bytes 3145736 | tf_op jit(solution)/shard_map/ppermute | solution.py:1084
  690.8 213.0 %collective-permute-start.38 = (bf16[1024,2304]{0,1:T(8,128)(2,1)}, bf16[1024,2304]{0,1:T(8,128)(2,1)}, u32[]{:S(2)}, u32[]{:S(2)}) collective-permute-start(bf16[1024,2304]{0,1:T(8,128)(2,1)} %pad_maximum_fusion.2), channel_id=1, source_target_pairs={{0,8},{4,12},{8,0},{12,4},{1,9},{5,13},{9,1},{13,5},{2,10},{6,14},... | collective-permute-start | bytes 14155784 | tf_op jit(solution)/shard_map/ppermute | solution.py:1064
  698.1 54.2 %collective-permute-start.12 = (bf16[256,2048]{1,0:T(8,128)(2,1)}, bf16[256,2048]{1,0:T(8,128)(2,1)}, u32[]{:S(2)}, u32[]{:S(2)}) collective-permute-start(bf16[256,2048]{1,0:T(8,128)(2,1)} %get-tuple-element.92), channel_id=1, source_target_pairs={{0,4},{4,0},{8,12},{12,8},{1,5},{5,1},{9,13},{13,9},{2,6},{6,2},{1... | collective-permute-start | bytes 3145736 | tf_op jit(solution)/shard_map/ppermute | solution.py:1064
  734.1 73.9 %collective-permute-start.19 = (bf16[512,1280]{1,0:T(8,128)(2,1)}, bf16[512,1280]{1,0:T(8,128)(2,1)}, u32[]{:S(2)}, u32[]{:S(2)}) collective-permute-start(bf16[512,1280]{1,0:T(8,128)(2,1)} %get-tuple-element.151), channel_id=1, source_target_pairs={{0,3},{1,0},{2,1},{3,2},{4,7},{5,4},{6,5},{7,6},{8,11},{9,8},{10,9... | collective-permute-start | bytes 3932168 | tf_op jit(solution)/shard_map/ppermute | solution.py:1084
  734.6 171.3 %collective-permute-start.40 = (bf16[1024,2304]{0,1:T(8,128)(2,1)}, bf16[1024,2304]{0,1:T(8,128)(2,1)}, u32[]{:S(2)}, u32[]{:S(2)}) collective-permute-start(bf16[1024,2304]{0,1:T(8,128)(2,1)} %add_convert_fusion.1), channel_id=1, source_target_pairs={{0,16},{16,0},{1,17},{17,1},{2,18},{18,2},{3,19},{19,3},{4,20},{20... | collective-permute-start | bytes 14155784 | tf_op jit(solution)/shard_map/ppermute | solution.py:1064
  801.4 97.2 %collective-permute-start.17 = (bf16[2,256,2048]{1,2,0:T(8,128)(2,1)}, bf16[2,256,2048]{1,2,0:T(8,128)(2,1)}, u32[]{:S(2)}, u32[]{:S(2)}) collective-permute-start(bf16[2,256,2048]{1,2,0:T(8,128)(2,1)} %pad_maximum_fusion.4), channel_id=1, source_target_pairs={{0,4},{4,0},{8,12},{12,8},{1,5},{5,1},{9,13},{13,9},{2,6},{6,2},{1... | collective-permute-start | bytes 6291464 | tf_op jit(solution)/shard_map/ppermute | solution.py:1064
  805.4 87.8 %collective-permute-start.20 = (bf16[512,1280]{1,0:T(8,128)(2,1)}, bf16[512,1280]{1,0:T(8,128)(2,1)}, u32[]{:S(2)}, u32[]{:S(2)}) collective-permute-start(bf16[512,1280]{1,0:T(8,128)(2,1)} %get-tuple-element.153), channel_id=1, source_target_pairs={{0,2},{1,3},{2,0},{3,1},{4,6},{5,7},{6,4},{7,5},{8,10},{9,11},{10,... | collective-permute-start | bytes 3932168 | tf_op jit(solution)/shard_map/ppermute | solution.py:1084
  808.0 86.4 %collective-permute-start.21 = (bf16[512,1280]{1,0:T(8,128)(2,1)}, bf16[512,1280]{1,0:T(8,128)(2,1)}, u32[]{:S(2)}, u32[]{:S(2)}) collective-permute-start(bf16[512,1280]{1,0:T(8,128)(2,1)} %get-tuple-element.152), channel_id=1, source_target_pairs={{0,1},{1,2},{2,3},{3,0},{4,5},{5,6},{6,7},{7,4},{8,9},{9,10},{10,1... | collective-permute-start | bytes 3932168 | tf_op jit(solution)/shard_map/ppermute | solution.py:1084
  898.9 86.1 %collective-permute-start.11 = (bf16[256,2048]{1,0:T(8,128)(2,1)S(1)}, bf16[256,2048]{1,0:T(8,128)(2,1)S(1)}, u32[]{:S(2)}, u32[]{:S(2)}) collective-permute-start(bf16[256,2048]{1,0:T(8,128)(2,1)S(1)} %copy-done.50), channel_id=1, source_target_pairs={{0,2},{1,3},{2,0},{3,1},{4,6},{5,7},{6,4},{7,5},{8,10},{9,11},{10,... | collective-permute-start | bytes 3145736 | tf_op jit(solution)/shard_map/ppermute | solution.py:1084
  903.9 84.3 %collective-permute-start.13 = (bf16[256,2048]{1,0:T(8,128)(2,1)S(1)}, bf16[256,2048]{1,0:T(8,128)(2,1)S(1)}, u32[]{:S(2)}, u32[]{:S(2)}) collective-permute-start(bf16[256,2048]{1,0:T(8,128)(2,1)S(1)} %copy-done.47), channel_id=1, source_target_pairs={{0,1},{1,2},{2,3},{3,0},{4,5},{5,6},{6,7},{7,4},{8,9},{9,10},{10,1... | collective-permute-start | bytes 3145736 | tf_op jit(solution)/shard_map/ppermute | solution.py:1084
  905.9 137.3 %collective-permute-start.32 = (bf16[4,128,1024]{2,0,1:T(4,128)(2,1)}, bf16[4,128,1024]{2,0,1:T(4,128)(2,1)}, u32[]{:S(2)}, u32[]{:S(2)}) collective-permute-start(bf16[4,128,1024]{2,0,1:T(4,128)(2,1)} %dynamic_update_slice.50), channel_id=1, source_target_pairs={{0,16},{16,0},{1,17},{17,1},{2,18},{18,2},{3,19},{19,3},{4,20},{20... | collective-permute-start | bytes 3145736 | tf_op jit(solution)/shard_map/ppermute | solution.py:1064
  917.2 73.2 %collective-permute-start.22 = (bf16[128,1280]{1,0:T(8,128)(2,1)S(1)}, bf16[128,1280]{1,0:T(8,128)(2,1)S(1)}, u32[]{:S(2)}, u32[]{:S(2)}) collective-permute-start(bf16[128,1280]{1,0:T(8,128)(2,1)S(1)} %get-tuple-element.173), channel_id=1, source_target_pairs={{0,4},{4,0},{8,12},{12,8},{1,5},{5,1},{9,13},{13,9},{2,6},{6,2},{1... | collective-permute-start | bytes 983048 | tf_op jit(solution)/shard_map/ppermute | solution.py:1064
  920.6 127.5 %collective-permute-start.18 = (bf16[256,2048]{0,1:T(8,128)(2,1)}, bf16[256,2048]{0,1:T(8,128)(2,1)}, u32[]{:S(2)}, u32[]{:S(2)}) collective-permute-start(bf16[256,2048]{0,1:T(8,128)(2,1)} %fusion.48), channel_id=1, source_target_pairs={{0,8},{4,12},{8,0},{12,4},{1,9},{5,13},{9,1},{13,5},{2,10},{6,14},... | collective-permute-start | bytes 3145736 | tf_op jit(solution)/shard_map/ppermute | solution.py:1064
  985.0 71.3 %collective-permute-start.42 = (bf16[512,2304]{0,1:T(8,128)(2,1)}, bf16[512,2304]{0,1:T(8,128)(2,1)}, u32[]{:S(2)}, u32[]{:S(2)}) collective-permute-start(bf16[512,2304]{0,1:T(8,128)(2,1)} %get-tuple-element.154), channel_id=1, source_target_pairs={{0,4},{4,0},{8,12},{12,8},{1,5},{5,1},{9,13},{13,9},{2,6},{6,2},{1... | collective-permute-start | bytes 7077896 | tf_op jit(solution)/shard_map/ppermute | solution.py:1064
  1054.8 72.7 %collective-permute-start.41 = (bf16[512,2304]{0,1:T(8,128)(2,1)}, bf16[512,2304]{0,1:T(8,128)(2,1)}, u32[]{:S(2)}, u32[]{:S(2)}) collective-permute-start(bf16[512,2304]{0,1:T(8,128)(2,1)} %get-tuple-element.155), channel_id=1, source_target_pairs={{0,16},{16,0},{1,17},{17,1},{2,18},{18,2},{3,19},{19,3},{4,20},{20... | collective-permute-start | bytes 7077896 | tf_op jit(solution)/shard_map/ppermute | solution.py:1064
  1056.3 121.6 %collective-permute-start.43 = (bf16[512,2304]{0,1:T(8,128)(2,1)}, bf16[512,2304]{0,1:T(8,128)(2,1)}, u32[]{:S(2)}, u32[]{:S(2)}) collective-permute-start(bf16[512,2304]{0,1:T(8,128)(2,1)} %collective-permute-done.42), channel_id=1, source_target_pairs={{0,16},{16,0},{1,17},{17,1},{2,18},{18,2},{3,19},{19,3},{4,20},{20... | collective-permute-start | bytes 7077896 | tf_op jit(solution)/shard_map/ppermute | solution.py:1064
  (98 other events, 1429.0 us)
